TPU v7x, 32 devices: a whole 2x2x4 slice. The times are simulated.
32 devices in a mesh: seq: 8 (over z, y), dp: 4 (over x, core).
Axes of the slice: x: 2, y: 2, z: 4, core: 2. Of those that a mesh axis runs over, the one named last changes fastest.
Arguments:
- queries: bfloat16 [4096, 20, 128], P(('dp', 'seq')), parts along dimension 0, may hold values from -6 to 6
- keys: bfloat16 [4096, 20, 128], P(('dp', 'seq')), parts along dimension 0, may hold values from -4 to 4
- values: bfloat16 [4096, 20, 128], P(('dp', 'seq')), parts along dimension 0, may hold values from -6 to 6
- out_grad: bfloat16 [4096, 20, 128], P(('dp', 'seq')), parts along dimension 0, may hold values from -96 to 96
- block_mask: int32 [20, 8, 5], replicated, may hold values from 0 to 1, as said below
Outputs:
- query_grad: bfloat16 [4096, 20, 128], P(('dp', 'seq')), parts along dimension 0
- key_grad: bfloat16 [4096, 20, 128], P(('dp', 'seq')), parts along dimension 0
- value_grad: bfloat16 [4096, 20, 128], P(('dp', 'seq')), parts along dimension 0
There are 4 independent parts, one for each index of `dp`. A program takes and returns all parts, laid end to end along the dimension named above; an argument that names none is the same for every part. Nothing has to cross between parts.
Inputs may be any that keep to these rules, and one draw needn't show every extreme that they name: `block_mask`: entry j of row i names key block i + j - 2. The entry for j = 2 is always 1; entries naming blocks outside 0 to 7 are 0.
All inputs are finite; a program needn't handle non-finite values.
Results may differ from a plain program's by a relative error of at most 0.0075.
Values may be sent and summed in bfloat16 or wider, within the bound.
No kernel may reach another device: no remote copies, remote signals or barrier semaphores. Data moves between devices by JAX's collectives and lax.ppermute only.
A program may use at most 64 MiB of HBM per device.

v0:
```python
from functools import partial
from functools import reduce
import math

import jax
import jax.numpy as jnp
from jax import lax
from jax.sharding import PartitionSpec as P

RANGE = 2


def swapped(value, axis, apart):
    mask = 2**apart
    pairs = [(source, source ^ mask) for source in range(lax.axis_size(axis))]
    return lax.ppermute(value, axis, pairs)


def from_behind(block, axis, distance):
    devices = range(lax.axis_size(axis))
    route = [(i - distance, i) for i in devices if i - distance in devices]
    return lax.ppermute(block, axis, route)


def for_sending(shard):

    def short(part):
        return part.astype(jnp.bfloat16) if part.dtype == jnp.float32 else part

    return jax.tree.map(short, shard)


def butterfly(slots, position, swapper):
    slot_count = slots.shape[0]
    half_span = 1 << 0
    shaped = slots.reshape((slot_count // (2 * half_span), 2, half_span) + slots.shape[1:])
    own_bit = position >> 0 & 1
    lower_half = shaped[:, 0]
    upper_half = shaped[:, 1]
    outgoing = jnp.where(own_bit == 0, upper_half, lower_half)
    incoming = swapper(outgoing, 0)
    new_lower = jnp.where(own_bit == 0, lower_half, incoming)
    new_upper = jnp.where(own_bit == 0, incoming, upper_half)
    slots = jnp.stack([new_lower, new_upper], axis=1).reshape(slots.shape)
    return slots


def place_values(targets, contents, length):
    places = jnp.arange(length, dtype=jnp.int32)
    matches = (targets[None, :] == places[:, None]).astype(jnp.int32)
    return jnp.sum(matches * contents[None, :], axis=1)


def side_table(mask_rows, first_offset, reach_blocks):
    group_size = mask_rows.shape[-2]
    breadth = mask_rows.shape[-1]
    query_place = jnp.arange(group_size)[:, None, None]
    key_place = jnp.arange(group_size)[None, :, None]
    column_index = jnp.arange(breadth)[None, None, :]
    picked = (column_index == first_offset + key_place - query_place + reach_blocks).astype(
        jnp.int32
    )
    return jnp.sum(mask_rows[..., :, None, :] * picked, axis=-1) > 0


def apply_mask(scores, block_table, block_size):
    group_size = block_table.shape[0]
    shaped = scores.reshape(group_size, block_size, group_size, block_size)
    return jnp.where(block_table[:, None, :, None], shaped, -jnp.inf).reshape(scores.shape)


def side_scores(query_rows, key_block, block_table, score_scale, block_size):
    scores = (
        jnp.einsum("qe,ke->qk", query_rows, key_block, preferred_element_type=jnp.float32)
        * score_scale
    )
    return apply_mask(scores, block_table, block_size)


def plain_product(left_operand, right_operand):
    return jnp.dot(left_operand, right_operand, preferred_element_type=jnp.float32)


def side_grads(
    scores,
    row_peak,
    row_total,
    weights_low,
    query_rows,
    grad_rows,
    key_block,
    value_block,
    row_delta,
    score_scale,
    want_query,
    want_keys,
):
    weights = jnp.exp(scores - row_peak[:, None]) / row_total[:, None]
    weight_grad = jnp.einsum(
        "qe,ke->qk", grad_rows, value_block, preferred_element_type=jnp.float32
    )
    score_grad = (weights * (weight_grad - row_delta[:, None])).astype(jnp.bfloat16)
    terms = []
    terms.append(jnp.dot(score_grad, key_block, preferred_element_type=jnp.float32))
    terms.append(
        score_scale
        * jnp.einsum("qk,qe->ke", score_grad, query_rows, preferred_element_type=jnp.float32)
    )
    terms.append(
        jnp.einsum("qk,qe->ke", weights_low, grad_rows, preferred_element_type=jnp.float32)
    )
    return jnp.stack(terms)


def own_pass(head_items, score_scale, with_sides):
    query_rows, grad_rows, key_sets, value_sets, tables = head_items
    row_count, head_width = query_rows.shape
    block_size = row_count // tables.shape[-1]
    actives = [jnp.any(tables[side_index]) for side_index in range(3)]
    scores = [
        lax.cond(
            actives[side_index],
            partial(
                side_scores,
                query_rows,
                key_sets[side_index],
                tables[side_index],
                score_scale,
                block_size,
            ),
            partial(jnp.full, (row_count, row_count), -jnp.inf, jnp.float32),
        )
        for side_index in range(3)
    ]
    row_peak = reduce(jnp.maximum, [jnp.max(element, axis=1) for element in scores])
    row_total = reduce(
        jnp.add, [jnp.sum(jnp.exp(element - row_peak[:, None]), axis=1) for element in scores]
    )
    weights_low = [
        (jnp.exp(element - row_peak[:, None]) / row_total[:, None]).astype(jnp.bfloat16)
        for element in scores
    ]
    zero_rows = partial(jnp.zeros, (row_count, head_width), jnp.float32)
    output = reduce(
        jnp.add,
        [
            lax.cond(
                actives[side_index],
                partial(plain_product, weights_low[side_index], value_sets[side_index]),
                zero_rows,
            )
            for side_index in range(3)
        ],
    )
    row_delta = jnp.sum(grad_rows.astype(jnp.float32) * output, axis=1)
    query_terms = []
    key_terms = []
    value_terms = []
    for side_index in range(3):
        wanted = with_sides or side_index == 1
        count_out = 3
        grad_maker = partial(
            side_grads,
            scores[side_index],
            row_peak,
            row_total,
            weights_low[side_index],
            query_rows,
            grad_rows,
            key_sets[side_index],
            value_sets[side_index],
            row_delta,
            score_scale,
            True,
            wanted,
        )
        blank_terms = partial(jnp.zeros, (count_out, row_count, head_width), jnp.float32)
        result = lax.cond(actives[side_index], grad_maker, blank_terms)
        query_terms.append(result[0])
        key_terms.append(result[1])
        value_terms.append(result[2])
    query_grad = score_scale * reduce(jnp.add, query_terms)
    return (
        query_grad,
        jnp.stack(key_terms),
        jnp.stack(value_terms),
        row_peak,
        row_total,
        row_delta,
    )


def per_device(queries, keys, values, out_grad, block_mask):
    block_size = queries.shape[0]
    head_count = queries.shape[1]
    head_width = queries.shape[2]
    group_size = RANGE
    local_heads = head_count // group_size
    range_length = group_size * block_size
    score_scale = 1.0 / math.sqrt(head_width)
    reach_blocks = (block_mask.shape[2] - 1) // 2
    device_index = lax.axis_index("seq")
    position = device_index % group_size
    range_index = device_index // group_size
    range_total = block_mask.shape[1] // group_size
    head_order = jnp.arange(head_count, dtype=jnp.int32)
    inverse = place_values(head_order, jnp.arange(head_count, dtype=jnp.int32), head_count)
    stacked = jnp.stack([queries, keys, values, out_grad], axis=0)
    stacked = jnp.take(stacked, head_order, axis=2).reshape(
        4, block_size, group_size, local_heads, head_width
    )
    stacked = jnp.transpose(stacked, (2, 0, 1, 3, 4))
    arrived = butterfly(
        stacked, position, lambda outgoing, bit_level: swapped(outgoing, "seq", bit_level)
    )
    owned_rows = jnp.transpose(arrived, (1, 3, 0, 2, 4)).reshape(
        4, local_heads, range_length, head_width
    )
    query_rows = owned_rows[0]
    key_rows = owned_rows[1]
    value_rows = owned_rows[2]
    grad_rows = owned_rows[3]
    chosen = lax.dynamic_slice_in_dim(head_order, position * local_heads, local_heads)
    head_masks = jnp.take(block_mask, chosen, axis=0)
    inside = ((range_index >= 0) & (range_index < range_total)).astype(jnp.int32)
    first_block = jnp.clip(range_index, 0, range_total - 1) * group_size
    own_rows = lax.dynamic_slice_in_dim(head_masks, first_block, group_size, axis=1) * inside
    own_tables = jnp.stack(
        [side_table(own_rows, direction * group_size, reach_blocks) for direction in (-1, 0, 1)],
        axis=1,
    )
    own_pair = jnp.stack([key_rows, value_rows], axis=0)
    neighbor_pairs = [from_behind(own_pair, "seq", offset) for offset in (group_size, -group_size)]
    key_sets = jnp.stack([neighbor_pairs[0][0], key_rows, neighbor_pairs[1][0]], axis=1)
    value_sets = jnp.stack([neighbor_pairs[0][1], value_rows, neighbor_pairs[1][1]], axis=1)
    query_grad, key_terms, value_terms, row_peak, row_total, row_delta = lax.map(
        partial(own_pass, score_scale=score_scale, with_sides=True),
        (query_rows, grad_rows, key_sets, value_sets, own_tables),
    )
    own_parts = jnp.stack([key_terms[:, 1], value_terms[:, 1]])
    left_parts = jnp.stack([key_terms[:, 0], value_terms[:, 0]])
    right_parts = jnp.stack([key_terms[:, 2], value_terms[:, 2]])
    returned = [
        from_behind(outgoing_parts, "seq", offset)
        for outgoing_parts, offset in ((left_parts, -group_size), (right_parts, group_size))
    ]
    grad_pair = own_parts + returned[0] + returned[1]
    leaving = jnp.stack(
        [
            query_grad.astype(jnp.bfloat16),
            grad_pair[0].astype(jnp.bfloat16),
            grad_pair[1].astype(jnp.bfloat16),
        ],
        axis=0,
    )
    leaving = leaving.reshape(3, local_heads, group_size, block_size, head_width)
    leaving = jnp.transpose(leaving, (2, 0, 3, 1, 4))
    returned_home = butterfly(
        leaving,
        position,
        lambda outgoing, bit_level: swapped(for_sending(outgoing), "seq", bit_level).astype(
            outgoing.dtype
        ),
    )
    at_home = jnp.transpose(returned_home, (1, 2, 0, 3, 4)).reshape(
        3, block_size, head_count, head_width
    )
    at_home = jnp.take(at_home, inverse, axis=2)
    return (at_home[0], at_home[1], at_home[2])


def solution(mesh):
    placed = (
        P(("dp", "seq"), None, None),
        P(("dp", "seq"), None, None),
        P(("dp", "seq"), None, None),
        P(("dp", "seq"), None, None),
        P(),
    )
    return jax.shard_map(
        per_device,
        mesh=mesh,
        in_specs=placed,
        out_specs=(
            P(("dp", "seq"), None, None),
            P(("dp", "seq"), None, None),
            P(("dp", "seq"), None, None),
        ),
        check_vma=False,
    )
```

profile of v0, /device:TPU:0, one launch (start us, length us, event | category | flops | bytes accessed | tf_op | source)
XLA Modules:
  0.0 417.7 jit_solution(16350826782164179178)
XLA Ops:
  0.7 2.0 pad_maximum_fusion.3
  2.7 2.6 gather_fusion.1
  5.3 2.1 fusion.21
  8.6 3.0 collective-permute-start
  12.5 28.1 %collective-permute-done = bf16[1,1,4,128,10,128]{5,3,4,2,1,0:T(8,128)(2,1)} collective-permute-done((bf16[1,1,4,128,10,128]{5,3,4,2,1,0:T(8,128)(2,1)}, bf16[1,1,4,128,10,128]{5,3,4,2,1,0:T(8,128)(2,1)}, u32[]{:S(2)}, u32[]{:S(2)}) %collective-permute-start) | collective-permute-done | bytes 1310752 | tf_op jit(solution)/shard_map/ppermute | solution.py:16
  40.6 1.5 select_bitcast_fusion.2
  43.8 4.8 %collective-permute-start.1 = (bf16[2,10,256,128]{3,2,1,0:T(8,128)(2,1)S(1)}, bf16[2,10,256,128]{3,2,1,0:T(8,128)(2,1)}, u32[]{:S(2)}, u32[]{:S(2)}) collective-permute-start(bf16[2,10,256,128]{3,2,1,0:T(8,128)(2,1)S(1)} %pad_maximum_fusion.8), channel_id=1, source_target_pairs={{0,8},{4,12},{8,16},{12,20},{16,24},{20,28},{1,9},{5,13},{9,17},{1... | collective-permute-start | bytes 3932168 | tf_op jit(solution)/shard_map/ppermute | solution.py:22
  50.3 24.4 %collective-permute-done.1 = bf16[2,10,256,128]{3,2,1,0:T(8,128)(2,1)} collective-permute-done((bf16[2,10,256,128]{3,2,1,0:T(8,128)(2,1)S(1)}, bf16[2,10,256,128]{3,2,1,0:T(8,128)(2,1)}, u32[]{:S(2)}, u32[]{:S(2)}) %collective-permute-start.1) | collective-permute-done | bytes 1310752 | tf_op jit(solution)/shard_map/ppermute | solution.py:22
  76.1 3.9 collective-permute-done.2
  81.5 1.6 pad_maximum_fusion.6
  83.1 201.1 %while.14 = (s32[]{:T(128)}, bf16[10,256,128]{2,1,0:T(8,128)(2,1)}, f32[10,3,256,128]{3,2,0,1:T(8,128)}, f32[10,3,256,128]{3,2,0,1:T(8,128)}, pred[10,3,2,2]{3,2...) while((s32[]{:T(128)}, bf16[10,256,128]{2,1,0:T(8,128)(2,1)}, ...), condition=%wide.region_33.34_spmd, body=%wide.region_4.33_spmd.sunk | while | flops 305889024 | bytes 36608776 | solution.py:236
  88.4 3.6 conditional.20
  88.8 1.5 fusion.31
  92.6 3.5 conditional.18
  98.9 2.0 conditional.26
  100.8 2.0 conditional.25
  109.8 3.6 conditional.20
  110.1 1.5 fusion.31
  114.0 3.5 conditional.18
  114.3 1.4 fusion.32
  120.2 2.0 conditional.26
  122.2 2.0 conditional.25
  131.3 3.6 conditional.20
  131.6 1.5 fusion.31
  135.5 3.5 conditional.18
  135.8 1.4 fusion.32
  141.7 2.0 conditional.26
  143.7 2.0 conditional.25
  152.6 3.6 conditional.20
  153.0 1.5 fusion.31
  160.7 2.0 conditional.26
  169.7 3.6 conditional.20
  170.1 1.5 fusion.31
  173.9 3.5 conditional.18
  174.3 1.4 fusion.32
  180.2 2.0 conditional.26
  182.1 2.0 conditional.25
  191.2 3.6 conditional.20
  191.5 1.5 fusion.31
  195.4 3.5 conditional.18
  201.6 2.0 conditional.26
  203.6 2.0 conditional.25
  212.6 3.6 conditional.20
  212.9 1.5 fusion.31
  220.6 2.0 conditional.26
  229.6 3.6 conditional.20
  230.0 1.5 fusion.31
  233.8 3.5 conditional.18
  240.1 2.0 conditional.26
  242.0 2.0 conditional.25
  251.1 3.6 conditional.20
  251.4 1.5 fusion.31
  255.2 3.5 conditional.18
  261.5 2.0 conditional.26
  263.5 2.0 conditional.25
  272.4 3.6 conditional.20
  272.8 1.5 fusion.31
  280.5 2.0 conditional.26
  284.3 2.6 slice_bitcast_fusion.10
  289.6 42.0 %collective-permute-start.4 = (f32[2,10,256,128]{3,2,1,0:T(8,128)S(1)}, f32[2,10,256,128]{3,2,1,0:T(8,128)S(1)}, u32[]{:S(2)}, u32[]{:S(2)}) collective-permute-start(f32[2,10,256,128]{3,2,1,0:T(8,128)S(1)} %pad_maximum_fusion.5), channel_id=1, source_target_pairs={{0,8},{4,12},{8,16},{12,20},{16,24},{20,28},{1,9},{5,13},{9,17},{1... | collective-permute-start | bytes 7864328 | tf_op jit(solution)/shard_map/ppermute | solution.py:22
  331.6 52.3 %collective-permute-done.3 = f32[2,10,256,128]{3,2,1,0:T(8,128)S(1)} collective-permute-done((f32[2,10,256,128]{3,2,1,0:T(8,128)S(1)}, f32[2,10,256,128]{3,2,1,0:T(8,128)S(1)}, u32[]{:S(2)}, u32[]{:S(2)}) %collective-permute-start.3) | collective-permute-done | bytes 2621472 | tf_op jit(solution)/shard_map/ppermute | solution.py:22
  387.3 5.9 %collective-permute-start.5 = (bf16[1,1,3,128,10,128]{5,3,4,2,1,0:T(8,128)(2,1)S(1)}, bf16[1,1,3,128,10,128]{5,3,4,2,1,0:T(8,128)(2,1)S(1)}, u32[]{:S(2)}, u32[]{:S(2)}) collective-permute-start(bf16[1,1,3,128,10,128]{5,3,4,2,1,0:T(8,128)(2,1)S(1)} %broadcast_select_fusion.1), channel_id=1, source_target_pairs={{0,4},{4,0},{8,12},{12,8},{16,20},{20,16},{24,28},{28,24},{1,5},{5... | collective-permute-start | bytes 2949128 | tf_op jit(solution)/shard_map/ppermute | solution.py:16
  393.3 18.6 %collective-permute-done.5 = bf16[1,1,3,128,10,128]{5,3,4,2,1,0:T(8,128)(2,1)S(1)} collective-permute-done((bf16[1,1,3,128,10,128]{5,3,4,2,1,0:T(8,128)(2,1)S(1)}, bf16[1,1,3,128,10,128]{5,3,4,2,1,0:T(8,128)(2,1)S(1)}, u32[]{:S(2)}, u32[]{:S(2)}) %collective-permute-start.5) | collective-permute-done | bytes 983072 | tf_op jit(solution)/shard_map/ppermute | solution.py:16
  413.7 2.5 gather_fusion.2
  (572 shorter events, 197.9 us)
Async XLA Ops:
  7.3 4.2 %copy-start.4 = (s32[20,8,5]{0,1,2:T(8,128)S(1)}, s32[20,8,5]{0,1,2:T(8,128)}, u32[]{:S(2)}) copy-start(s32[20,8,5]{0,1,2:T(8,128)} %param.29) | copy-start | bytes 9604
  8.6 32.1 %collective-permute-start = (bf16[1,1,4,128,10,128]{5,3,4,2,1,0:T(8,128)(2,1)}, bf16[1,1,4,128,10,128]{5,3,4,2,1,0:T(8,128)(2,1)}, u32[]{:S(2)}, u32[]{:S(2)}) collective-permute-start(bf16[1,1,4,128,10,128]{5,3,4,2,1,0:T(8,128)(2,1)} %broadcast_select_fusion), channel_id=1, source_target_pairs={{0,4},{4,0},{8,12},{12,8},{16,20},{20,16},{24,28},{28,24},{1,5},{5... | collective-permute-start | bytes 3932168 | tf_op jit(solution)/shard_map/ppermute | solution.py:16
  43.8 30.9 %collective-permute-start.1 = (bf16[2,10,256,128]{3,2,1,0:T(8,128)(2,1)S(1)}, bf16[2,10,256,128]{3,2,1,0:T(8,128)(2,1)}, u32[]{:S(2)}, u32[]{:S(2)}) collective-permute-start(bf16[2,10,256,128]{3,2,1,0:T(8,128)(2,1)S(1)} %pad_maximum_fusion.8), channel_id=1, source_target_pairs={{0,8},{4,12},{8,16},{12,20},{16,24},{20,28},{1,9},{5,13},{9,17},{1... | collective-permute-start | bytes 3932168 | tf_op jit(solution)/shard_map/ppermute | solution.py:22
  48.6 31.4 %collective-permute-start.2 = (bf16[2,10,256,128]{3,2,1,0:T(8,128)(2,1)S(1)}, bf16[2,10,256,128]{3,2,1,0:T(8,128)(2,1)}, u32[]{:S(2)}, u32[]{:S(2)}) collective-permute-start(bf16[2,10,256,128]{3,2,1,0:T(8,128)(2,1)S(1)} %pad_maximum_fusion.8), channel_id=1, source_target_pairs={{8,0},{12,4},{16,8},{20,12},{24,16},{28,20},{9,1},{13,5},{17,9},{2... | collective-permute-start | bytes 3932168 | tf_op jit(solution)/shard_map/ppermute | solution.py:22
  83.1 13.6 %copy-start = (bf16[10,3,256,128]{3,2,1,0:T(8,128)(2,1)}, bf16[10,3,256,128]{3,2,1,0:T(8,128)(2,1)S(1)}, u32[]{:S(2)}) copy-start(bf16[10,3,256,128]{3,2,1,0:T(8,128)(2,1)S(1)} %get-tuple-element.685) | copy-start | bytes 5898244 | tf_op jit(solution)/shard_map/while
  102.9 1.6 copy-start.1
  104.5 13.6 %copy-start = (bf16[10,3,256,128]{3,2,1,0:T(8,128)(2,1)}, bf16[10,3,256,128]{3,2,1,0:T(8,128)(2,1)S(1)}, u32[]{:S(2)}) copy-start(bf16[10,3,256,128]{3,2,1,0:T(8,128)(2,1)S(1)} %get-tuple-element.685) | copy-start | bytes 5898244 | tf_op jit(solution)/shard_map/while
  124.2 1.7 copy-start.1
  126.0 13.6 %copy-start = (bf16[10,3,256,128]{3,2,1,0:T(8,128)(2,1)}, bf16[10,3,256,128]{3,2,1,0:T(8,128)(2,1)S(1)}, u32[]{:S(2)}) copy-start(bf16[10,3,256,128]{3,2,1,0:T(8,128)(2,1)S(1)} %get-tuple-element.685) | copy-start | bytes 5898244 | tf_op jit(solution)/shard_map/while
  145.7 1.6 copy-start.1
  147.4 11.4 %copy-start = (bf16[10,3,256,128]{3,2,1,0:T(8,128)(2,1)}, bf16[10,3,256,128]{3,2,1,0:T(8,128)(2,1)S(1)}, u32[]{:S(2)}) copy-start(bf16[10,3,256,128]{3,2,1,0:T(8,128)(2,1)S(1)} %get-tuple-element.685) | copy-start | bytes 5898244 | tf_op jit(solution)/shard_map/while
  162.8 1.7 copy-start.1
  164.5 13.6 %copy-start = (bf16[10,3,256,128]{3,2,1,0:T(8,128)(2,1)}, bf16[10,3,256,128]{3,2,1,0:T(8,128)(2,1)S(1)}, u32[]{:S(2)}) copy-start(bf16[10,3,256,128]{3,2,1,0:T(8,128)(2,1)S(1)} %get-tuple-element.685) | copy-start | bytes 5898244 | tf_op jit(solution)/shard_map/while
  184.2 1.7 copy-start.1
  185.9 13.6 %copy-start = (bf16[10,3,256,128]{3,2,1,0:T(8,128)(2,1)}, bf16[10,3,256,128]{3,2,1,0:T(8,128)(2,1)S(1)}, u32[]{:S(2)}) copy-start(bf16[10,3,256,128]{3,2,1,0:T(8,128)(2,1)S(1)} %get-tuple-element.685) | copy-start | bytes 5898244 | tf_op jit(solution)/shard_map/while
  205.6 1.7 copy-start.1
  207.3 11.4 %copy-start = (bf16[10,3,256,128]{3,2,1,0:T(8,128)(2,1)}, bf16[10,3,256,128]{3,2,1,0:T(8,128)(2,1)S(1)}, u32[]{:S(2)}) copy-start(bf16[10,3,256,128]{3,2,1,0:T(8,128)(2,1)S(1)} %get-tuple-element.685) | copy-start | bytes 5898244 | tf_op jit(solution)/shard_map/while
  222.7 1.6 copy-start.1
  224.4 13.6 %copy-start = (bf16[10,3,256,128]{3,2,1,0:T(8,128)(2,1)}, bf16[10,3,256,128]{3,2,1,0:T(8,128)(2,1)S(1)}, u32[]{:S(2)}) copy-start(bf16[10,3,256,128]{3,2,1,0:T(8,128)(2,1)S(1)} %get-tuple-element.685) | copy-start | bytes 5898244 | tf_op jit(solution)/shard_map/while
  244.1 1.7 copy-start.1
  245.8 13.6 %copy-start = (bf16[10,3,256,128]{3,2,1,0:T(8,128)(2,1)}, bf16[10,3,256,128]{3,2,1,0:T(8,128)(2,1)S(1)}, u32[]{:S(2)}) copy-start(bf16[10,3,256,128]{3,2,1,0:T(8,128)(2,1)S(1)} %get-tuple-element.685) | copy-start | bytes 5898244 | tf_op jit(solution)/shard_map/while
  265.5 1.6 copy-start.1
  267.1 11.4 %copy-start = (bf16[10,3,256,128]{3,2,1,0:T(8,128)(2,1)}, bf16[10,3,256,128]{3,2,1,0:T(8,128)(2,1)S(1)}, u32[]{:S(2)}) copy-start(bf16[10,3,256,128]{3,2,1,0:T(8,128)(2,1)S(1)} %get-tuple-element.685) | copy-start | bytes 5898244 | tf_op jit(solution)/shard_map/while
  282.6 1.7 copy-start.1
  284.3 3.3 copy-start.2
  288.0 95.8 %collective-permute-start.3 = (f32[2,10,256,128]{3,2,1,0:T(8,128)S(1)}, f32[2,10,256,128]{3,2,1,0:T(8,128)S(1)}, u32[]{:S(2)}, u32[]{:S(2)}) collective-permute-start(f32[2,10,256,128]{3,2,1,0:T(8,128)S(1)} %pad_maximum_fusion.4), channel_id=1, source_target_pairs={{8,0},{12,4},{16,8},{20,12},{24,16},{28,20},{9,1},{13,5},{17,9},{2... | collective-permute-start | bytes 7864328 | tf_op jit(solution)/shard_map/ppermute | solution.py:22
  289.6 95.7 %collective-permute-start.4 = (f32[2,10,256,128]{3,2,1,0:T(8,128)S(1)}, f32[2,10,256,128]{3,2,1,0:T(8,128)S(1)}, u32[]{:S(2)}, u32[]{:S(2)}) collective-permute-start(f32[2,10,256,128]{3,2,1,0:T(8,128)S(1)} %pad_maximum_fusion.5), channel_id=1, source_target_pairs={{0,8},{4,12},{8,16},{12,20},{16,24},{20,28},{1,9},{5,13},{9,17},{1... | collective-permute-start | bytes 7864328 | tf_op jit(solution)/shard_map/ppermute | solution.py:22
  385.9 1.1 copy-start.3
  387.3 24.6 %collective-permute-start.5 = (bf16[1,1,3,128,10,128]{5,3,4,2,1,0:T(8,128)(2,1)S(1)}, bf16[1,1,3,128,10,128]{5,3,4,2,1,0:T(8,128)(2,1)S(1)}, u32[]{:S(2)}, u32[]{:S(2)}) collective-permute-start(bf16[1,1,3,128,10,128]{5,3,4,2,1,0:T(8,128)(2,1)S(1)} %broadcast_select_fusion.1), channel_id=1, source_target_pairs={{0,4},{4,0},{8,12},{12,8},{16,20},{20,16},{24,28},{28,24},{1,5},{5... | collective-permute-start | bytes 2949128 | tf_op jit(solution)/shard_map/ppermute | solution.py:16
where the time goes:
time: 422 us; the launch traced here: 418 us
  waiting for transfers between devices  129 us (31%)
  local copies, waits for them, and re-layouts  106 us (25%)
  other arithmetic  59 us (14%)
  starting transfers between devices  58.2 us (14%)
  matrix products  41.4 us (10%)
  loops' own time  23.5 us (6%)
    ppermute x4, waiting for transfers between devices, from_behind(): return lax.ppermute(block, axis, route)  82 us
    ppermute x4, starting transfers between devices, from_behind(): return lax.ppermute(block, axis, route)  49.3 us
    ppermute x2, waiting for transfers between devices, swapped(): return lax.ppermute(value, axis, pairs)  46.7 us
    another operation x69, local copies, waits for them, and re-layouts  28.4 us
    dot_general x17, matrix products, side_scores(): jnp.einsum('qe,ke->qk', query_rows, key_block, preferred_element_type=jnp...  24.7 us
    another operation x1, loops' own time, per_device(): lax.map(partial(own_pass, score_scale=score_scale, with_sides=True), (que...  20.6 us
    cond x17, local copies, waits for them, and re-layouts, own_pass(): lax.cond(actives[side_index], partial(side_scores, query_rows, key_sets[s...  18.3 us
    cond x34, local copies, waits for them, and re-layouts  11.7 us
  transfers between devices with their start and end apart: 6, of which 6 were waited for; matrix products, arithmetic and copies ran while one was open for 1% of the time, Pallas kernels for 0%

commit v1 on v0

v1 whole, which is shorter than its diff:
```python
from functools import partial
import math

import jax
import jax.numpy as jnp
from jax import lax
from jax.experimental import pallas as pl
from jax.experimental.pallas import tpu as pltpu
from jax.sharding import PartitionSpec as P

RANGE = 2
NEVER = -1e30
VMEM_BYTES = 40 * 2**20


def across(value, axis):
    size = lax.axis_size(axis)
    return lax.ppermute(value, axis, [(i, i ^ 1) for i in range(size)])


def partner_of(index, kind, range_total):
    other = index ^ 1 if kind == 0 else (index - 1 if index % 2 == 0 else index + 1)
    return other if 0 <= other < range_total else None


def beside(value, axis, kind):
    size = lax.axis_size(axis)
    pairs = []
    for i in range(size):
        other = partner_of(i // RANGE, kind, size // RANGE)
        if other is not None:
            pairs.append((i, other * RANGE + i % RANGE))
    return lax.ppermute(value, axis, pairs)


def nt(left, right):
    return lax.dot_general(left, right, (((1,), (1,)), ((), ())), preferred_element_type=jnp.float32)


def nn(left, right):
    return lax.dot_general(left, right, (((1,), (0,)), ((), ())), preferred_element_type=jnp.float32)


def tn(left, right):
    return lax.dot_general(left, right, (((0,), (0,)), ((), ())), preferred_element_type=jnp.float32)


def both(keep, other, head, which):
    return jnp.concatenate([keep[head, which], other[head, which]], axis=0)


def biased(scores, biases, block):
    rows = []
    for a in range(2):
        rows.append(
            jnp.concatenate(
                [
                    scores[a * block : (a + 1) * block, b * block : (b + 1) * block] + biases[a][b]
                    for b in range(2)
                ],
                axis=1,
            )
        )
    return jnp.concatenate(rows, axis=0)


def query_kernel(factor, scale, heads, table, qd_k, qd_o, *refs):
    key_refs, (dq_k, dq_o, stats) = refs[:6], refs[6:]
    block = qd_k.shape[2]
    first = pl.program_id(0) * heads
    for head in range(heads):
        queries = both(qd_k, qd_o, head, 0)
        grads = both(qd_k, qd_o, head, 1)
        scores = []
        for side in range(3):
            keys = both(key_refs[2 * side], key_refs[2 * side + 1], head, 0)
            at = (first + head) * 24 + side * 8
            biases = [[table[at + 2 * a + b] for b in range(2)] for a in range(2)]
            scores.append(biased(nt(keys, queries) * factor, biases, block))
        peak = jnp.max(jnp.maximum(jnp.maximum(scores[0], scores[1]), scores[2]), axis=0, keepdims=True)
        exps = [jnp.exp2(element - peak) for element in scores]
        total = jnp.sum(exps[0] + exps[1] + exps[2], axis=0, keepdims=True)
        weight_grads = [
            nt(both(key_refs[2 * side], key_refs[2 * side + 1], head, 1), grads) for side in range(3)
        ]
        mixed = exps[0] * weight_grads[0] + exps[1] * weight_grads[1] + exps[2] * weight_grads[2]
        inverse = 1.0 / total
        delta = jnp.sum(mixed, axis=0, keepdims=True) * inverse
        result = None
        for side in range(3):
            score_grad = (exps[side] * inverse * (weight_grads[side] - delta)).astype(jnp.bfloat16)
            term = tn(score_grad, both(key_refs[2 * side], key_refs[2 * side + 1], head, 0))
            result = term if result is None else result + term
        result = (result * scale).astype(jnp.bfloat16)
        dq_k[head] = result[:block]
        dq_o[head] = result[block:]
        stats[head, 0:1, :] = peak + jnp.log2(total)
        stats[head, 1:2, :] = delta


def key_kernel(factor, scale, heads, offset, table, kv_k, kv_o, *refs):
    query_refs, stat_refs, (dkv_k, dkv_o) = refs[:6], refs[6:9], refs[9:]
    block = kv_k.shape[2]
    first = pl.program_id(0) * heads + offset
    for head in range(heads):
        keys = both(kv_k, kv_o, head, 0)
        values = both(kv_k, kv_o, head, 1)
        key_grad = None
        value_grad = None
        for side in range(3):
            queries = both(query_refs[2 * side], query_refs[2 * side + 1], head, 0)
            grads = both(query_refs[2 * side], query_refs[2 * side + 1], head, 1)
            at = (first + head) * 24 + side * 8 + 4
            biases = [[table[at + 2 * a + b] for b in range(2)] for a in range(2)]
            level = stat_refs[side][head, 0:1, :]
            delta = stat_refs[side][head, 1:2, :]
            weights = jnp.exp2(biased(nt(keys, queries) * factor, biases, block) - level)
            weight_grad = nt(values, grads)
            score_grad = (weights * (weight_grad - delta)).astype(jnp.bfloat16)
            value_term = nn(weights.astype(jnp.bfloat16), grads)
            key_term = nn(score_grad, queries)
            value_grad = value_term if value_grad is None else value_grad + value_term
            key_grad = key_term if key_grad is None else key_grad + key_term
        key_grad = (key_grad * scale).astype(jnp.bfloat16)
        value_grad = value_grad.astype(jnp.bfloat16)
        dkv_k[head, 0] = key_grad[:block]
        dkv_o[head, 0] = key_grad[block:]
        dkv_k[head, 1] = value_grad[:block]
        dkv_o[head, 1] = value_grad[block:]


def bias_table(block_mask, heads, range_index, position, range_total):
    reach = (block_mask.shape[2] - 1) // 2
    even = range_index % 2 == 0
    ranges = jnp.stack(
        [range_index, range_index ^ 1, jnp.where(even, range_index - 1, range_index + 1)]
    )
    slots = jnp.stack([position, 1 - position])
    mine = range_index * RANGE + slots
    others = ranges[:, None] * RANGE + slots[None, :]
    shape = (3, 2, 2)
    key_first = jnp.broadcast_to(others[:, :, None], shape)
    query_first = jnp.broadcast_to(mine[None, None, :], shape)
    key_second = jnp.broadcast_to(mine[None, :, None], shape)
    query_second = jnp.broadcast_to(others[:, None, :], shape)
    key = jnp.stack([key_first, key_second], axis=1)
    query = jnp.stack([query_first, query_second], axis=1)
    total = range_total * RANGE
    inside = (key >= 0) & (key < total) & (query >= 0) & (query < total) & (abs(key - query) <= reach)
    picked = jax.nn.one_hot(query.reshape(-1), total, dtype=jnp.int32)[:, :, None] * (
        jax.nn.one_hot((key - query + reach).reshape(-1), 2 * reach + 1, dtype=jnp.int32)[:, None, :]
    )
    own = lax.dynamic_slice_in_dim(block_mask, position * heads, heads)
    found = jnp.sum(own[:, None] * picked[None], axis=(2, 3))
    allowed = (found > 0) & inside.reshape(-1)[None]
    return jnp.where(allowed, 0.0, NEVER).astype(jnp.float32).reshape(-1)


def per_device(queries, keys, values, out_grad, block_mask):
    block, head_count, width = queries.shape
    local = head_count // RANGE
    scale = 1.0 / math.sqrt(width)
    factor = scale * math.log2(math.e)
    device = lax.axis_index("seq")
    position = device % RANGE
    range_total = lax.axis_size("seq") // RANGE

    def by_head(left, right):
        return jnp.stack([jnp.transpose(left, (1, 0, 2)), jnp.transpose(right, (1, 0, 2))], axis=1)

    def half(pair, place):
        return lax.dynamic_slice_in_dim(pair, place * local, local)

    kv, qd = by_head(keys, values), by_head(queries, out_grad)
    kv_send, kv_keep = half(kv, 1 - position), half(kv, position)
    qd_send, qd_keep = half(qd, 1 - position), half(qd, position)
    kv_other = across(kv_send, "seq")
    kv_sides = [beside(kv_keep, "seq", 1), beside(kv_keep, "seq", 0)]
    qd_other = across(qd_send, "seq")
    kv_sides_other = [beside(kv_other, "seq", 1), beside(kv_other, "seq", 0)]
    qd_sides = [beside(qd_keep, "seq", 1), beside(qd_keep, "seq", 0)]
    qd_sides_other = [beside(qd_other, "seq", 1), beside(qd_other, "seq", 0)]
    table = bias_table(block_mask, local, device // RANGE, position, range_total)

    heads = 2 if local % 2 == 0 else 1
    pair_spec = pl.BlockSpec((heads, 2, block, width), lambda i: (i, 0, 0, 0))
    one_spec = pl.BlockSpec((heads, block, width), lambda i: (i, 0, 0))
    stat_spec = pl.BlockSpec((heads, 2, 2 * block), lambda i: (i, 0, 0))
    table_spec = pl.BlockSpec(memory_space=pltpu.SMEM)
    params = pltpu.CompilerParams(vmem_limit_bytes=VMEM_BYTES)
    tile = 4 * block * block * width

    dq_keep, dq_send, stats = pl.pallas_call(
        partial(query_kernel, factor, scale, heads),
        grid=(local // heads,),
        in_specs=[table_spec] + [pair_spec] * 8,
        out_specs=[one_spec, one_spec, stat_spec],
        out_shape=[
            jax.ShapeDtypeStruct((local, block, width), jnp.bfloat16),
            jax.ShapeDtypeStruct((local, block, width), jnp.bfloat16),
            jax.ShapeDtypeStruct((local, 2, 2 * block), jnp.float32),
        ],
        compiler_params=params,
        cost_estimate=pl.CostEstimate(
            flops=2 * 9 * local * tile, bytes_accessed=20 * local * block * width * 2, transcendentals=0
        ),
    )(
        table,
        qd_keep,
        qd_other,
        kv_keep,
        kv_other,
        kv_sides[1],
        kv_sides_other[1],
        kv_sides[0],
        kv_sides_other[0],
    )
    stat_sides = [beside(stats, "seq", 1), beside(stats, "seq", 0)]
    dq_back = across(dq_send, "seq")
    dkv_keep, dkv_send = pl.pallas_call(
        partial(key_kernel, factor, scale, heads, 0),
        grid=(local // heads,),
        in_specs=[table_spec] + [pair_spec] * 8 + [stat_spec] * 3,
        out_specs=[pair_spec, pair_spec],
        out_shape=[jax.ShapeDtypeStruct((local, 2, block, width), jnp.bfloat16)] * 2,
        compiler_params=params,
        cost_estimate=pl.CostEstimate(
            flops=2 * 12 * local * tile, bytes_accessed=20 * local * block * width * 2, transcendentals=0
        ),
    )(
        table,
        kv_keep,
        kv_other,
        qd_keep,
        qd_other,
        qd_sides[1],
        qd_sides_other[1],
        qd_sides[0],
        qd_sides_other[0],
        stats,
        stat_sides[1],
        stat_sides[0],
    )
    dkv_back = across(dkv_send, "seq")

    def home(mine, returned):
        low = jnp.where(position == 0, mine, returned)
        high = jnp.where(position == 0, returned, mine)
        return jnp.transpose(jnp.concatenate([low, high], axis=0), (1, 0, 2))

    return (
        home(dq_keep, dq_back),
        home(dkv_keep[:, 0], dkv_back[:, 0]),
        home(dkv_keep[:, 1], dkv_back[:, 1]),
    )


def solution(mesh):
    rows = P(("dp", "seq"), None, None)
    return jax.shard_map(
        per_device,
        mesh=mesh,
        in_specs=(rows, rows, rows, rows, P()),
        out_specs=(rows, rows, rows),
        check_vma=False,
    )
```

time: 422 us -> 111 us (0.26)
  local copies, waits for them, and re-layouts: 106 us -> 1.7 us
  waiting for transfers between devices: 129 us -> 58.7 us
  other arithmetic: 59 us -> 7.17 us
  matrix products: 41.4 us -> 0 us
  starting transfers between devices: 58.2 us -> 23.9 us
  loops' own time: 23.5 us -> 0 us
  Pallas kernels: 0 us -> 17.6 us
    ppermute x6 -> x14, waiting for transfers between devices: 129 us -> 58.7 us  [the longest x4 39 us: across(): return lax.ppermute(value, axis, [(i, i ^ 1) for i in range(size)])]
    dot_general x102 -> x0, matrix products: 41.4 us -> none  [the longest x17 24.7 us: side_scores(): jnp.einsum('qe,ke->qk', query_rows, key_block, preferred_element_type=jnp...]
    ppermute x6 -> x14, starting transfers between devices: 58.2 us -> 23.9 us  [the longest x10 18.8 us: beside(): return lax.ppermute(value, axis, pairs)]
    another operation x73 -> x5, local copies, waits for them, and re-layouts: 34 us -> 0.23 us  [the longest x3 0.23 us: bias_table(): key = jnp.stack([key_first, key_second], axis=1)]
    cond x51 -> x0, local copies, waits for them, and re-layouts: 30 us -> none  [the longest x17 18.3 us: own_pass(): lax.cond(actives[side_index], partial(side_scores, query_rows, key_sets[s...]
    another operation x91 -> x0, loops' own time: 23.5 us -> none  [the longest x1 20.6 us: per_device(): lax.map(partial(own_pass, score_scale=score_scale, with_sides=True), (que...]
    pallas_call x0 -> x2, Pallas kernels: none -> 17.6 us  [the longest x1 9.05 us: per_device(): pl.pallas_call(partial(query_kernel, factor, scale, heads), grid=(local /...]
    reduce_sum x22 -> x1, other arithmetic: 13.3 us -> 0.13 us  [bias_table(): found = jnp.sum(own[:, None] * picked[None], axis=(2, 3))]
  transfers between devices with their start and end apart: 6 -> 14, of which waited for: 6 -> 6; matrix products, arithmetic and copies ran while one was open for 1% -> 4% of each run, Pallas kernels for 0% -> 16%
where the time goes in v1:
time: 111 us; the launch traced here: 110 us
  waiting for transfers between devices  58.7 us (53%)
  starting transfers between devices  23.9 us (22%)
  Pallas kernels  17.6 us (16%)
  other arithmetic  7.17 us (6%)
  local copies, waits for them, and re-layouts  1.7 us (2%)
    ppermute x4, waiting for transfers between devices, across(): return lax.ppermute(value, axis, [(i, i ^ 1) for i in range(size)])  39 us
    ppermute x10, waiting for transfers between devices, beside(): return lax.ppermute(value, axis, pairs)  19.6 us
    ppermute x10, starting transfers between devices, beside(): return lax.ppermute(value, axis, pairs)  18.8 us
    pallas_call x1, Pallas kernels, per_device(): pl.pallas_call(partial(query_kernel, factor, scale, heads), grid=(local /...  9.05 us
    pallas_call x1, Pallas kernels, per_device(): pl.pallas_call(partial(key_kernel, factor, scale, heads, 0), grid=(local...  8.55 us
    ppermute x4, starting transfers between devices, across(): return lax.ppermute(value, axis, [(i, i ^ 1) for i in range(size)])  5.13 us
    another operation x2, other arithmetic, by_head(): jnp.stack([jnp.transpose(left, (1, 0, 2)), jnp.transpose(right, (1, 0, 2)...  3.28 us
  transfers between devices with their start and end apart: 14, of which 6 were waited for; matrix products, arithmetic and copies ran while one was open for 4% of the time, Pallas kernels for 16%

profile of v1, /device:TPU:0, one launch (start us, length us, event | category | flops | bytes accessed | tf_op | source)
XLA Modules:
  0.0 109.9 jit_solution(6105767833117663565)
XLA Ops:
  0.6 0.0 copy-start
  0.7 0.0 copy-start.3
  0.7 0.0 copy-start.4
  0.7 2.3 %fusion = (bf16[10,2,128,128]{3,2,1,0:T(8,128)(2,1)}, bf16[10,2,128,128]{3,2,1,0:T(8,128)(2,1)S(1)}) fusion(s32[]{:T(128)S(6)} %select_n.85, bf16[20,1,128,128]{3,2,1,0:T(8,128)(2,1)} %bitcast.47, bf16[20,1,128,128]{3,2,1,0:T(8,128)(2,1)} %bitcast.48, s32[]{:T(128)S(6)} %select_n.79), kind=kLoop, calls=%fused_computation.8 | loop fusion | flops 655360 | bytes 2621448 | tf_op jit(solution)/shard_map/stack | solution.py:169
  3.0 3.0 %collective-permute-start.2 = (bf16[10,2,128,128]{3,2,1,0:T(8,128)(2,1)S(1)}, bf16[10,2,128,128]{3,2,1,0:T(8,128)(2,1)}, u32[]{:S(2)}, u32[]{:S(2)}) collective-permute-start(bf16[10,2,128,128]{3,2,1,0:T(8,128)(2,1)S(1)} %get-tuple-element.19.refs_0_.kv_k), channel_id=1, source_target_pairs={{0,8},{4,12},{8,0},{12,4},{16,24},{20,28},{24,16},{28,20},{1,9},{5... | collective-permute-start | bytes 1966088 | tf_op jit(solution)/shard_map/ppermute | solution.py:33
  6.0 1.5 %collective-permute-start.4 = (bf16[10,2,128,128]{3,2,1,0:T(8,128)(2,1)S(1)}, bf16[10,2,128,128]{3,2,1,0:T(8,128)(2,1)}, u32[]{:S(2)}, u32[]{:S(2)}) collective-permute-start(bf16[10,2,128,128]{3,2,1,0:T(8,128)(2,1)S(1)} %get-tuple-element.19.refs_0_.kv_k), channel_id=1, source_target_pairs={{8,16},{12,20},{16,8},{20,12},{9,17},{13,21},{17,9},{21,13},{10,18... | collective-permute-start | bytes 1966088 | tf_op jit(solution)/shard_map/ppermute | solution.py:33
  7.6 0.0 copy-done.3
  7.6 0.0 copy-done.4
  7.6 1.0 fusion.2
  8.5 1.5 %collective-permute-start = (bf16[10,2,128,128]{3,2,1,0:T(8,128)(2,1)}, bf16[10,2,128,128]{3,2,1,0:T(8,128)(2,1)S(1)}, u32[]{:S(2)}, u32[]{:S(2)}) collective-permute-start(bf16[10,2,128,128]{3,2,1,0:T(8,128)(2,1)} %get-tuple-element.20), channel_id=1, source_target_pairs={{0,4},{4,0},{8,12},{12,8},{16,20},{20,16},{24,28},{28,24},{1,5},{5... | collective-permute-start | bytes 1966088 | tf_op jit(solution)/shard_map/ppermute | solution.py:18
  10.0 0.5 collective-permute-start.1
  10.5 0.1 broadcast_add_fusion.2
  10.6 0.1 add_multiply_fusion
  10.7 0.1 broadcast_add_fusion
  10.8 0.1 stack_broadcast_in_dim.11
  10.8 0.1 stack_broadcast_in_dim.10
  10.9 0.1 stack.56
  11.0 0.1 eq.66
  11.1 27.8 %collective-permute-done.1.refs_1_.kv_o = bf16[10,2,128,128]{3,2,1,0:T(8,128)(2,1)S(1)} collective-permute-done((bf16[10,2,128,128]{3,2,1,0:T(8,128)(2,1)}, bf16[10,2,128,128]{3,2,1,0:T(8,128)(2,1)S(1)}, u32[]{:S(2)}, u32[]{:S(2)}) %collective-permute-start.1) | collective-permute-done | bytes 655392 | tf_op jit(solution)/shard_map/ppermute | solution.py:18
  39.0 0.0 copy-start.1
  39.0 3.3 %collective-permute-start.3 = (bf16[10,2,128,128]{3,2,1,0:T(8,128)(2,1)S(1)}, bf16[10,2,128,128]{3,2,1,0:T(8,128)(2,1)}, u32[]{:S(2)}, u32[]{:S(2)}) collective-permute-start(bf16[10,2,128,128]{3,2,1,0:T(8,128)(2,1)S(1)} %collective-permute-done.1.refs_1_.kv_o), channel_id=1, source_target_pairs={{0,8},{4,12},{8,0},{12,4},{16,24},{20,28},{24,16},{28,20},{1,9},{5... | collective-permute-start | bytes 1966088 | tf_op jit(solution)/shard_map/ppermute | solution.py:33
  42.3 1.5 %collective-permute-start.5 = (bf16[10,2,128,128]{3,2,1,0:T(8,128)(2,1)S(1)}, bf16[10,2,128,128]{3,2,1,0:T(8,128)(2,1)}, u32[]{:S(2)}, u32[]{:S(2)}) collective-permute-start(bf16[10,2,128,128]{3,2,1,0:T(8,128)(2,1)S(1)} %collective-permute-done.1.refs_1_.kv_o), channel_id=1, source_target_pairs={{8,16},{12,20},{16,8},{20,12},{9,17},{13,21},{17,9},{21,13},{10,18... | collective-permute-start | bytes 1966088 | tf_op jit(solution)/shard_map/ppermute | solution.py:33
  43.8 0.0 copy-done
  43.8 0.1 constant_dynamic-slice_fusion
  43.9 0.1 copy.22
  44.0 0.0 collective-permute-done.qd_o.refs_1_
  44.0 0.8 collective-permute-start.7
  44.8 0.0 collective-permute-done.2.refs_2_
  44.8 1.5 %collective-permute-start.9 = (bf16[10,2,128,128]{3,2,1,0:T(8,128)(2,1)S(1)}, bf16[10,2,128,128]{3,2,1,0:T(8,128)(2,1)}, u32[]{:S(2)}, u32[]{:S(2)}) collective-permute-start(bf16[10,2,128,128]{3,2,1,0:T(8,128)(2,1)S(1)} %get-tuple-element.21.qd_k.refs_0_), channel_id=1, source_target_pairs={{8,16},{12,20},{16,8},{20,12},{9,17},{13,21},{17,9},{21,13},{10,18... | collective-permute-start | bytes 1966088 | tf_op jit(solution)/shard_map/ppermute | solution.py:33
  46.3 0.0 collective-permute-done.4.refs_4_
  46.3 2.2 %collective-permute-start.8 = (bf16[10,2,128,128]{3,2,1,0:T(8,128)(2,1)S(1)}, bf16[10,2,128,128]{3,2,1,0:T(8,128)(2,1)}, u32[]{:S(2)}, u32[]{:S(2)}) collective-permute-start(bf16[10,2,128,128]{3,2,1,0:T(8,128)(2,1)S(1)} %collective-permute-done.qd_o.refs_1_), channel_id=1, source_target_pairs={{0,8},{4,12},{8,0},{12,4},{16,24},{20,28},{24,16},{28,20},{1,9},{5... | collective-permute-start | bytes 1966088 | tf_op jit(solution)/shard_map/ppermute | solution.py:33
  48.5 9.5 %collective-permute-done.3.refs_3_ = bf16[10,2,128,128]{3,2,1,0:T(8,128)(2,1)} collective-permute-done((bf16[10,2,128,128]{3,2,1,0:T(8,128)(2,1)S(1)}, bf16[10,2,128,128]{3,2,1,0:T(8,128)(2,1)}, u32[]{:S(2)}, u32[]{:S(2)}) %collective-permute-start.3) | collective-permute-done | bytes 655392 | tf_op jit(solution)/shard_map/ppermute | solution.py:33
  58.0 1.5 %collective-permute-start.10 = (bf16[10,2,128,128]{3,2,1,0:T(8,128)(2,1)S(1)}, bf16[10,2,128,128]{3,2,1,0:T(8,128)(2,1)}, u32[]{:S(2)}, u32[]{:S(2)}) collective-permute-start(bf16[10,2,128,128]{3,2,1,0:T(8,128)(2,1)S(1)} %collective-permute-done.qd_o.refs_1_), channel_id=1, source_target_pairs={{8,16},{12,20},{16,8},{20,12},{9,17},{13,21},{17,9},{21,13},{10,18... | collective-permute-start | bytes 1966088 | tf_op jit(solution)/shard_map/ppermute | solution.py:33
  59.5 0.1 multiply_reduce_fusion
  59.7 0.1 select_n.84.table
  59.7 0.0 collective-permute-done.5.refs_5_
  59.7 9.1 %shard_map.76 = (bf16[10,128,128]{2,1,0:T(8,128)(2,1)S(1)}, bf16[10,128,128]{2,1,0:T(8,128)(2,1)S(1)}, f32[10,2,256]{2,1,0:T(2,128)S(1)}) custom-call(f32[240]{0:T(256)S(1)} %select_n.84.table, bf16[10,2,128,128]{3,2,1,0:T(8,128)(2,1)S(1)} %get-tuple-element.21.qd_k.refs_0_, bf16[10,2,128,128]{3,2,1,0:T(8,128)(2,1)S(1)} %collective-permute-done.qd_o.refs_1_, ...), custom_call_target="tpu_custom_call" | custom-call | flops 1509949440 | bytes 6553600 | tf_op jit(solution)/shard_map/pallas_call | solution.py:193
  68.8 0.0 copy-done.1
  68.8 2.8 %collective-permute-start.11 = (f32[10,2,256]{2,1,0:T(2,128)S(1)}, f32[10,2,256]{2,1,0:T(2,128)S(1)}, u32[]{:S(2)}, u32[]{:S(2)}) collective-permute-start(f32[10,2,256]{2,1,0:T(2,128)S(1)} %get-tuple-element.10.refs_6_), channel_id=1, source_target_pairs={{0,8},{4,12},{8,0},{12,4},{16,24},{20,28},{24,16},{28,20},{1,9},{5... | collective-permute-start | bytes 61448 | tf_op jit(solution)/shard_map/ppermute | solution.py:33
  71.6 0.4 collective-permute-done.7.refs_2_
  72.0 0.7 collective-permute-start.12
  72.7 0.0 collective-permute-done.9.refs_4_
  72.7 1.6 %collective-permute-start.6 = (bf16[10,128,128]{2,1,0:T(8,128)(2,1)S(1)}, bf16[10,128,128]{2,1,0:T(8,128)(2,1)}, u32[]{:S(2)}, u32[]{:S(2)}) collective-permute-start(bf16[10,128,128]{2,1,0:T(8,128)(2,1)S(1)} %get-tuple-element.9), channel_id=1, source_target_pairs={{0,4},{4,0},{8,12},{12,8},{16,20},{20,16},{24,28},{28,24},{1,5},{5... | collective-permute-start | bytes 983048 | tf_op jit(solution)/shard_map/ppermute | solution.py:18
  74.3 9.6 %collective-permute-done.8.refs_3_ = bf16[10,2,128,128]{3,2,1,0:T(8,128)(2,1)} collective-permute-done((bf16[10,2,128,128]{3,2,1,0:T(8,128)(2,1)S(1)}, bf16[10,2,128,128]{3,2,1,0:T(8,128)(2,1)}, u32[]{:S(2)}, u32[]{:S(2)}) %collective-permute-start.8) | collective-permute-done | bytes 655392 | tf_op jit(solution)/shard_map/ppermute | solution.py:33
  83.9 0.0 collective-permute-done.10.refs_5_
  83.9 0.1 collective-permute-done.11.refs_7_
  84.0 0.0 collective-permute-done.12.refs_8_
  84.0 0.0 copy-start.2
  84.0 1.1 copy-done.2
  85.1 8.5 %shard_map.77 = (bf16[10,2,128,128]{3,2,1,0:T(8,128)(2,1)S(1)}, bf16[10,2,128,128]{3,2,1,0:T(8,128)(2,1)}) custom-call(f32[240]{0:T(256)S(1)} %select_n.84.table, bf16[10,2,128,128]{3,2,1,0:T(8,128)(2,1)S(1)} %get-tuple-element.19.refs_0_.kv_k, bf16[10,2,128,128]{3,2,1,0:T(8,128)(2,1)S(1)} %copy-done.2, ...), custom_call_target="tpu_custom_call" | custom-call | flops 2013265920 | bytes 6553600 | tf_op jit(solution)/shard_map/pallas_call | solution.py:220
  93.7 1.5 %collective-permute-start.13 = (bf16[10,2,128,128]{3,2,1,0:T(8,128)(2,1)}, bf16[10,2,128,128]{3,2,1,0:T(8,128)(2,1)S(1)}, u32[]{:S(2)}, u32[]{:S(2)}) collective-permute-start(bf16[10,2,128,128]{3,2,1,0:T(8,128)(2,1)} %get-tuple-element.12), channel_id=1, source_target_pairs={{0,4},{4,0},{8,12},{12,8},{16,20},{20,16},{24,28},{28,24},{1,5},{5... | collective-permute-start | bytes 1966088 | tf_op jit(solution)/shard_map/ppermute | solution.py:18
  95.2 0.0 collective-permute-done.6
  95.2 1.0 broadcast_select_fusion.1
  96.2 0.9 maximum_bitcast_fusion
  97.1 11.2 %collective-permute-done.13 = bf16[10,2,128,128]{3,2,1,0:T(8,128)(2,1)S(1)} collective-permute-done((bf16[10,2,128,128]{3,2,1,0:T(8,128)(2,1)}, bf16[10,2,128,128]{3,2,1,0:T(8,128)(2,1)S(1)}, u32[]{:S(2)}, u32[]{:S(2)}) %collective-permute-start.13) | collective-permute-done | bytes 655392 | tf_op jit(solution)/shard_map/ppermute | solution.py:18
  108.3 0.3 fusion.5
  108.6 0.1 fusion.4
  108.7 1.2 %maximum_bitcast_fusion.1 = (bf16[128,20,128]{2,0,1:T(8,128)(2,1)}, bf16[128,20,128]{2,0,1:T(8,128)(2,1)}) fusion(bf16[10,128,128]{2,1,0:T(8,128)(2,1)S(1)} %get-tuple-element.16, bf16[10,128,128]{2,1,0:T(8,128)(2,1)S(1)} %get-tuple-element.17, bf16[10,128,128]{2,1,0:T(8,128)(2,1)S(1)} %fusion.4, bf16[10,128,128]{2,1,0:T(8,128)(2,1)S(1)} %get-tuple-element.15), kind=kLoop, calls=%fused_computation.13 | loop fusion | flops 655360 | bytes 2621440 | tf_op jit(solution)/shard_map/transpose | solution.py:249
  (10 shorter events, 0.1 us)
Async XLA Ops:
  0.6 43.2 %copy-start = (s32[20,8,5]{0,1,2:T(8,128)S(1)}, s32[20,8,5]{0,1,2:T(8,128)}, u32[]{:S(2)}) copy-start(s32[20,8,5]{0,1,2:T(8,128)} %param.9) | copy-start | bytes 9604
  0.7 6.9 %copy-start.3 = (bf16[128,20,128]{2,0,1:T(8,128)(2,1)S(1)}, bf16[128,20,128]{2,0,1:T(8,128)(2,1)}, u32[]{:S(2)}) copy-start(bf16[128,20,128]{2,0,1:T(8,128)(2,1)} %param.5) | copy-start | bytes 1966084
  0.7 6.9 %copy-start.4 = (bf16[128,20,128]{2,0,1:T(8,128)(2,1)S(1)}, bf16[128,20,128]{2,0,1:T(8,128)(2,1)}, u32[]{:S(2)}) copy-start(bf16[128,20,128]{2,0,1:T(8,128)(2,1)} %param.8) | copy-start | bytes 1966084
  3.0 41.8 %collective-permute-start.2 = (bf16[10,2,128,128]{3,2,1,0:T(8,128)(2,1)S(1)}, bf16[10,2,128,128]{3,2,1,0:T(8,128)(2,1)}, u32[]{:S(2)}, u32[]{:S(2)}) collective-permute-start(bf16[10,2,128,128]{3,2,1,0:T(8,128)(2,1)S(1)} %get-tuple-element.19.refs_0_.kv_k), channel_id=1, source_target_pairs={{0,8},{4,12},{8,0},{12,4},{16,24},{20,28},{24,16},{28,20},{1,9},{5... | collective-permute-start | bytes 1966088 | tf_op jit(solution)/shard_map/ppermute | solution.py:33
  6.0 40.2 %collective-permute-start.4 = (bf16[10,2,128,128]{3,2,1,0:T(8,128)(2,1)S(1)}, bf16[10,2,128,128]{3,2,1,0:T(8,128)(2,1)}, u32[]{:S(2)}, u32[]{:S(2)}) collective-permute-start(bf16[10,2,128,128]{3,2,1,0:T(8,128)(2,1)S(1)} %get-tuple-element.19.refs_0_.kv_k), channel_id=1, source_target_pairs={{8,16},{12,20},{16,8},{20,12},{9,17},{13,21},{17,9},{21,13},{10,18... | collective-permute-start | bytes 1966088 | tf_op jit(solution)/shard_map/ppermute | solution.py:33
  8.5 35.5 %collective-permute-start = (bf16[10,2,128,128]{3,2,1,0:T(8,128)(2,1)}, bf16[10,2,128,128]{3,2,1,0:T(8,128)(2,1)S(1)}, u32[]{:S(2)}, u32[]{:S(2)}) collective-permute-start(bf16[10,2,128,128]{3,2,1,0:T(8,128)(2,1)} %get-tuple-element.20), channel_id=1, source_target_pairs={{0,4},{4,0},{8,12},{12,8},{16,20},{20,16},{24,28},{28,24},{1,5},{5... | collective-permute-start | bytes 1966088 | tf_op jit(solution)/shard_map/ppermute | solution.py:18
  10.0 28.9 %collective-permute-start.1 = (bf16[10,2,128,128]{3,2,1,0:T(8,128)(2,1)}, bf16[10,2,128,128]{3,2,1,0:T(8,128)(2,1)S(1)}, u32[]{:S(2)}, u32[]{:S(2)}) collective-permute-start(bf16[10,2,128,128]{3,2,1,0:T(8,128)(2,1)} %get-tuple-element.18), channel_id=1, source_target_pairs={{0,4},{4,0},{8,12},{12,8},{16,20},{20,16},{24,28},{28,24},{1,5},{5... | collective-permute-start | bytes 1966088 | tf_op jit(solution)/shard_map/ppermute | solution.py:18
  39.0 29.8 %copy-start.1 = (bf16[10,2,128,128]{3,2,1,0:T(8,128)(2,1)}, bf16[10,2,128,128]{3,2,1,0:T(8,128)(2,1)S(1)}, u32[]{:S(2)}) copy-start(bf16[10,2,128,128]{3,2,1,0:T(8,128)(2,1)S(1)} %collective-permute-done.1.refs_1_.kv_o) | copy-start | bytes 1966084
  39.0 19.0 %collective-permute-start.3 = (bf16[10,2,128,128]{3,2,1,0:T(8,128)(2,1)S(1)}, bf16[10,2,128,128]{3,2,1,0:T(8,128)(2,1)}, u32[]{:S(2)}, u32[]{:S(2)}) collective-permute-start(bf16[10,2,128,128]{3,2,1,0:T(8,128)(2,1)S(1)} %collective-permute-done.1.refs_1_.kv_o), channel_id=1, source_target_pairs={{0,8},{4,12},{8,0},{12,4},{16,24},{20,28},{24,16},{28,20},{1,9},{5... | collective-permute-start | bytes 1966088 | tf_op jit(solution)/shard_map/ppermute | solution.py:33
  42.3 17.5 %collective-permute-start.5 = (bf16[10,2,128,128]{3,2,1,0:T(8,128)(2,1)S(1)}, bf16[10,2,128,128]{3,2,1,0:T(8,128)(2,1)}, u32[]{:S(2)}, u32[]{:S(2)}) collective-permute-start(bf16[10,2,128,128]{3,2,1,0:T(8,128)(2,1)S(1)} %collective-permute-done.1.refs_1_.kv_o), channel_id=1, source_target_pairs={{8,16},{12,20},{16,8},{20,12},{9,17},{13,21},{17,9},{21,13},{10,18... | collective-permute-start | bytes 1966088 | tf_op jit(solution)/shard_map/ppermute | solution.py:33
  44.0 28.0 %collective-permute-start.7 = (bf16[10,2,128,128]{3,2,1,0:T(8,128)(2,1)S(1)}, bf16[10,2,128,128]{3,2,1,0:T(8,128)(2,1)}, u32[]{:S(2)}, u32[]{:S(2)}) collective-permute-start(bf16[10,2,128,128]{3,2,1,0:T(8,128)(2,1)S(1)} %get-tuple-element.21.qd_k.refs_0_), channel_id=1, source_target_pairs={{0,8},{4,12},{8,0},{12,4},{16,24},{20,28},{24,16},{28,20},{1,9},{5... | collective-permute-start | bytes 1966088 | tf_op jit(solution)/shard_map/ppermute | solution.py:33
  44.8 27.9 %collective-permute-start.9 = (bf16[10,2,128,128]{3,2,1,0:T(8,128)(2,1)S(1)}, bf16[10,2,128,128]{3,2,1,0:T(8,128)(2,1)}, u32[]{:S(2)}, u32[]{:S(2)}) collective-permute-start(bf16[10,2,128,128]{3,2,1,0:T(8,128)(2,1)S(1)} %get-tuple-element.21.qd_k.refs_0_), channel_id=1, source_target_pairs={{8,16},{12,20},{16,8},{20,12},{9,17},{13,21},{17,9},{21,13},{10,18... | collective-permute-start | bytes 1966088 | tf_op jit(solution)/shard_map/ppermute | solution.py:33
  46.3 37.6 %collective-permute-start.8 = (bf16[10,2,128,128]{3,2,1,0:T(8,128)(2,1)S(1)}, bf16[10,2,128,128]{3,2,1,0:T(8,128)(2,1)}, u32[]{:S(2)}, u32[]{:S(2)}) collective-permute-start(bf16[10,2,128,128]{3,2,1,0:T(8,128)(2,1)S(1)} %collective-permute-done.qd_o.refs_1_), channel_id=1, source_target_pairs={{0,8},{4,12},{8,0},{12,4},{16,24},{20,28},{24,16},{28,20},{1,9},{5... | collective-permute-start | bytes 1966088 | tf_op jit(solution)/shard_map/ppermute | solution.py:33
  58.0 25.9 %collective-permute-start.10 = (bf16[10,2,128,128]{3,2,1,0:T(8,128)(2,1)S(1)}, bf16[10,2,128,128]{3,2,1,0:T(8,128)(2,1)}, u32[]{:S(2)}, u32[]{:S(2)}) collective-permute-start(bf16[10,2,128,128]{3,2,1,0:T(8,128)(2,1)S(1)} %collective-permute-done.qd_o.refs_1_), channel_id=1, source_target_pairs={{8,16},{12,20},{16,8},{20,12},{9,17},{13,21},{17,9},{21,13},{10,18... | collective-permute-start | bytes 1966088 | tf_op jit(solution)/shard_map/ppermute | solution.py:33
  68.8 15.2 %collective-permute-start.11 = (f32[10,2,256]{2,1,0:T(2,128)S(1)}, f32[10,2,256]{2,1,0:T(2,128)S(1)}, u32[]{:S(2)}, u32[]{:S(2)}) collective-permute-start(f32[10,2,256]{2,1,0:T(2,128)S(1)} %get-tuple-element.10.refs_6_), channel_id=1, source_target_pairs={{0,8},{4,12},{8,0},{12,4},{16,24},{20,28},{24,16},{28,20},{1,9},{5... | collective-permute-start | bytes 61448 | tf_op jit(solution)/shard_map/ppermute | solution.py:33
  72.0 12.0 %collective-permute-start.12 = (f32[10,2,256]{2,1,0:T(2,128)S(1)}, f32[10,2,256]{2,1,0:T(2,128)S(1)}, u32[]{:S(2)}, u32[]{:S(2)}) collective-permute-start(f32[10,2,256]{2,1,0:T(2,128)S(1)} %get-tuple-element.10.refs_6_), channel_id=1, source_target_pairs={{8,16},{12,20},{16,8},{20,12},{9,17},{13,21},{17,9},{21,13},{10,18... | collective-permute-start | bytes 61448 | tf_op jit(solution)/shard_map/ppermute | solution.py:33
  72.7 22.5 %collective-permute-start.6 = (bf16[10,128,128]{2,1,0:T(8,128)(2,1)S(1)}, bf16[10,128,128]{2,1,0:T(8,128)(2,1)}, u32[]{:S(2)}, u32[]{:S(2)}) collective-permute-start(bf16[10,128,128]{2,1,0:T(8,128)(2,1)S(1)} %get-tuple-element.9), channel_id=1, source_target_pairs={{0,4},{4,0},{8,12},{12,8},{16,20},{20,16},{24,28},{28,24},{1,5},{5... | collective-permute-start | bytes 983048 | tf_op jit(solution)/shard_map/ppermute | solution.py:18
  84.0 1.1 copy-start.2
  93.7 14.7 %collective-permute-start.13 = (bf16[10,2,128,128]{3,2,1,0:T(8,128)(2,1)}, bf16[10,2,128,128]{3,2,1,0:T(8,128)(2,1)S(1)}, u32[]{:S(2)}, u32[]{:S(2)}) collective-permute-start(bf16[10,2,128,128]{3,2,1,0:T(8,128)(2,1)} %get-tuple-element.12), channel_id=1, source_target_pairs={{0,4},{4,0},{8,12},{12,8},{16,20},{20,16},{24,28},{28,24},{1,5},{5... | collective-permute-start | bytes 1966088 | tf_op jit(solution)/shard_map/ppermute | solution.py:18

commit v2 on v1

--- a/solution.py
+++ b/solution.py
@@ -10,7 +10,13 @@
 
 RANGE = 2
 NEVER = -1e30
+WORK = 8
 VMEM_BYTES = 40 * 2**20
+
+
+def cut_heads(local):
+    step = (2 * local // 5 + 1) // 2 * 2
+    return sorted({0, min(step, local), min(2 * step, local), local})
 
 
 def across(value, axis):
@@ -18,19 +24,26 @@
     return lax.ppermute(value, axis, [(i, i ^ 1) for i in range(size)])
 
 
+def after(value, *earlier):
+    return lax.optimization_barrier((value, *earlier))[0]
+
+
 def partner_of(index, kind, range_total):
     other = index ^ 1 if kind == 0 else (index - 1 if index % 2 == 0 else index + 1)
     return other if 0 <= other < range_total else None
 
 
-def beside(value, axis, kind):
-    size = lax.axis_size(axis)
+def beside(value, kind):
+    size, clips = lax.axis_size("seq"), lax.axis_size("dp")
     pairs = []
     for i in range(size):
         other = partner_of(i // RANGE, kind, size // RANGE)
-        if other is not None:
-            pairs.append((i, other * RANGE + i % RANGE))
-    return lax.ppermute(value, axis, pairs)
+        for clip in range(clips):
+            if other is not None:
+                pairs.append((i * clips + clip, (other * RANGE + i % RANGE) * clips + clip))
+            elif clips % 2 == 0:
+                pairs.append((i * clips + clip, i * clips + (clip ^ 1)))
+    return lax.ppermute(value, ("seq", "dp"), pairs)
 
 
 def nt(left, right):
@@ -98,8 +111,8 @@
         stats[head, 1:2, :] = delta
 
 
-def key_kernel(factor, scale, heads, offset, table, kv_k, kv_o, *refs):
-    query_refs, stat_refs, (dkv_k, dkv_o) = refs[:6], refs[6:9], refs[9:]
+def key_kernel(factor, scale, heads, offset, table, kv_k, kv_o, qd_k, qd_o, side_a, side_b, *refs):
+    stat_refs, (dkv_k, dkv_o) = refs[:3], refs[3:]
     block = kv_k.shape[2]
     first = pl.program_id(0) * heads + offset
     for head in range(heads):
@@ -108,8 +121,12 @@
         key_grad = None
         value_grad = None
         for side in range(3):
-            queries = both(query_refs[2 * side], query_refs[2 * side + 1], head, 0)
-            grads = both(query_refs[2 * side], query_refs[2 * side + 1], head, 1)
+            if side == 0:
+                queries, grads = both(qd_k, qd_o, head, 0), both(qd_k, qd_o, head, 1)
+            else:
+                ref = (side_a, side_b)[side - 1]
+                queries = jnp.concatenate([ref[head, 0], ref[head, 2]], axis=0)
+                grads = jnp.concatenate([ref[head, 1], ref[head, 3]], axis=0)
             at = (first + head) * 24 + side * 8 + 4
             biases = [[table[at + 2 * a + b] for b in range(2)] for a in range(2)]
             level = stat_refs[side][head, 0:1, :]
@@ -172,18 +189,23 @@
         return lax.dynamic_slice_in_dim(pair, place * local, local)
 
     kv, qd = by_head(keys, values), by_head(queries, out_grad)
-    kv_send, kv_keep = half(kv, 1 - position), half(kv, position)
+    kv_send = half(kv, 1 - position)
+    kv_keep = half(after(kv, kv_send), position)
     qd_send, qd_keep = half(qd, 1 - position), half(qd, position)
     kv_other = across(kv_send, "seq")
-    kv_sides = [beside(kv_keep, "seq", 1), beside(kv_keep, "seq", 0)]
-    qd_other = across(qd_send, "seq")
-    kv_sides_other = [beside(kv_other, "seq", 1), beside(kv_other, "seq", 0)]
-    qd_sides = [beside(qd_keep, "seq", 1), beside(qd_keep, "seq", 0)]
-    qd_sides_other = [beside(qd_other, "seq", 1), beside(qd_other, "seq", 0)]
+    kv_sides = [beside(kv_keep, 0), beside(kv_keep, 1)]
+    qd_other = across(after(qd_send, kv_other), "seq")
+    kv_sides_other = [beside(kv_other, 0), beside(kv_other, 1)]
+    cuts = cut_heads(local)
+    qd_pieces = [
+        jnp.concatenate([qd_keep[low:high], qd_other[low:high]], axis=1) for low, high in zip(cuts, cuts[1:])
+    ]
+    qd_sides = [[beside(qd_pieces[0], 0), beside(qd_pieces[0], 1)]]
     table = bias_table(block_mask, local, device // RANGE, position, range_total)
 
     heads = 2 if local % 2 == 0 else 1
     pair_spec = pl.BlockSpec((heads, 2, block, width), lambda i: (i, 0, 0, 0))
+    quad_spec = pl.BlockSpec((heads, 4, block, width), lambda i: (i, 0, 0, 0))
     one_spec = pl.BlockSpec((heads, block, width), lambda i: (i, 0, 0))
     stat_spec = pl.BlockSpec((heads, 2, 2 * block), lambda i: (i, 0, 0))
     table_spec = pl.BlockSpec(memory_space=pltpu.SMEM)
@@ -202,7 +224,7 @@
         ],
         compiler_params=params,
         cost_estimate=pl.CostEstimate(
-            flops=2 * 9 * local * tile, bytes_accessed=20 * local * block * width * 2, transcendentals=0
+            flops=WORK * 2 * 9 * local * tile, bytes_accessed=20 * local * block * width * 2, transcendentals=0
         ),
     )(
         table,
@@ -210,38 +232,46 @@
         qd_other,
         kv_keep,
         kv_other,
+        kv_sides[0],
+        kv_sides_other[0],
         kv_sides[1],
         kv_sides_other[1],
-        kv_sides[0],
-        kv_sides_other[0],
-    )
-    stat_sides = [beside(stats, "seq", 1), beside(stats, "seq", 0)]
-    dq_back = across(dq_send, "seq")
-    dkv_keep, dkv_send = pl.pallas_call(
-        partial(key_kernel, factor, scale, heads, 0),
-        grid=(local // heads,),
-        in_specs=[table_spec] + [pair_spec] * 8 + [stat_spec] * 3,
-        out_specs=[pair_spec, pair_spec],
-        out_shape=[jax.ShapeDtypeStruct((local, 2, block, width), jnp.bfloat16)] * 2,
-        compiler_params=params,
-        cost_estimate=pl.CostEstimate(
-            flops=2 * 12 * local * tile, bytes_accessed=20 * local * block * width * 2, transcendentals=0
-        ),
-    )(
-        table,
-        kv_keep,
-        kv_other,
-        qd_keep,
-        qd_other,
-        qd_sides[1],
-        qd_sides_other[1],
-        qd_sides[0],
-        qd_sides_other[0],
-        stats,
-        stat_sides[1],
-        stat_sides[0],
-    )
-    dkv_back = across(dkv_send, "seq")
+    )
+    stat_sides = [beside(stats, 0), beside(stats, 1)]
+    dq_back = across(after(dq_send, *stat_sides), "seq")
+    dkv_keep, dkv_back = [], []
+    for index, (low, high) in enumerate(zip(cuts, cuts[1:])):
+        arrived = qd_sides[index]
+        if index + 1 < len(qd_pieces):
+            piece = after(qd_pieces[index + 1], qd_sides[-1][0])
+            qd_sides.append([beside(piece, 0), beside(piece, 1)])
+        count, shift = high - low, low // heads
+        part_spec = pl.BlockSpec((heads, 2, block, width), lambda i, shift=shift: (i + shift, 0, 0, 0))
+        stat_part = pl.BlockSpec((heads, 2, 2 * block), lambda i, shift=shift: (i + shift, 0, 0))
+        keep, send = pl.pallas_call(
+            partial(key_kernel, factor, scale, heads, low),
+            grid=(count // heads,),
+            in_specs=[table_spec] + [part_spec] * 4 + [quad_spec] * 2 + [stat_part] * 3,
+            out_specs=[pair_spec, pair_spec],
+            out_shape=[jax.ShapeDtypeStruct((count, 2, block, width), jnp.bfloat16)] * 2,
+            compiler_params=params,
+            cost_estimate=pl.CostEstimate(
+                flops=WORK * 2 * 12 * count * tile, bytes_accessed=20 * count * block * width * 2, transcendentals=0
+            ),
+        )(
+            table,
+            kv_keep,
+            kv_other,
+            qd_keep,
+            qd_other,
+            *arrived,
+            stats,
+            *stat_sides,
+        )
+        dkv_keep.append(keep)
+        dkv_back.append(across(send, "seq"))
+    dkv_keep = jnp.concatenate(dkv_keep, axis=0)
+    dkv_back = jnp.concatenate(dkv_back, axis=0)
 
     def home(mine, returned):
         low = jnp.where(position == 0, mine, returned)

time: 111 us -> 84.6 us (0.76)
  waiting for transfers between devices: 58.7 us -> 39.1 us
  starting transfers between devices: 23.9 us -> 19.1 us
    ppermute x10 -> x12, waiting for transfers between devices: 19.6 us -> 5.08 us  [beside(): return lax.ppermute(value, ('seq', 'dp'), pairs)]
    ppermute x10 -> x12, starting transfers between devices: 18.8 us -> 10.3 us  [beside(): return lax.ppermute(value, ('seq', 'dp'), pairs)]
    ppermute x4 -> x6, waiting for transfers between devices: 39 us -> 34 us  [across(): return lax.ppermute(value, axis, [(i, i ^ 1) for i in range(size)])]
    ppermute x4 -> x6, starting transfers between devices: 5.13 us -> 8.83 us  [across(): return lax.ppermute(value, axis, [(i, i ^ 1) for i in range(size)])]
    select_n x2, other arithmetic: 1.32 us -> 0.13 us  [home(): low = jnp.where(position == 0, mine, returned)]
    another operation x2 -> x3, other arithmetic: 3.28 us -> 4.24 us  [by_head(): jnp.stack([jnp.transpose(left, (1, 0, 2)), jnp.transpose(right, (1, 0, 2)...]
    pallas_call x1 -> x3, Pallas kernels: 8.55 us -> 8.34 us  [per_device(): pl.pallas_call(partial(key_kernel, factor, scale, heads, low), grid=(coun...]
  transfers between devices with their start and end apart: 14 -> 18, of which waited for: 6 -> 8; matrix products, arithmetic and copies ran while one was open for 4% -> 5% of each run, Pallas kernels for 16% -> 21%
where the time goes in v2:
time: 84.6 us; the launch traced here: 84.4 us
  waiting for transfers between devices  39.1 us (46%)
  starting transfers between devices  19.1 us (23%)
  Pallas kernels  17.3 us (20%)
  other arithmetic  7.01 us (8%)
  between operations  0.98 us (1%)
  local copies, waits for them, and re-layouts  0.9 us (1%)
    ppermute x6, waiting for transfers between devices, across(): return lax.ppermute(value, axis, [(i, i ^ 1) for i in range(size)])  34 us
    ppermute x12, starting transfers between devices, beside(): return lax.ppermute(value, ('seq', 'dp'), pairs)  10.3 us
    pallas_call x1, Pallas kernels, per_device(): pl.pallas_call(partial(query_kernel, factor, scale, heads), grid=(local /...  8.97 us
    ppermute x6, starting transfers between devices, across(): return lax.ppermute(value, axis, [(i, i ^ 1) for i in range(size)])  8.83 us
    pallas_call x3, Pallas kernels, per_device(): pl.pallas_call(partial(key_kernel, factor, scale, heads, low), grid=(coun...  8.34 us
    ppermute x12, waiting for transfers between devices, beside(): return lax.ppermute(value, ('seq', 'dp'), pairs)  5.08 us
    another operation x3, other arithmetic, by_head(): jnp.stack([jnp.transpose(left, (1, 0, 2)), jnp.transpose(right, (1, 0, 2)...  4.24 us
    transpose x2, other arithmetic, home(): return jnp.transpose(jnp.concatenate([low, high], axis=0), (1, 0, 2))  2.07 us
  transfers between devices with their start and end apart: 18, of which 8 were waited for; matrix products, arithmetic and copies ran while one was open for 5% of the time, Pallas kernels for 21%

profile of v2, /device:TPU:0, one launch (start us, length us, event | category | flops | bytes accessed | tf_op | source)
XLA Modules:
  0.0 84.4 jit_solution(3677077714721558448)
XLA Ops:
  0.6 0.0 copy-start
  0.6 0.0 copy-start.2
  0.7 0.0 copy-start.1
  0.7 2.1 %fusion = bf16[10,2,128,128]{3,2,1,0:T(8,128)(2,1)} fusion(s32[]{:T(128)S(6)} %select_n.85, bf16[20,1,128,128]{3,2,1,0:T(8,128)(2,1)} %bitcast.57, bf16[20,1,128,128]{3,2,1,0:T(8,128)(2,1)} %bitcast.55), kind=kLoop, calls=%fused_computation.7 | loop fusion | flops 327680 | bytes 1966084 | tf_op jit(solution)/shard_map/stack | solution.py:186
  2.8 3.0 %collective-permute-start = (bf16[10,2,128,128]{3,2,1,0:T(8,128)(2,1)}, bf16[10,2,128,128]{3,2,1,0:T(8,128)(2,1)S(1)}, u32[]{:S(2)}, u32[]{:S(2)}) collective-permute-start(bf16[10,2,128,128]{3,2,1,0:T(8,128)(2,1)} %fusion), channel_id=1, source_target_pairs={{0,4},{4,0},{8,12},{12,8},{16,20},{20,16},{24,28},{28,24},{1,5},{5... | collective-permute-start | bytes 1966088 | tf_op jit(solution)/shard_map/ppermute | solution.py:24
  5.7 0.0 copy-done.2
  5.7 0.0 copy-done.1
  5.7 0.1 pad_maximum_fusion
  5.9 0.0 copy-start.3
  5.9 1.6 %collective-permute-start.2 = (bf16[10,2,128,128]{3,2,1,0:T(8,128)(2,1)S(1)}, bf16[10,2,128,128]{3,2,1,0:T(8,128)(2,1)S(1)}, u32[]{:S(2)}, u32[]{:S(2)}) collective-permute-start(bf16[10,2,128,128]{3,2,1,0:T(8,128)(2,1)S(1)} %constant_dynamic-slice_fusion.refs_0_.kv_k), channel_id=1, source_target_pairs={{0,8},{1,9},{2,10},{3,11},{4,12},{5,13},{6,14},{7,15},{8,0},{9,1},... | collective-permute-start | bytes 1966088 | tf_op jit(solution)/shard_map/ppermute | solution.py:46
  7.6 0.0 collective-permute-start.4
  7.6 0.1 broadcast_add_fusion.2
  7.7 0.1 add_multiply_fusion
  7.7 0.1 broadcast_add_fusion
  7.8 0.1 stack_broadcast_in_dim.11
  7.9 0.1 stack_broadcast_in_dim.10
  8.0 0.1 stack.56
  8.1 0.1 eq.66
  8.2 0.0 copy-done
  8.2 0.1 constant_dynamic-slice_fusion.1
  8.3 0.1 copy.24
  8.4 0.1 multiply_reduce_fusion
  8.6 2.0 %fusion.1 = (bf16[10,2,128,128]{3,2,1,0:T(8,128)(2,1)}, bf16[10,2,128,128]{3,2,1,0:T(8,128)(2,1)S(1)}) fusion(s32[]{:T(128)S(6)} %select_n.85, bf16[20,1,128,128]{3,2,1,0:T(8,128)(2,1)S(1)} %bitcast.59, bf16[20,1,128,128]{3,2,1,0:T(8,128)(2,1)} %bitcast.60, s32[]{:T(128)S(6)} %select_n.79), kind=kLoop, calls=%fused_computation.8 | loop fusion | flops 655360 | bytes 2621448 | tf_op jit(solution)/shard_map/stack | solution.py:186
  10.6 10.1 %collective-permute-done.refs_1_.kv_o = bf16[10,2,128,128]{3,2,1,0:T(8,128)(2,1)S(1)} collective-permute-done((bf16[10,2,128,128]{3,2,1,0:T(8,128)(2,1)}, bf16[10,2,128,128]{3,2,1,0:T(8,128)(2,1)S(1)}, u32[]{:S(2)}, u32[]{:S(2)}) %collective-permute-start) | collective-permute-done | bytes 655392 | tf_op jit(solution)/shard_map/ppermute | solution.py:24
  20.7 1.7 %collective-permute-start.1 = (bf16[10,2,128,128]{3,2,1,0:T(8,128)(2,1)}, bf16[10,2,128,128]{3,2,1,0:T(8,128)(2,1)S(1)}, u32[]{:S(2)}, u32[]{:S(2)}) collective-permute-start(bf16[10,2,128,128]{3,2,1,0:T(8,128)(2,1)} %get-tuple-element.17), channel_id=1, source_target_pairs={{0,4},{4,0},{8,12},{12,8},{16,20},{20,16},{24,28},{28,24},{1,5},{5... | collective-permute-start | bytes 1966088 | tf_op jit(solution)/shard_map/ppermute | solution.py:24
  22.4 1.6 %collective-permute-start.3 = (bf16[10,2,128,128]{3,2,1,0:T(8,128)(2,1)S(1)}, bf16[10,2,128,128]{3,2,1,0:T(8,128)(2,1)}, u32[]{:S(2)}, u32[]{:S(2)}) collective-permute-start(bf16[10,2,128,128]{3,2,1,0:T(8,128)(2,1)S(1)} %collective-permute-done.refs_1_.kv_o), channel_id=1, source_target_pairs={{0,8},{1,9},{2,10},{3,11},{4,12},{5,13},{6,14},{7,15},{8,0},{9,1},... | collective-permute-start | bytes 1966088 | tf_op jit(solution)/shard_map/ppermute | solution.py:46
  24.1 0.0 collective-permute-start.5
  24.1 0.1 select_n.84.table
  24.2 12.6 %collective-permute-done.1.qd_o = bf16[10,2,128,128]{3,2,1,0:T(8,128)(2,1)S(1)} collective-permute-done((bf16[10,2,128,128]{3,2,1,0:T(8,128)(2,1)}, bf16[10,2,128,128]{3,2,1,0:T(8,128)(2,1)S(1)}, u32[]{:S(2)}, u32[]{:S(2)}) %collective-permute-start.1) | collective-permute-done | bytes 655392 | tf_op jit(solution)/shard_map/ppermute | solution.py:24
  36.9 1.7 %collective-permute-start.9 = (bf16[4,4,128,128]{3,2,1,0:T(8,128)(2,1)S(1)}, bf16[4,4,128,128]{3,2,1,0:T(8,128)(2,1)S(1)}, u32[]{:S(2)}, u32[]{:S(2)}) collective-permute-start(bf16[4,4,128,128]{3,2,1,0:T(8,128)(2,1)S(1)} %pad_maximum_fusion.1), channel_id=1, source_target_pairs={{0,8},{1,9},{2,10},{3,11},{4,12},{5,13},{6,14},{7,15},{8,0},{9,1},... | collective-permute-start | bytes 1572872 | tf_op jit(solution)/shard_map/ppermute | solution.py:46
  38.5 0.0 collective-permute-done.2.refs_2_
  38.6 0.0 collective-permute-start.10
  38.6 0.0 collective-permute-done.4.refs_4_
  38.6 0.0 collective-permute-done.3.refs_3_
  38.6 0.0 collective-permute-done.5.refs_5_
  38.6 9.0 %shard_map.76 = (bf16[10,128,128]{2,1,0:T(8,128)(2,1)S(1)}, bf16[10,128,128]{2,1,0:T(8,128)(2,1)S(1)}, f32[10,2,256]{2,1,0:T(2,128)S(1)}) custom-call(f32[240]{0:T(256)S(1)} %select_n.84.table, bf16[10,2,128,128]{3,2,1,0:T(8,128)(2,1)S(1)} %get-tuple-element.37.qd_k, bf16[10,2,128,128]{3,2,1,0:T(8,128)(2,1)S(1)} %collective-permute-done.1.qd_o, ...), custom_call_target="tpu_custom_call" | custom-call | flops 12079595520 | bytes 6553600 | tf_op jit(solution)/shard_map/pallas_call | solution.py:215
  47.6 3.1 %collective-permute-start.6 = (f32[10,2,256]{2,1,0:T(2,128)S(1)}, f32[10,2,256]{2,1,0:T(2,128)S(1)}, u32[]{:S(2)}, u32[]{:S(2)}) collective-permute-start(f32[10,2,256]{2,1,0:T(2,128)S(1)} %get-tuple-element.21.refs_0_), channel_id=1, source_target_pairs={{0,8},{1,9},{2,10},{3,11},{4,12},{5,13},{6,14},{7,15},{8,0},{9,1},... | collective-permute-start | bytes 61448 | tf_op jit(solution)/shard_map/ppermute | solution.py:46
  50.7 0.0 collective-permute-start.7
  50.8 1.7 %collective-permute-done.6.refs_1_ = f32[10,2,256]{2,1,0:T(2,128)S(1)} collective-permute-done((f32[10,2,256]{2,1,0:T(2,128)S(1)}, f32[10,2,256]{2,1,0:T(2,128)S(1)}, u32[]{:S(2)}, u32[]{:S(2)}) %collective-permute-start.6) | collective-permute-done | bytes 20512 | tf_op jit(solution)/shard_map/ppermute | solution.py:46
  52.4 0.0 collective-permute-done.7.refs_2_
  52.4 1.5 %collective-permute-start.8 = (bf16[10,128,128]{2,1,0:T(8,128)(2,1)S(1)}, bf16[10,128,128]{2,1,0:T(8,128)(2,1)S(1)}, u32[]{:S(2)}, u32[]{:S(2)}) collective-permute-start(bf16[10,128,128]{2,1,0:T(8,128)(2,1)S(1)} %get-tuple-element.22), channel_id=1, source_target_pairs={{0,4},{4,0},{8,12},{12,8},{16,20},{20,16},{24,28},{28,24},{1,5},{5... | collective-permute-start | bytes 983048 | tf_op jit(solution)/shard_map/ppermute | solution.py:24
  53.9 0.0 collective-permute-done.9.side_a
  53.9 2.1 %collective-permute-start.11 = (bf16[4,4,128,128]{3,2,1,0:T(8,128)(2,1)S(1)}, bf16[4,4,128,128]{3,2,1,0:T(8,128)(2,1)S(1)}, u32[]{:S(2)}, u32[]{:S(2)}) collective-permute-start(bf16[4,4,128,128]{3,2,1,0:T(8,128)(2,1)S(1)} %pad_maximum_fusion.2), channel_id=1, source_target_pairs={{0,8},{1,9},{2,10},{3,11},{4,12},{5,13},{6,14},{7,15},{8,0},{9,1},... | collective-permute-start | bytes 1572872 | tf_op jit(solution)/shard_map/ppermute | solution.py:46
  56.0 0.0 collective-permute-start.12
  56.0 0.0 collective-permute-done.10.side_b
  56.0 3.2 %shard_map.77 = (bf16[4,2,128,128]{3,2,1,0:T(8,128)(2,1)S(1)}, bf16[4,2,128,128]{3,2,1,0:T(8,128)(2,1)S(1)}) custom-call(f32[240]{0:T(256)S(1)} %select_n.84.table, bf16[10,2,128,128]{3,2,1,0:T(8,128)(2,1)S(1)} %constant_dynamic-slice_fusion.refs_0_.kv_k, bf16[10,2,128,128]{3,2,1,0:T(8,128)(2,1)S(1)} %collective-permute-done.refs_1_.kv_o, ...), custom_call_target="tpu_custom_call" | custom-call | flops 6442450944 | bytes 2621440 | tf_op jit(solution)/shard_map/pallas_call | solution.py:251
  59.3 0.6 collective-permute-start.15
  59.9 1.8 %collective-permute-done.8 = bf16[10,128,128]{2,1,0:T(8,128)(2,1)S(1)} collective-permute-done((bf16[10,128,128]{2,1,0:T(8,128)(2,1)S(1)}, bf16[10,128,128]{2,1,0:T(8,128)(2,1)S(1)}, u32[]{:S(2)}, u32[]{:S(2)}) %collective-permute-start.8) | collective-permute-done | bytes 327712 | tf_op jit(solution)/shard_map/ppermute | solution.py:24
  61.7 0.9 %maximum_bitcast_fusion = bf16[128,20,128]{2,0,1:T(8,128)(2,1)} fusion(bf16[10,128,128]{2,1,0:T(8,128)(2,1)S(1)} %get-tuple-element.43, bf16[10,128,128]{2,1,0:T(8,128)(2,1)S(1)} %get-tuple-element.42), kind=kLoop, calls=%fused_computation.10 | loop fusion | flops 327680 | bytes 1310720 | tf_op jit(solution)/shard_map/transpose | solution.py:279
  62.6 5.5 %collective-permute-done.15 = bf16[4,2,128,128]{3,2,1,0:T(8,128)(2,1)S(1)} collective-permute-done((bf16[4,2,128,128]{3,2,1,0:T(8,128)(2,1)S(1)}, bf16[4,2,128,128]{3,2,1,0:T(8,128)(2,1)S(1)}, u32[]{:S(2)}, u32[]{:S(2)}) %collective-permute-start.15) | collective-permute-done | bytes 262176 | tf_op jit(solution)/shard_map/ppermute | solution.py:24
  68.1 0.0 collective-permute-done.11.side_a
  68.1 0.1 collective-permute-start.13
  68.2 0.1 collective-permute-start.14
  68.3 0.0 collective-permute-done.12.side_b
  68.3 3.2 %shard_map.78 = (bf16[4,2,128,128]{3,2,1,0:T(8,128)(2,1)S(1)}, bf16[4,2,128,128]{3,2,1,0:T(8,128)(2,1)S(1)}) custom-call(f32[240]{0:T(256)S(1)} %select_n.84.table, bf16[10,2,128,128]{3,2,1,0:T(8,128)(2,1)S(1)} %constant_dynamic-slice_fusion.refs_0_.kv_k, bf16[10,2,128,128]{3,2,1,0:T(8,128)(2,1)S(1)} %collective-permute-done.refs_1_.kv_o, ...), custom_call_target="tpu_custom_call" | custom-call | flops 6442450944 | bytes 2621440 | tf_op jit(solution)/shard_map/pallas_call | solution.py:251
  71.5 1.1 %collective-permute-start.16 = (bf16[4,2,128,128]{3,2,1,0:T(8,128)(2,1)S(1)}, bf16[4,2,128,128]{3,2,1,0:T(8,128)(2,1)S(1)}, u32[]{:S(2)}, u32[]{:S(2)}) collective-permute-start(bf16[4,2,128,128]{3,2,1,0:T(8,128)(2,1)S(1)} %get-tuple-element.29), channel_id=1, source_target_pairs={{0,4},{4,0},{8,12},{12,8},{16,20},{20,16},{24,28},{28,24},{1,5},{5... | collective-permute-start | bytes 786440 | tf_op jit(solution)/shard_map/ppermute | solution.py:24
  72.7 3.4 %collective-permute-done.13.side_a = bf16[2,4,128,128]{3,2,1,0:T(8,128)(2,1)S(1)} collective-permute-done((bf16[2,4,128,128]{3,2,1,0:T(8,128)(2,1)S(1)}, bf16[2,4,128,128]{3,2,1,0:T(8,128)(2,1)S(1)}, u32[]{:S(2)}, u32[]{:S(2)}) %collective-permute-start.13) | collective-permute-done | bytes 262176 | tf_op jit(solution)/shard_map/ppermute | solution.py:46
  76.1 0.0 collective-permute-done.14.side_b
  76.1 1.9 %shard_map.79 = (bf16[2,2,128,128]{3,2,1,0:T(8,128)(2,1)S(1)}, bf16[2,2,128,128]{3,2,1,0:T(8,128)(2,1)S(1)}) custom-call(f32[240]{0:T(256)S(1)} %select_n.84.table, bf16[10,2,128,128]{3,2,1,0:T(8,128)(2,1)S(1)} %constant_dynamic-slice_fusion.refs_0_.kv_k, bf16[10,2,128,128]{3,2,1,0:T(8,128)(2,1)S(1)} %collective-permute-done.refs_1_.kv_o, ...), custom_call_target="tpu_custom_call" | custom-call | flops 3221225472 | bytes 1310720 | tf_op jit(solution)/shard_map/pallas_call | solution.py:251
  78.0 0.9 %collective-permute-start.17 = (bf16[2,2,128,128]{3,2,1,0:T(8,128)(2,1)S(1)}, bf16[2,2,128,128]{3,2,1,0:T(8,128)(2,1)S(1)}, u32[]{:S(2)}, u32[]{:S(2)}) collective-permute-start(bf16[2,2,128,128]{3,2,1,0:T(8,128)(2,1)S(1)} %get-tuple-element.30), channel_id=1, source_target_pairs={{0,4},{4,0},{8,12},{12,8},{16,20},{20,16},{24,28},{28,24},{1,5},{5... | collective-permute-start | bytes 393224 | tf_op jit(solution)/shard_map/ppermute | solution.py:24
  78.9 1.8 %collective-permute-done.16 = bf16[4,2,128,128]{3,2,1,0:T(8,128)(2,1)S(1)} collective-permute-done((bf16[4,2,128,128]{3,2,1,0:T(8,128)(2,1)S(1)}, bf16[4,2,128,128]{3,2,1,0:T(8,128)(2,1)S(1)}, u32[]{:S(2)}, u32[]{:S(2)}) %collective-permute-start.16) | collective-permute-done | bytes 262176 | tf_op jit(solution)/shard_map/ppermute | solution.py:24
  80.7 2.3 %collective-permute-done.17 = bf16[2,2,128,128]{3,2,1,0:T(8,128)(2,1)S(1)} collective-permute-done((bf16[2,2,128,128]{3,2,1,0:T(8,128)(2,1)S(1)}, bf16[2,2,128,128]{3,2,1,0:T(8,128)(2,1)S(1)}, u32[]{:S(2)}, u32[]{:S(2)}) %collective-permute-start.17) | collective-permute-done | bytes 131104 | tf_op jit(solution)/shard_map/ppermute | solution.py:24
  83.1 0.1 fusion.4
  83.2 1.2 %maximum_bitcast_fusion.1 = (bf16[128,20,128]{2,0,1:T(8,128)(2,1)}, bf16[128,20,128]{2,0,1:T(8,128)(2,1)}) fusion(bf16[10,128,128]{2,1,0:T(8,128)(2,1)S(1)} %get-tuple-element.34, bf16[10,128,128]{2,1,0:T(8,128)(2,1)S(1)} %get-tuple-element.35, bf16[10,128,128]{2,1,0:T(8,128)(2,1)S(1)} %fusion.3, bf16[10,128,128]{2,1,0:T(8,128)(2,1)S(1)} %get-tuple-element.33), kind=kLoop, calls=%fused_computation.11 | loop fusion | flops 655360 | bytes 2621440 | tf_op jit(solution)/shard_map/transpose | solution.py:279
  (27 shorter events, 0.6 us)
Async XLA Ops:
  0.6 7.6 %copy-start = (s32[20,8,5]{0,1,2:T(8,128)S(1)}, s32[20,8,5]{0,1,2:T(8,128)}, u32[]{:S(2)}) copy-start(s32[20,8,5]{0,1,2:T(8,128)} %param.9) | copy-start | bytes 9604
  0.6 5.1 %copy-start.2 = (bf16[128,20,128]{2,0,1:T(8,128)(2,1)S(1)}, bf16[128,20,128]{2,0,1:T(8,128)(2,1)}, u32[]{:S(2)}) copy-start(bf16[128,20,128]{2,0,1:T(8,128)(2,1)} %param.6) | copy-start | bytes 1966084
  0.7 5.1 %copy-start.1 = (bf16[128,20,128]{2,0,1:T(8,128)(2,1)S(1)}, bf16[128,20,128]{2,0,1:T(8,128)(2,1)}, u32[]{:S(2)}) copy-start(bf16[128,20,128]{2,0,1:T(8,128)(2,1)} %param.7) | copy-start | bytes 1966084
  2.8 17.9 %collective-permute-start = (bf16[10,2,128,128]{3,2,1,0:T(8,128)(2,1)}, bf16[10,2,128,128]{3,2,1,0:T(8,128)(2,1)S(1)}, u32[]{:S(2)}, u32[]{:S(2)}) collective-permute-start(bf16[10,2,128,128]{3,2,1,0:T(8,128)(2,1)} %fusion), channel_id=1, source_target_pairs={{0,4},{4,0},{8,12},{12,8},{16,20},{20,16},{24,28},{28,24},{1,5},{5... | collective-permute-start | bytes 1966088 | tf_op jit(solution)/shard_map/ppermute | solution.py:24
  5.9 2.7 %copy-start.3 = (bf16[128,20,128]{2,0,1:T(8,128)(2,1)S(1)}, bf16[128,20,128]{2,0,1:T(8,128)(2,1)}, u32[]{:S(2)}) copy-start(bf16[128,20,128]{2,0,1:T(8,128)(2,1)} %param.5) | copy-start | bytes 1966084
  5.9 32.6 %collective-permute-start.2 = (bf16[10,2,128,128]{3,2,1,0:T(8,128)(2,1)S(1)}, bf16[10,2,128,128]{3,2,1,0:T(8,128)(2,1)S(1)}, u32[]{:S(2)}, u32[]{:S(2)}) collective-permute-start(bf16[10,2,128,128]{3,2,1,0:T(8,128)(2,1)S(1)} %constant_dynamic-slice_fusion.refs_0_.kv_k), channel_id=1, source_target_pairs={{0,8},{1,9},{2,10},{3,11},{4,12},{5,13},{6,14},{7,15},{8,0},{9,1},... | collective-permute-start | bytes 1966088 | tf_op jit(solution)/shard_map/ppermute | solution.py:46
  7.6 31.0 %collective-permute-start.4 = (bf16[10,2,128,128]{3,2,1,0:T(8,128)(2,1)S(1)}, bf16[10,2,128,128]{3,2,1,0:T(8,128)(2,1)}, u32[]{:S(2)}, u32[]{:S(2)}) collective-permute-start(bf16[10,2,128,128]{3,2,1,0:T(8,128)(2,1)S(1)} %constant_dynamic-slice_fusion.refs_0_.kv_k), channel_id=1, source_target_pairs={{0,1},{1,0},{2,3},{3,2},{4,5},{5,4},{6,7},{7,6},{8,16},{9,17},{10,... | collective-permute-start | bytes 1966088 | tf_op jit(solution)/shard_map/ppermute | solution.py:46
  20.7 16.1 %collective-permute-start.1 = (bf16[10,2,128,128]{3,2,1,0:T(8,128)(2,1)}, bf16[10,2,128,128]{3,2,1,0:T(8,128)(2,1)S(1)}, u32[]{:S(2)}, u32[]{:S(2)}) collective-permute-start(bf16[10,2,128,128]{3,2,1,0:T(8,128)(2,1)} %get-tuple-element.17), channel_id=1, source_target_pairs={{0,4},{4,0},{8,12},{12,8},{16,20},{20,16},{24,28},{28,24},{1,5},{5... | collective-permute-start | bytes 1966088 | tf_op jit(solution)/shard_map/ppermute | solution.py:24
  22.4 16.1 %collective-permute-start.3 = (bf16[10,2,128,128]{3,2,1,0:T(8,128)(2,1)S(1)}, bf16[10,2,128,128]{3,2,1,0:T(8,128)(2,1)}, u32[]{:S(2)}, u32[]{:S(2)}) collective-permute-start(bf16[10,2,128,128]{3,2,1,0:T(8,128)(2,1)S(1)} %collective-permute-done.refs_1_.kv_o), channel_id=1, source_target_pairs={{0,8},{1,9},{2,10},{3,11},{4,12},{5,13},{6,14},{7,15},{8,0},{9,1},... | collective-permute-start | bytes 1966088 | tf_op jit(solution)/shard_map/ppermute | solution.py:46
  24.1 14.5 %collective-permute-start.5 = (bf16[10,2,128,128]{3,2,1,0:T(8,128)(2,1)S(1)}, bf16[10,2,128,128]{3,2,1,0:T(8,128)(2,1)}, u32[]{:S(2)}, u32[]{:S(2)}) collective-permute-start(bf16[10,2,128,128]{3,2,1,0:T(8,128)(2,1)S(1)} %collective-permute-done.refs_1_.kv_o), channel_id=1, source_target_pairs={{0,1},{1,0},{2,3},{3,2},{4,5},{5,4},{6,7},{7,6},{8,16},{9,17},{10,... | collective-permute-start | bytes 1966088 | tf_op jit(solution)/shard_map/ppermute | solution.py:46
  36.9 17.0 %collective-permute-start.9 = (bf16[4,4,128,128]{3,2,1,0:T(8,128)(2,1)S(1)}, bf16[4,4,128,128]{3,2,1,0:T(8,128)(2,1)S(1)}, u32[]{:S(2)}, u32[]{:S(2)}) collective-permute-start(bf16[4,4,128,128]{3,2,1,0:T(8,128)(2,1)S(1)} %pad_maximum_fusion.1), channel_id=1, source_target_pairs={{0,8},{1,9},{2,10},{3,11},{4,12},{5,13},{6,14},{7,15},{8,0},{9,1},... | collective-permute-start | bytes 1572872 | tf_op jit(solution)/shard_map/ppermute | solution.py:46
  38.6 17.5 %collective-permute-start.10 = (bf16[4,4,128,128]{3,2,1,0:T(8,128)(2,1)S(1)}, bf16[4,4,128,128]{3,2,1,0:T(8,128)(2,1)S(1)}, u32[]{:S(2)}, u32[]{:S(2)}) collective-permute-start(bf16[4,4,128,128]{3,2,1,0:T(8,128)(2,1)S(1)} %pad_maximum_fusion.1), channel_id=1, source_target_pairs={{0,1},{1,0},{2,3},{3,2},{4,5},{5,4},{6,7},{7,6},{8,16},{9,17},{10,... | collective-permute-start | bytes 1572872 | tf_op jit(solution)/shard_map/ppermute | solution.py:46
  47.6 4.9 %collective-permute-start.6 = (f32[10,2,256]{2,1,0:T(2,128)S(1)}, f32[10,2,256]{2,1,0:T(2,128)S(1)}, u32[]{:S(2)}, u32[]{:S(2)}) collective-permute-start(f32[10,2,256]{2,1,0:T(2,128)S(1)} %get-tuple-element.21.refs_0_), channel_id=1, source_target_pairs={{0,8},{1,9},{2,10},{3,11},{4,12},{5,13},{6,14},{7,15},{8,0},{9,1},... | collective-permute-start | bytes 61448 | tf_op jit(solution)/shard_map/ppermute | solution.py:46
  50.7 1.8 %collective-permute-start.7 = (f32[10,2,256]{2,1,0:T(2,128)S(1)}, f32[10,2,256]{2,1,0:T(2,128)S(1)}, u32[]{:S(2)}, u32[]{:S(2)}) collective-permute-start(f32[10,2,256]{2,1,0:T(2,128)S(1)} %get-tuple-element.21.refs_0_), channel_id=1, source_target_pairs={{0,1},{1,0},{2,3},{3,2},{4,5},{5,4},{6,7},{7,6},{8,16},{9,17},{10,... | collective-permute-start | bytes 61448 | tf_op jit(solution)/shard_map/ppermute | solution.py:46
  52.4 9.2 %collective-permute-start.8 = (bf16[10,128,128]{2,1,0:T(8,128)(2,1)S(1)}, bf16[10,128,128]{2,1,0:T(8,128)(2,1)S(1)}, u32[]{:S(2)}, u32[]{:S(2)}) collective-permute-start(bf16[10,128,128]{2,1,0:T(8,128)(2,1)S(1)} %get-tuple-element.22), channel_id=1, source_target_pairs={{0,4},{4,0},{8,12},{12,8},{16,20},{20,16},{24,28},{28,24},{1,5},{5... | collective-permute-start | bytes 983048 | tf_op jit(solution)/shard_map/ppermute | solution.py:24
  53.9 14.1 %collective-permute-start.11 = (bf16[4,4,128,128]{3,2,1,0:T(8,128)(2,1)S(1)}, bf16[4,4,128,128]{3,2,1,0:T(8,128)(2,1)S(1)}, u32[]{:S(2)}, u32[]{:S(2)}) collective-permute-start(bf16[4,4,128,128]{3,2,1,0:T(8,128)(2,1)S(1)} %pad_maximum_fusion.2), channel_id=1, source_target_pairs={{0,8},{1,9},{2,10},{3,11},{4,12},{5,13},{6,14},{7,15},{8,0},{9,1},... | collective-permute-start | bytes 1572872 | tf_op jit(solution)/shard_map/ppermute | solution.py:46
  56.0 12.2 %collective-permute-start.12 = (bf16[4,4,128,128]{3,2,1,0:T(8,128)(2,1)S(1)}, bf16[4,4,128,128]{3,2,1,0:T(8,128)(2,1)S(1)}, u32[]{:S(2)}, u32[]{:S(2)}) collective-permute-start(bf16[4,4,128,128]{3,2,1,0:T(8,128)(2,1)S(1)} %pad_maximum_fusion.2), channel_id=1, source_target_pairs={{0,1},{1,0},{2,3},{3,2},{4,5},{5,4},{6,7},{7,6},{8,16},{9,17},{10,... | collective-permute-start | bytes 1572872 | tf_op jit(solution)/shard_map/ppermute | solution.py:46
  59.3 8.8 %collective-permute-start.15 = (bf16[4,2,128,128]{3,2,1,0:T(8,128)(2,1)S(1)}, bf16[4,2,128,128]{3,2,1,0:T(8,128)(2,1)S(1)}, u32[]{:S(2)}, u32[]{:S(2)}) collective-permute-start(bf16[4,2,128,128]{3,2,1,0:T(8,128)(2,1)S(1)} %get-tuple-element.28), channel_id=1, source_target_pairs={{0,4},{4,0},{8,12},{12,8},{16,20},{20,16},{24,28},{28,24},{1,5},{5... | collective-permute-start | bytes 786440 | tf_op jit(solution)/shard_map/ppermute | solution.py:24
  68.1 8.0 %collective-permute-start.13 = (bf16[2,4,128,128]{3,2,1,0:T(8,128)(2,1)S(1)}, bf16[2,4,128,128]{3,2,1,0:T(8,128)(2,1)S(1)}, u32[]{:S(2)}, u32[]{:S(2)}) collective-permute-start(bf16[2,4,128,128]{3,2,1,0:T(8,128)(2,1)S(1)} %pad_maximum_fusion.3), channel_id=1, source_target_pairs={{0,8},{1,9},{2,10},{3,11},{4,12},{5,13},{6,14},{7,15},{8,0},{9,1},... | collective-permute-start | bytes 786440 | tf_op jit(solution)/shard_map/ppermute | solution.py:46
  68.2 7.9 %collective-permute-start.14 = (bf16[2,4,128,128]{3,2,1,0:T(8,128)(2,1)S(1)}, bf16[2,4,128,128]{3,2,1,0:T(8,128)(2,1)S(1)}, u32[]{:S(2)}, u32[]{:S(2)}) collective-permute-start(bf16[2,4,128,128]{3,2,1,0:T(8,128)(2,1)S(1)} %pad_maximum_fusion.3), channel_id=1, source_target_pairs={{0,1},{1,0},{2,3},{3,2},{4,5},{5,4},{6,7},{7,6},{8,16},{9,17},{10,... | collective-permute-start | bytes 786440 | tf_op jit(solution)/shard_map/ppermute | solution.py:46
  71.5 9.2 %collective-permute-start.16 = (bf16[4,2,128,128]{3,2,1,0:T(8,128)(2,1)S(1)}, bf16[4,2,128,128]{3,2,1,0:T(8,128)(2,1)S(1)}, u32[]{:S(2)}, u32[]{:S(2)}) collective-permute-start(bf16[4,2,128,128]{3,2,1,0:T(8,128)(2,1)S(1)} %get-tuple-element.29), channel_id=1, source_target_pairs={{0,4},{4,0},{8,12},{12,8},{16,20},{20,16},{24,28},{28,24},{1,5},{5... | collective-permute-start | bytes 786440 | tf_op jit(solution)/shard_map/ppermute | solution.py:24
  78.0 5.1 %collective-permute-start.17 = (bf16[2,2,128,128]{3,2,1,0:T(8,128)(2,1)S(1)}, bf16[2,2,128,128]{3,2,1,0:T(8,128)(2,1)S(1)}, u32[]{:S(2)}, u32[]{:S(2)}) collective-permute-start(bf16[2,2,128,128]{3,2,1,0:T(8,128)(2,1)S(1)} %get-tuple-element.30), channel_id=1, source_target_pairs={{0,4},{4,0},{8,12},{12,8},{16,20},{20,16},{24,28},{28,24},{1,5},{5... | collective-permute-start | bytes 393224 | tf_op jit(solution)/shard_map/ppermute | solution.py:24

commit v3 on v2

--- a/solution.py
+++ b/solution.py
@@ -237,15 +237,20 @@
         kv_sides[1],
         kv_sides_other[1],
     )
+    stats = after(stats, qd_sides[0][0])
     stat_sides = [beside(stats, 0), beside(stats, 1)]
-    dq_back = across(after(dq_send, *stat_sides), "seq")
+    dq_back = across(dq_send, "seq")
     dkv_keep, dkv_back = [], []
     for index, (low, high) in enumerate(zip(cuts, cuts[1:])):
         arrived = qd_sides[index]
         if index + 1 < len(qd_pieces):
-            piece = after(qd_pieces[index + 1], qd_sides[-1][0])
+            piece = after(qd_pieces[index + 1], qd_sides[-1][0] if index == 0 else dkv_back[0])
             qd_sides.append([beside(piece, 0), beside(piece, 1)])
-        count, shift = high - low, low // heads
+        count = high - low
+        heads = 2 if low % 2 == 0 and count % 2 == 0 else 1
+        shift = low // heads
+        pair_spec = pl.BlockSpec((heads, 2, block, width), lambda i: (i, 0, 0, 0))
+        quad_spec = pl.BlockSpec((heads, 4, block, width), lambda i: (i, 0, 0, 0))
         part_spec = pl.BlockSpec((heads, 2, block, width), lambda i, shift=shift: (i + shift, 0, 0, 0))
         stat_part = pl.BlockSpec((heads, 2, 2 * block), lambda i, shift=shift: (i + shift, 0, 0))
         keep, send = pl.pallas_call(

time: 84.6 us -> 82.6 us (0.976)
  waiting for transfers between devices: 39.1 us -> 36.7 us
    ppermute x12, waiting for transfers between devices: 5.08 us -> 3.66 us  [beside(): return lax.ppermute(value, ('seq', 'dp'), pairs)]
    ppermute x6, waiting for transfers between devices: 34 us -> 33 us  [across(): return lax.ppermute(value, axis, [(i, i ^ 1) for i in range(size)])]
    ppermute x6, starting transfers between devices: 8.83 us -> 9.75 us  [across(): return lax.ppermute(value, axis, [(i, i ^ 1) for i in range(size)])]
where the time goes in v3:
time: 82.6 us; the launch traced here: 82.4 us
  waiting for transfers between devices  36.7 us (44%)
  starting transfers between devices  19.6 us (24%)
  Pallas kernels  17.3 us (21%)
  other arithmetic  7 us (8%)
  between operations  0.95 us (1%)
  local copies, waits for them, and re-layouts  0.9 us (1%)
    ppermute x6, waiting for transfers between devices, across(): return lax.ppermute(value, axis, [(i, i ^ 1) for i in range(size)])  33 us
    ppermute x12, starting transfers between devices, beside(): return lax.ppermute(value, ('seq', 'dp'), pairs)  9.85 us
    ppermute x6, starting transfers between devices, across(): return lax.ppermute(value, axis, [(i, i ^ 1) for i in range(size)])  9.75 us
    pallas_call x1, Pallas kernels, per_device(): pl.pallas_call(partial(query_kernel, factor, scale, heads), grid=(local /...  8.97 us
    pallas_call x3, Pallas kernels, per_device(): pl.pallas_call(partial(key_kernel, factor, scale, heads, low), grid=(coun...  8.33 us
    another operation x3, other arithmetic, by_head(): jnp.stack([jnp.transpose(left, (1, 0, 2)), jnp.transpose(right, (1, 0, 2)...  4.24 us
    ppermute x12, waiting for transfers between devices, beside(): return lax.ppermute(value, ('seq', 'dp'), pairs)  3.66 us
    transpose x2, other arithmetic, home(): return jnp.transpose(jnp.concatenate([low, high], axis=0), (1, 0, 2))  2.07 us
  transfers between devices with their start and end apart: 18, of which 8 were waited for; matrix products, arithmetic and copies ran while one was open for 5% of the time, Pallas kernels for 21%

profile of v3, /device:TPU:0, one launch (start us, length us, event | category | flops | bytes accessed | tf_op | source)
XLA Modules:
  0.0 82.4 jit_solution(3073888886547504510)
XLA Ops:
  0.6 0.0 copy-start
  0.6 0.0 copy-start.2
  0.7 0.0 copy-start.1
  0.7 2.1 %fusion = bf16[10,2,128,128]{3,2,1,0:T(8,128)(2,1)} fusion(s32[]{:T(128)S(6)} %select_n.85, bf16[20,1,128,128]{3,2,1,0:T(8,128)(2,1)} %bitcast.57, bf16[20,1,128,128]{3,2,1,0:T(8,128)(2,1)} %bitcast.55), kind=kLoop, calls=%fused_computation.7 | loop fusion | flops 327680 | bytes 1966084 | tf_op jit(solution)/shard_map/stack | solution.py:186
  2.8 3.0 %collective-permute-start = (bf16[10,2,128,128]{3,2,1,0:T(8,128)(2,1)}, bf16[10,2,128,128]{3,2,1,0:T(8,128)(2,1)S(1)}, u32[]{:S(2)}, u32[]{:S(2)}) collective-permute-start(bf16[10,2,128,128]{3,2,1,0:T(8,128)(2,1)} %fusion), channel_id=1, source_target_pairs={{0,4},{4,0},{8,12},{12,8},{16,20},{20,16},{24,28},{28,24},{1,5},{5... | collective-permute-start | bytes 1966088 | tf_op jit(solution)/shard_map/ppermute | solution.py:24
  5.7 0.0 copy-done.2
  5.7 0.0 copy-done.1
  5.7 0.1 pad_maximum_fusion
  5.9 0.0 copy-start.3
  5.9 1.6 %collective-permute-start.2 = (bf16[10,2,128,128]{3,2,1,0:T(8,128)(2,1)S(1)}, bf16[10,2,128,128]{3,2,1,0:T(8,128)(2,1)S(1)}, u32[]{:S(2)}, u32[]{:S(2)}) collective-permute-start(bf16[10,2,128,128]{3,2,1,0:T(8,128)(2,1)S(1)} %constant_dynamic-slice_fusion.refs_0_.kv_k), channel_id=1, source_target_pairs={{0,8},{1,9},{2,10},{3,11},{4,12},{5,13},{6,14},{7,15},{8,0},{9,1},... | collective-permute-start | bytes 1966088 | tf_op jit(solution)/shard_map/ppermute | solution.py:46
  7.6 0.0 collective-permute-start.4
  7.6 0.1 broadcast_add_fusion.2
  7.7 0.1 add_multiply_fusion
  7.7 0.1 broadcast_add_fusion
  7.8 0.1 stack_broadcast_in_dim.11
  7.9 0.1 stack_broadcast_in_dim.10
  8.0 0.1 stack.56
  8.1 0.1 eq.66
  8.2 0.0 copy-done
  8.2 0.1 constant_dynamic-slice_fusion.1
  8.3 0.1 copy.24
  8.4 0.1 multiply_reduce_fusion
  8.6 2.0 %fusion.1 = (bf16[10,2,128,128]{3,2,1,0:T(8,128)(2,1)}, bf16[10,2,128,128]{3,2,1,0:T(8,128)(2,1)S(1)}) fusion(s32[]{:T(128)S(6)} %select_n.85, bf16[20,1,128,128]{3,2,1,0:T(8,128)(2,1)S(1)} %bitcast.59, bf16[20,1,128,128]{3,2,1,0:T(8,128)(2,1)} %bitcast.60, s32[]{:T(128)S(6)} %select_n.79), kind=kLoop, calls=%fused_computation.8 | loop fusion | flops 655360 | bytes 2621448 | tf_op jit(solution)/shard_map/stack | solution.py:186
  10.6 10.1 %collective-permute-done.refs_1_.kv_o = bf16[10,2,128,128]{3,2,1,0:T(8,128)(2,1)S(1)} collective-permute-done((bf16[10,2,128,128]{3,2,1,0:T(8,128)(2,1)}, bf16[10,2,128,128]{3,2,1,0:T(8,128)(2,1)S(1)}, u32[]{:S(2)}, u32[]{:S(2)}) %collective-permute-start) | collective-permute-done | bytes 655392 | tf_op jit(solution)/shard_map/ppermute | solution.py:24
  20.7 1.7 %collective-permute-start.1 = (bf16[10,2,128,128]{3,2,1,0:T(8,128)(2,1)}, bf16[10,2,128,128]{3,2,1,0:T(8,128)(2,1)S(1)}, u32[]{:S(2)}, u32[]{:S(2)}) collective-permute-start(bf16[10,2,128,128]{3,2,1,0:T(8,128)(2,1)} %get-tuple-element.17), channel_id=1, source_target_pairs={{0,4},{4,0},{8,12},{12,8},{16,20},{20,16},{24,28},{28,24},{1,5},{5... | collective-permute-start | bytes 1966088 | tf_op jit(solution)/shard_map/ppermute | solution.py:24
  22.4 1.6 %collective-permute-start.3 = (bf16[10,2,128,128]{3,2,1,0:T(8,128)(2,1)S(1)}, bf16[10,2,128,128]{3,2,1,0:T(8,128)(2,1)}, u32[]{:S(2)}, u32[]{:S(2)}) collective-permute-start(bf16[10,2,128,128]{3,2,1,0:T(8,128)(2,1)S(1)} %collective-permute-done.refs_1_.kv_o), channel_id=1, source_target_pairs={{0,8},{1,9},{2,10},{3,11},{4,12},{5,13},{6,14},{7,15},{8,0},{9,1},... | collective-permute-start | bytes 1966088 | tf_op jit(solution)/shard_map/ppermute | solution.py:46
  24.1 0.0 collective-permute-start.5
  24.1 0.1 select_n.84.table
  24.2 12.6 %collective-permute-done.1.qd_o = bf16[10,2,128,128]{3,2,1,0:T(8,128)(2,1)S(1)} collective-permute-done((bf16[10,2,128,128]{3,2,1,0:T(8,128)(2,1)}, bf16[10,2,128,128]{3,2,1,0:T(8,128)(2,1)S(1)}, u32[]{:S(2)}, u32[]{:S(2)}) %collective-permute-start.1) | collective-permute-done | bytes 655392 | tf_op jit(solution)/shard_map/ppermute | solution.py:24
  36.9 1.7 %collective-permute-start.7 = (bf16[4,4,128,128]{3,2,1,0:T(8,128)(2,1)S(1)}, bf16[4,4,128,128]{3,2,1,0:T(8,128)(2,1)S(1)}, u32[]{:S(2)}, u32[]{:S(2)}) collective-permute-start(bf16[4,4,128,128]{3,2,1,0:T(8,128)(2,1)S(1)} %pad_maximum_fusion.1), channel_id=1, source_target_pairs={{0,8},{1,9},{2,10},{3,11},{4,12},{5,13},{6,14},{7,15},{8,0},{9,1},... | collective-permute-start | bytes 1572872 | tf_op jit(solution)/shard_map/ppermute | solution.py:46
  38.5 0.0 collective-permute-done.2.refs_2_
  38.6 0.0 collective-permute-start.8
  38.6 0.0 collective-permute-done.4.refs_4_
  38.6 0.0 collective-permute-done.3.refs_3_
  38.6 0.0 collective-permute-done.5.refs_5_
  38.6 9.0 %shard_map.76 = (bf16[10,128,128]{2,1,0:T(8,128)(2,1)S(1)}, bf16[10,128,128]{2,1,0:T(8,128)(2,1)S(1)}, f32[10,2,256]{2,1,0:T(2,128)S(1)}) custom-call(f32[240]{0:T(256)S(1)} %select_n.84.table, bf16[10,2,128,128]{3,2,1,0:T(8,128)(2,1)S(1)} %get-tuple-element.37.qd_k, bf16[10,2,128,128]{3,2,1,0:T(8,128)(2,1)S(1)} %collective-permute-done.1.qd_o, ...), custom_call_target="tpu_custom_call" | custom-call | flops 12079595520 | bytes 6553600 | tf_op jit(solution)/shard_map/pallas_call | solution.py:215
  47.6 1.6 %collective-permute-start.6 = (bf16[10,128,128]{2,1,0:T(8,128)(2,1)S(1)}, bf16[10,128,128]{2,1,0:T(8,128)(2,1)S(1)}, u32[]{:S(2)}, u32[]{:S(2)}) collective-permute-start(bf16[10,128,128]{2,1,0:T(8,128)(2,1)S(1)} %get-tuple-element.20), channel_id=1, source_target_pairs={{0,4},{4,0},{8,12},{12,8},{16,20},{20,16},{24,28},{28,24},{1,5},{5... | collective-permute-start | bytes 983048 | tf_op jit(solution)/shard_map/ppermute | solution.py:24
  49.2 0.0 collective-permute-done.7.side_a
  49.3 3.1 %collective-permute-start.9 = (f32[10,2,256]{2,1,0:T(2,128)S(1)}, f32[10,2,256]{2,1,0:T(2,128)S(1)}, u32[]{:S(2)}, u32[]{:S(2)}) collective-permute-start(f32[10,2,256]{2,1,0:T(2,128)S(1)} %get-tuple-element.22.refs_0_), channel_id=1, source_target_pairs={{0,8},{1,9},{2,10},{3,11},{4,12},{5,13},{6,14},{7,15},{8,0},{9,1},... | collective-permute-start | bytes 61448 | tf_op jit(solution)/shard_map/ppermute | solution.py:46
  52.3 0.0 collective-permute-start.10
  52.4 1.5 %collective-permute-start.11 = (bf16[4,4,128,128]{3,2,1,0:T(8,128)(2,1)S(1)}, bf16[4,4,128,128]{3,2,1,0:T(8,128)(2,1)S(1)}, u32[]{:S(2)}, u32[]{:S(2)}) collective-permute-start(bf16[4,4,128,128]{3,2,1,0:T(8,128)(2,1)S(1)} %pad_maximum_fusion.2), channel_id=1, source_target_pairs={{0,8},{1,9},{2,10},{3,11},{4,12},{5,13},{6,14},{7,15},{8,0},{9,1},... | collective-permute-start | bytes 1572872 | tf_op jit(solution)/shard_map/ppermute | solution.py:46
  53.9 0.0 collective-permute-done.8.side_b
  53.9 0.0 collective-permute-start.12
  53.9 0.2 collective-permute-done.9.refs_1_
  54.1 0.0 collective-permute-done.10.refs_2_
  54.1 3.2 %shard_map.77 = (bf16[4,2,128,128]{3,2,1,0:T(8,128)(2,1)S(1)}, bf16[4,2,128,128]{3,2,1,0:T(8,128)(2,1)S(1)}) custom-call(f32[240]{0:T(256)S(1)} %select_n.84.table, bf16[10,2,128,128]{3,2,1,0:T(8,128)(2,1)S(1)} %constant_dynamic-slice_fusion.refs_0_.kv_k, bf16[10,2,128,128]{3,2,1,0:T(8,128)(2,1)S(1)} %collective-permute-done.refs_1_.kv_o, ...), custom_call_target="tpu_custom_call" | custom-call | flops 6442450944 | bytes 2621440 | tf_op jit(solution)/shard_map/pallas_call | solution.py:256
  57.3 1.2 %collective-permute-start.13 = (bf16[4,2,128,128]{3,2,1,0:T(8,128)(2,1)S(1)}, bf16[4,2,128,128]{3,2,1,0:T(8,128)(2,1)S(1)}, u32[]{:S(2)}, u32[]{:S(2)}) collective-permute-start(bf16[4,2,128,128]{3,2,1,0:T(8,128)(2,1)S(1)} %get-tuple-element.26), channel_id=1, source_target_pairs={{0,4},{4,0},{8,12},{12,8},{16,20},{20,16},{24,28},{28,24},{1,5},{5... | collective-permute-start | bytes 786440 | tf_op jit(solution)/shard_map/ppermute | solution.py:24
  58.5 0.0 collective-permute-done.6
  58.6 0.9 %maximum_bitcast_fusion = bf16[128,20,128]{2,0,1:T(8,128)(2,1)} fusion(bf16[10,128,128]{2,1,0:T(8,128)(2,1)S(1)} %get-tuple-element.43, bf16[10,128,128]{2,1,0:T(8,128)(2,1)S(1)} %get-tuple-element.42), kind=kLoop, calls=%fused_computation.10 | loop fusion | flops 327680 | bytes 1310720 | tf_op jit(solution)/shard_map/transpose | solution.py:284
  59.5 6.4 %collective-permute-done.13 = bf16[4,2,128,128]{3,2,1,0:T(8,128)(2,1)S(1)} collective-permute-done((bf16[4,2,128,128]{3,2,1,0:T(8,128)(2,1)S(1)}, bf16[4,2,128,128]{3,2,1,0:T(8,128)(2,1)S(1)}, u32[]{:S(2)}, u32[]{:S(2)}) %collective-permute-start.13) | collective-permute-done | bytes 262176 | tf_op jit(solution)/shard_map/ppermute | solution.py:24
  65.9 0.3 collective-permute-start.14
  66.2 0.0 collective-permute-start.15
  66.2 0.5 collective-permute-done.11.side_a
  66.8 0.0 collective-permute-done.12.side_b
  66.8 3.2 %shard_map.78 = (bf16[4,2,128,128]{3,2,1,0:T(8,128)(2,1)S(1)}, bf16[4,2,128,128]{3,2,1,0:T(8,128)(2,1)S(1)}) custom-call(f32[240]{0:T(256)S(1)} %select_n.84.table, bf16[10,2,128,128]{3,2,1,0:T(8,128)(2,1)S(1)} %constant_dynamic-slice_fusion.refs_0_.kv_k, bf16[10,2,128,128]{3,2,1,0:T(8,128)(2,1)S(1)} %collective-permute-done.refs_1_.kv_o, ...), custom_call_target="tpu_custom_call" | custom-call | flops 6442450944 | bytes 2621440 | tf_op jit(solution)/shard_map/pallas_call | solution.py:256
  70.0 0.7 collective-permute-start.16
  70.7 2.9 %collective-permute-done.14.side_a = bf16[2,4,128,128]{3,2,1,0:T(8,128)(2,1)S(1)} collective-permute-done((bf16[2,4,128,128]{3,2,1,0:T(8,128)(2,1)S(1)}, bf16[2,4,128,128]{3,2,1,0:T(8,128)(2,1)S(1)}, u32[]{:S(2)}, u32[]{:S(2)}) %collective-permute-start.14) | collective-permute-done | bytes 262176 | tf_op jit(solution)/shard_map/ppermute | solution.py:46
  73.6 0.0 collective-permute-done.15.side_b
  73.6 1.9 %shard_map.79 = (bf16[2,2,128,128]{3,2,1,0:T(8,128)(2,1)S(1)}, bf16[2,2,128,128]{3,2,1,0:T(8,128)(2,1)S(1)}) custom-call(f32[240]{0:T(256)S(1)} %select_n.84.table, bf16[10,2,128,128]{3,2,1,0:T(8,128)(2,1)S(1)} %constant_dynamic-slice_fusion.refs_0_.kv_k, bf16[10,2,128,128]{3,2,1,0:T(8,128)(2,1)S(1)} %collective-permute-done.refs_1_.kv_o, ...), custom_call_target="tpu_custom_call" | custom-call | flops 3221225472 | bytes 1310720 | tf_op jit(solution)/shard_map/pallas_call | solution.py:256
  75.5 1.6 %collective-permute-start.17 = (bf16[2,2,128,128]{3,2,1,0:T(8,128)(2,1)S(1)}, bf16[2,2,128,128]{3,2,1,0:T(8,128)(2,1)S(1)}, u32[]{:S(2)}, u32[]{:S(2)}) collective-permute-start(bf16[2,2,128,128]{3,2,1,0:T(8,128)(2,1)S(1)} %get-tuple-element.30), channel_id=1, source_target_pairs={{0,4},{4,0},{8,12},{12,8},{16,20},{20,16},{24,28},{28,24},{1,5},{5... | collective-permute-start | bytes 393224 | tf_op jit(solution)/shard_map/ppermute | solution.py:24
  77.1 2.1 %collective-permute-done.16 = bf16[4,2,128,128]{3,2,1,0:T(8,128)(2,1)S(1)} collective-permute-done((bf16[4,2,128,128]{3,2,1,0:T(8,128)(2,1)S(1)}, bf16[4,2,128,128]{3,2,1,0:T(8,128)(2,1)S(1)}, u32[]{:S(2)}, u32[]{:S(2)}) %collective-permute-start.16) | collective-permute-done | bytes 262176 | tf_op jit(solution)/shard_map/ppermute | solution.py:24
  79.3 1.8 %collective-permute-done.17 = bf16[2,2,128,128]{3,2,1,0:T(8,128)(2,1)S(1)} collective-permute-done((bf16[2,2,128,128]{3,2,1,0:T(8,128)(2,1)S(1)}, bf16[2,2,128,128]{3,2,1,0:T(8,128)(2,1)S(1)}, u32[]{:S(2)}, u32[]{:S(2)}) %collective-permute-start.17) | collective-permute-done | bytes 131104 | tf_op jit(solution)/shard_map/ppermute | solution.py:24
  81.1 0.1 fusion.4
  81.3 1.2 %maximum_bitcast_fusion.1 = (bf16[128,20,128]{2,0,1:T(8,128)(2,1)}, bf16[128,20,128]{2,0,1:T(8,128)(2,1)}) fusion(bf16[10,128,128]{2,1,0:T(8,128)(2,1)S(1)} %get-tuple-element.34, bf16[10,128,128]{2,1,0:T(8,128)(2,1)S(1)} %get-tuple-element.35, bf16[10,128,128]{2,1,0:T(8,128)(2,1)S(1)} %fusion.3, bf16[10,128,128]{2,1,0:T(8,128)(2,1)S(1)} %get-tuple-element.33), kind=kLoop, calls=%fused_computation.11 | loop fusion | flops 655360 | bytes 2621440 | tf_op jit(solution)/shard_map/transpose | solution.py:284
  (27 shorter events, 0.6 us)
Async XLA Ops:
  0.6 7.6 %copy-start = (s32[20,8,5]{0,1,2:T(8,128)S(1)}, s32[20,8,5]{0,1,2:T(8,128)}, u32[]{:S(2)}) copy-start(s32[20,8,5]{0,1,2:T(8,128)} %param.9) | copy-start | bytes 9604
  0.6 5.1 %copy-start.2 = (bf16[128,20,128]{2,0,1:T(8,128)(2,1)S(1)}, bf16[128,20,128]{2,0,1:T(8,128)(2,1)}, u32[]{:S(2)}) copy-start(bf16[128,20,128]{2,0,1:T(8,128)(2,1)} %param.6) | copy-start | bytes 1966084
  0.7 5.1 %copy-start.1 = (bf16[128,20,128]{2,0,1:T(8,128)(2,1)S(1)}, bf16[128,20,128]{2,0,1:T(8,128)(2,1)}, u32[]{:S(2)}) copy-start(bf16[128,20,128]{2,0,1:T(8,128)(2,1)} %param.7) | copy-start | bytes 1966084
  2.8 17.9 %collective-permute-start = (bf16[10,2,128,128]{3,2,1,0:T(8,128)(2,1)}, bf16[10,2,128,128]{3,2,1,0:T(8,128)(2,1)S(1)}, u32[]{:S(2)}, u32[]{:S(2)}) collective-permute-start(bf16[10,2,128,128]{3,2,1,0:T(8,128)(2,1)} %fusion), channel_id=1, source_target_pairs={{0,4},{4,0},{8,12},{12,8},{16,20},{20,16},{24,28},{28,24},{1,5},{5... | collective-permute-start | bytes 1966088 | tf_op jit(solution)/shard_map/ppermute | solution.py:24
  5.9 2.7 %copy-start.3 = (bf16[128,20,128]{2,0,1:T(8,128)(2,1)S(1)}, bf16[128,20,128]{2,0,1:T(8,128)(2,1)}, u32[]{:S(2)}) copy-start(bf16[128,20,128]{2,0,1:T(8,128)(2,1)} %param.5) | copy-start | bytes 1966084
  5.9 32.6 %collective-permute-start.2 = (bf16[10,2,128,128]{3,2,1,0:T(8,128)(2,1)S(1)}, bf16[10,2,128,128]{3,2,1,0:T(8,128)(2,1)S(1)}, u32[]{:S(2)}, u32[]{:S(2)}) collective-permute-start(bf16[10,2,128,128]{3,2,1,0:T(8,128)(2,1)S(1)} %constant_dynamic-slice_fusion.refs_0_.kv_k), channel_id=1, source_target_pairs={{0,8},{1,9},{2,10},{3,11},{4,12},{5,13},{6,14},{7,15},{8,0},{9,1},... | collective-permute-start | bytes 1966088 | tf_op jit(solution)/shard_map/ppermute | solution.py:46
  7.6 31.0 %collective-permute-start.4 = (bf16[10,2,128,128]{3,2,1,0:T(8,128)(2,1)S(1)}, bf16[10,2,128,128]{3,2,1,0:T(8,128)(2,1)}, u32[]{:S(2)}, u32[]{:S(2)}) collective-permute-start(bf16[10,2,128,128]{3,2,1,0:T(8,128)(2,1)S(1)} %constant_dynamic-slice_fusion.refs_0_.kv_k), channel_id=1, source_target_pairs={{0,1},{1,0},{2,3},{3,2},{4,5},{5,4},{6,7},{7,6},{8,16},{9,17},{10,... | collective-permute-start | bytes 1966088 | tf_op jit(solution)/shard_map/ppermute | solution.py:46
  20.7 16.1 %collective-permute-start.1 = (bf16[10,2,128,128]{3,2,1,0:T(8,128)(2,1)}, bf16[10,2,128,128]{3,2,1,0:T(8,128)(2,1)S(1)}, u32[]{:S(2)}, u32[]{:S(2)}) collective-permute-start(bf16[10,2,128,128]{3,2,1,0:T(8,128)(2,1)} %get-tuple-element.17), channel_id=1, source_target_pairs={{0,4},{4,0},{8,12},{12,8},{16,20},{20,16},{24,28},{28,24},{1,5},{5... | collective-permute-start | bytes 1966088 | tf_op jit(solution)/shard_map/ppermute | solution.py:24
  22.4 16.1 %collective-permute-start.3 = (bf16[10,2,128,128]{3,2,1,0:T(8,128)(2,1)S(1)}, bf16[10,2,128,128]{3,2,1,0:T(8,128)(2,1)}, u32[]{:S(2)}, u32[]{:S(2)}) collective-permute-start(bf16[10,2,128,128]{3,2,1,0:T(8,128)(2,1)S(1)} %collective-permute-done.refs_1_.kv_o), channel_id=1, source_target_pairs={{0,8},{1,9},{2,10},{3,11},{4,12},{5,13},{6,14},{7,15},{8,0},{9,1},... | collective-permute-start | bytes 1966088 | tf_op jit(solution)/shard_map/ppermute | solution.py:46
  24.1 14.5 %collective-permute-start.5 = (bf16[10,2,128,128]{3,2,1,0:T(8,128)(2,1)S(1)}, bf16[10,2,128,128]{3,2,1,0:T(8,128)(2,1)}, u32[]{:S(2)}, u32[]{:S(2)}) collective-permute-start(bf16[10,2,128,128]{3,2,1,0:T(8,128)(2,1)S(1)} %collective-permute-done.refs_1_.kv_o), channel_id=1, source_target_pairs={{0,1},{1,0},{2,3},{3,2},{4,5},{5,4},{6,7},{7,6},{8,16},{9,17},{10,... | collective-permute-start | bytes 1966088 | tf_op jit(solution)/shard_map/ppermute | solution.py:46
  36.9 12.4 %collective-permute-start.7 = (bf16[4,4,128,128]{3,2,1,0:T(8,128)(2,1)S(1)}, bf16[4,4,128,128]{3,2,1,0:T(8,128)(2,1)S(1)}, u32[]{:S(2)}, u32[]{:S(2)}) collective-permute-start(bf16[4,4,128,128]{3,2,1,0:T(8,128)(2,1)S(1)} %pad_maximum_fusion.1), channel_id=1, source_target_pairs={{0,8},{1,9},{2,10},{3,11},{4,12},{5,13},{6,14},{7,15},{8,0},{9,1},... | collective-permute-start | bytes 1572872 | tf_op jit(solution)/shard_map/ppermute | solution.py:46
  38.6 15.3 %collective-permute-start.8 = (bf16[4,4,128,128]{3,2,1,0:T(8,128)(2,1)S(1)}, bf16[4,4,128,128]{3,2,1,0:T(8,128)(2,1)S(1)}, u32[]{:S(2)}, u32[]{:S(2)}) collective-permute-start(bf16[4,4,128,128]{3,2,1,0:T(8,128)(2,1)S(1)} %pad_maximum_fusion.1), channel_id=1, source_target_pairs={{0,1},{1,0},{2,3},{3,2},{4,5},{5,4},{6,7},{7,6},{8,16},{9,17},{10,... | collective-permute-start | bytes 1572872 | tf_op jit(solution)/shard_map/ppermute | solution.py:46
  47.6 11.0 %collective-permute-start.6 = (bf16[10,128,128]{2,1,0:T(8,128)(2,1)S(1)}, bf16[10,128,128]{2,1,0:T(8,128)(2,1)S(1)}, u32[]{:S(2)}, u32[]{:S(2)}) collective-permute-start(bf16[10,128,128]{2,1,0:T(8,128)(2,1)S(1)} %get-tuple-element.20), channel_id=1, source_target_pairs={{0,4},{4,0},{8,12},{12,8},{16,20},{20,16},{24,28},{28,24},{1,5},{5... | collective-permute-start | bytes 983048 | tf_op jit(solution)/shard_map/ppermute | solution.py:24
  49.3 4.8 %collective-permute-start.9 = (f32[10,2,256]{2,1,0:T(2,128)S(1)}, f32[10,2,256]{2,1,0:T(2,128)S(1)}, u32[]{:S(2)}, u32[]{:S(2)}) collective-permute-start(f32[10,2,256]{2,1,0:T(2,128)S(1)} %get-tuple-element.22.refs_0_), channel_id=1, source_target_pairs={{0,8},{1,9},{2,10},{3,11},{4,12},{5,13},{6,14},{7,15},{8,0},{9,1},... | collective-permute-start | bytes 61448 | tf_op jit(solution)/shard_map/ppermute | solution.py:46
  52.3 1.8 %collective-permute-start.10 = (f32[10,2,256]{2,1,0:T(2,128)S(1)}, f32[10,2,256]{2,1,0:T(2,128)S(1)}, u32[]{:S(2)}, u32[]{:S(2)}) collective-permute-start(f32[10,2,256]{2,1,0:T(2,128)S(1)} %get-tuple-element.22.refs_0_), channel_id=1, source_target_pairs={{0,1},{1,0},{2,3},{3,2},{4,5},{5,4},{6,7},{7,6},{8,16},{9,17},{10,... | collective-permute-start | bytes 61448 | tf_op jit(solution)/shard_map/ppermute | solution.py:46
  52.4 14.4 %collective-permute-start.11 = (bf16[4,4,128,128]{3,2,1,0:T(8,128)(2,1)S(1)}, bf16[4,4,128,128]{3,2,1,0:T(8,128)(2,1)S(1)}, u32[]{:S(2)}, u32[]{:S(2)}) collective-permute-start(bf16[4,4,128,128]{3,2,1,0:T(8,128)(2,1)S(1)} %pad_maximum_fusion.2), channel_id=1, source_target_pairs={{0,8},{1,9},{2,10},{3,11},{4,12},{5,13},{6,14},{7,15},{8,0},{9,1},... | collective-permute-start | bytes 1572872 | tf_op jit(solution)/shard_map/ppermute | solution.py:46
  53.9 12.9 %collective-permute-start.12 = (bf16[4,4,128,128]{3,2,1,0:T(8,128)(2,1)S(1)}, bf16[4,4,128,128]{3,2,1,0:T(8,128)(2,1)S(1)}, u32[]{:S(2)}, u32[]{:S(2)}) collective-permute-start(bf16[4,4,128,128]{3,2,1,0:T(8,128)(2,1)S(1)} %pad_maximum_fusion.2), channel_id=1, source_target_pairs={{0,1},{1,0},{2,3},{3,2},{4,5},{5,4},{6,7},{7,6},{8,16},{9,17},{10,... | collective-permute-start | bytes 1572872 | tf_op jit(solution)/shard_map/ppermute | solution.py:46
  57.3 8.6 %collective-permute-start.13 = (bf16[4,2,128,128]{3,2,1,0:T(8,128)(2,1)S(1)}, bf16[4,2,128,128]{3,2,1,0:T(8,128)(2,1)S(1)}, u32[]{:S(2)}, u32[]{:S(2)}) collective-permute-start(bf16[4,2,128,128]{3,2,1,0:T(8,128)(2,1)S(1)} %get-tuple-element.26), channel_id=1, source_target_pairs={{0,4},{4,0},{8,12},{12,8},{16,20},{20,16},{24,28},{28,24},{1,5},{5... | collective-permute-start | bytes 786440 | tf_op jit(solution)/shard_map/ppermute | solution.py:24
  65.9 7.7 %collective-permute-start.14 = (bf16[2,4,128,128]{3,2,1,0:T(8,128)(2,1)S(1)}, bf16[2,4,128,128]{3,2,1,0:T(8,128)(2,1)S(1)}, u32[]{:S(2)}, u32[]{:S(2)}) collective-permute-start(bf16[2,4,128,128]{3,2,1,0:T(8,128)(2,1)S(1)} %pad_maximum_fusion.3), channel_id=1, source_target_pairs={{0,8},{1,9},{2,10},{3,11},{4,12},{5,13},{6,14},{7,15},{8,0},{9,1},... | collective-permute-start | bytes 786440 | tf_op jit(solution)/shard_map/ppermute | solution.py:46
  66.2 7.4 %collective-permute-start.15 = (bf16[2,4,128,128]{3,2,1,0:T(8,128)(2,1)S(1)}, bf16[2,4,128,128]{3,2,1,0:T(8,128)(2,1)S(1)}, u32[]{:S(2)}, u32[]{:S(2)}) collective-permute-start(bf16[2,4,128,128]{3,2,1,0:T(8,128)(2,1)S(1)} %pad_maximum_fusion.3), channel_id=1, source_target_pairs={{0,1},{1,0},{2,3},{3,2},{4,5},{5,4},{6,7},{7,6},{8,16},{9,17},{10,... | collective-permute-start | bytes 786440 | tf_op jit(solution)/shard_map/ppermute | solution.py:46
  70.0 9.2 %collective-permute-start.16 = (bf16[4,2,128,128]{3,2,1,0:T(8,128)(2,1)S(1)}, bf16[4,2,128,128]{3,2,1,0:T(8,128)(2,1)S(1)}, u32[]{:S(2)}, u32[]{:S(2)}) collective-permute-start(bf16[4,2,128,128]{3,2,1,0:T(8,128)(2,1)S(1)} %get-tuple-element.29), channel_id=1, source_target_pairs={{0,4},{4,0},{8,12},{12,8},{16,20},{20,16},{24,28},{28,24},{1,5},{5... | collective-permute-start | bytes 786440 | tf_op jit(solution)/shard_map/ppermute | solution.py:24
  75.5 5.6 %collective-permute-start.17 = (bf16[2,2,128,128]{3,2,1,0:T(8,128)(2,1)S(1)}, bf16[2,2,128,128]{3,2,1,0:T(8,128)(2,1)S(1)}, u32[]{:S(2)}, u32[]{:S(2)}) collective-permute-start(bf16[2,2,128,128]{3,2,1,0:T(8,128)(2,1)S(1)} %get-tuple-element.30), channel_id=1, source_target_pairs={{0,4},{4,0},{8,12},{12,8},{16,20},{20,16},{24,28},{28,24},{1,5},{5... | collective-permute-start | bytes 393224 | tf_op jit(solution)/shard_map/ppermute | solution.py:24

commit v4 on v3

--- a/solution.py
+++ b/solution.py
@@ -96,12 +96,16 @@
         weight_grads = [
             nt(both(key_refs[2 * side], key_refs[2 * side + 1], head, 1), grads) for side in range(3)
         ]
-        mixed = exps[0] * weight_grads[0] + exps[1] * weight_grads[1] + exps[2] * weight_grads[2]
         inverse = 1.0 / total
-        delta = jnp.sum(mixed, axis=0, keepdims=True) * inverse
+        weights = [element * inverse for element in exps]
+        mixed = [
+            weight.astype(jnp.bfloat16).astype(jnp.float32) * weight_grad
+            for weight, weight_grad in zip(weights, weight_grads)
+        ]
+        delta = jnp.sum(mixed[0] + mixed[1] + mixed[2], axis=0, keepdims=True)
         result = None
         for side in range(3):
-            score_grad = (exps[side] * inverse * (weight_grads[side] - delta)).astype(jnp.bfloat16)
+            score_grad = (weights[side] * (weight_grads[side] - delta)).astype(jnp.bfloat16)
             term = tn(score_grad, both(key_refs[2 * side], key_refs[2 * side + 1], head, 0))
             result = term if result is None else result + term
         result = (result * scale).astype(jnp.bfloat16)
@@ -247,7 +251,7 @@
             piece = after(qd_pieces[index + 1], qd_sides[-1][0] if index == 0 else dkv_back[0])
             qd_sides.append([beside(piece, 0), beside(piece, 1)])
         count = high - low
-        heads = 2 if low % 2 == 0 and count % 2 == 0 else 1
+        heads = count
         shift = low // heads
         pair_spec = pl.BlockSpec((heads, 2, block, width), lambda i: (i, 0, 0, 0))
         quad_spec = pl.BlockSpec((heads, 4, block, width), lambda i: (i, 0, 0, 0))

time: 82.6 us -> 82.6 us (level)
  no operation moved by 1% of the time
where the time goes in v4:
time: 82.6 us; the launch traced here: 82.5 us
  waiting for transfers between devices  36.6 us (44%)
  starting transfers between devices  19.6 us (24%)
  Pallas kernels  17.4 us (21%)
  other arithmetic  7 us (8%)
  between operations  0.95 us (1%)
  local copies, waits for them, and re-layouts  0.9 us (1%)
    ppermute x6, waiting for transfers between devices, across(): return lax.ppermute(value, axis, [(i, i ^ 1) for i in range(size)])  33.2 us
    ppermute x12, starting transfers between devices, beside(): return lax.ppermute(value, ('seq', 'dp'), pairs)  9.85 us
    ppermute x6, starting transfers between devices, across(): return lax.ppermute(value, axis, [(i, i ^ 1) for i in range(size)])  9.76 us
    pallas_call x1, Pallas kernels, per_device(): pl.pallas_call(partial(query_kernel, factor, scale, heads), grid=(local /...  9.44 us
    pallas_call x3, Pallas kernels, per_device(): pl.pallas_call(partial(key_kernel, factor, scale, heads, low), grid=(coun...  7.92 us
    another operation x3, other arithmetic, by_head(): jnp.stack([jnp.transpose(left, (1, 0, 2)), jnp.transpose(right, (1, 0, 2)...  4.24 us
    ppermute x12, waiting for transfers between devices, beside(): return lax.ppermute(value, ('seq', 'dp'), pairs)  3.41 us
    transpose x2, other arithmetic, home(): return jnp.transpose(jnp.concatenate([low, high], axis=0), (1, 0, 2))  2.07 us
  transfers between devices with their start and end apart: 18, of which 8 were waited for; matrix products, arithmetic and copies ran while one was open for 5% of the time, Pallas kernels for 21%

profile of v4, /device:TPU:0, one launch (start us, length us, event | category | flops | bytes accessed | tf_op | source)
XLA Modules:
  0.0 82.5 jit_solution(12706072103006276985)
XLA Ops:
  0.6 0.0 copy-start
  0.6 0.0 copy-start.2
  0.7 0.0 copy-start.1
  0.7 2.1 %fusion = bf16[10,2,128,128]{3,2,1,0:T(8,128)(2,1)} fusion(s32[]{:T(128)S(6)} %select_n.85, bf16[20,1,128,128]{3,2,1,0:T(8,128)(2,1)} %bitcast.57, bf16[20,1,128,128]{3,2,1,0:T(8,128)(2,1)} %bitcast.55), kind=kLoop, calls=%fused_computation.7 | loop fusion | flops 327680 | bytes 1966084 | tf_op jit(solution)/shard_map/stack | solution.py:190
  2.8 3.0 %collective-permute-start = (bf16[10,2,128,128]{3,2,1,0:T(8,128)(2,1)}, bf16[10,2,128,128]{3,2,1,0:T(8,128)(2,1)S(1)}, u32[]{:S(2)}, u32[]{:S(2)}) collective-permute-start(bf16[10,2,128,128]{3,2,1,0:T(8,128)(2,1)} %fusion), channel_id=1, source_target_pairs={{0,4},{4,0},{8,12},{12,8},{16,20},{20,16},{24,28},{28,24},{1,5},{5... | collective-permute-start | bytes 1966088 | tf_op jit(solution)/shard_map/ppermute | solution.py:24
  5.7 0.0 copy-done.2
  5.7 0.0 copy-done.1
  5.7 0.1 pad_maximum_fusion
  5.9 0.0 copy-start.3
  5.9 1.6 %collective-permute-start.2 = (bf16[10,2,128,128]{3,2,1,0:T(8,128)(2,1)S(1)}, bf16[10,2,128,128]{3,2,1,0:T(8,128)(2,1)S(1)}, u32[]{:S(2)}, u32[]{:S(2)}) collective-permute-start(bf16[10,2,128,128]{3,2,1,0:T(8,128)(2,1)S(1)} %constant_dynamic-slice_fusion.refs_0_.kv_k), channel_id=1, source_target_pairs={{0,8},{1,9},{2,10},{3,11},{4,12},{5,13},{6,14},{7,15},{8,0},{9,1},... | collective-permute-start | bytes 1966088 | tf_op jit(solution)/shard_map/ppermute | solution.py:46
  7.6 0.0 collective-permute-start.4
  7.6 0.1 broadcast_add_fusion.2
  7.7 0.1 add_multiply_fusion
  7.7 0.1 broadcast_add_fusion
  7.8 0.1 stack_broadcast_in_dim.11
  7.9 0.1 stack_broadcast_in_dim.10
  8.0 0.1 stack.56
  8.1 0.1 eq.66
  8.2 0.0 copy-done
  8.2 0.1 constant_dynamic-slice_fusion.1
  8.3 0.1 copy.24
  8.4 0.1 multiply_reduce_fusion
  8.6 2.0 %fusion.1 = (bf16[10,2,128,128]{3,2,1,0:T(8,128)(2,1)}, bf16[10,2,128,128]{3,2,1,0:T(8,128)(2,1)S(1)}) fusion(s32[]{:T(128)S(6)} %select_n.85, bf16[20,1,128,128]{3,2,1,0:T(8,128)(2,1)S(1)} %bitcast.59, bf16[20,1,128,128]{3,2,1,0:T(8,128)(2,1)} %bitcast.60, s32[]{:T(128)S(6)} %select_n.79), kind=kLoop, calls=%fused_computation.8 | loop fusion | flops 655360 | bytes 2621448 | tf_op jit(solution)/shard_map/stack | solution.py:190
  10.6 10.1 %collective-permute-done.refs_1_.kv_o = bf16[10,2,128,128]{3,2,1,0:T(8,128)(2,1)S(1)} collective-permute-done((bf16[10,2,128,128]{3,2,1,0:T(8,128)(2,1)}, bf16[10,2,128,128]{3,2,1,0:T(8,128)(2,1)S(1)}, u32[]{:S(2)}, u32[]{:S(2)}) %collective-permute-start) | collective-permute-done | bytes 655392 | tf_op jit(solution)/shard_map/ppermute | solution.py:24
  20.7 1.7 %collective-permute-start.1 = (bf16[10,2,128,128]{3,2,1,0:T(8,128)(2,1)}, bf16[10,2,128,128]{3,2,1,0:T(8,128)(2,1)S(1)}, u32[]{:S(2)}, u32[]{:S(2)}) collective-permute-start(bf16[10,2,128,128]{3,2,1,0:T(8,128)(2,1)} %get-tuple-element.17), channel_id=1, source_target_pairs={{0,4},{4,0},{8,12},{12,8},{16,20},{20,16},{24,28},{28,24},{1,5},{5... | collective-permute-start | bytes 1966088 | tf_op jit(solution)/shard_map/ppermute | solution.py:24
  22.4 1.6 %collective-permute-start.3 = (bf16[10,2,128,128]{3,2,1,0:T(8,128)(2,1)S(1)}, bf16[10,2,128,128]{3,2,1,0:T(8,128)(2,1)}, u32[]{:S(2)}, u32[]{:S(2)}) collective-permute-start(bf16[10,2,128,128]{3,2,1,0:T(8,128)(2,1)S(1)} %collective-permute-done.refs_1_.kv_o), channel_id=1, source_target_pairs={{0,8},{1,9},{2,10},{3,11},{4,12},{5,13},{6,14},{7,15},{8,0},{9,1},... | collective-permute-start | bytes 1966088 | tf_op jit(solution)/shard_map/ppermute | solution.py:46
  24.1 0.0 collective-permute-start.5
  24.1 0.1 select_n.84.table
  24.2 12.6 %collective-permute-done.1.qd_o = bf16[10,2,128,128]{3,2,1,0:T(8,128)(2,1)S(1)} collective-permute-done((bf16[10,2,128,128]{3,2,1,0:T(8,128)(2,1)}, bf16[10,2,128,128]{3,2,1,0:T(8,128)(2,1)S(1)}, u32[]{:S(2)}, u32[]{:S(2)}) %collective-permute-start.1) | collective-permute-done | bytes 655392 | tf_op jit(solution)/shard_map/ppermute | solution.py:24
  36.9 1.7 %collective-permute-start.7 = (bf16[4,4,128,128]{3,2,1,0:T(8,128)(2,1)S(1)}, bf16[4,4,128,128]{3,2,1,0:T(8,128)(2,1)S(1)}, u32[]{:S(2)}, u32[]{:S(2)}) collective-permute-start(bf16[4,4,128,128]{3,2,1,0:T(8,128)(2,1)S(1)} %pad_maximum_fusion.1), channel_id=1, source_target_pairs={{0,8},{1,9},{2,10},{3,11},{4,12},{5,13},{6,14},{7,15},{8,0},{9,1},... | collective-permute-start | bytes 1572872 | tf_op jit(solution)/shard_map/ppermute | solution.py:46
  38.5 0.0 collective-permute-done.2.refs_2_
  38.6 0.0 collective-permute-start.8
  38.6 0.0 collective-permute-done.4.refs_4_
  38.6 0.0 collective-permute-done.3.refs_3_
  38.6 0.0 collective-permute-done.5.refs_5_
  38.6 9.4 %shard_map.76 = (bf16[10,128,128]{2,1,0:T(8,128)(2,1)S(1)}, bf16[10,128,128]{2,1,0:T(8,128)(2,1)S(1)}, f32[10,2,256]{2,1,0:T(2,128)S(1)}) custom-call(f32[240]{0:T(256)S(1)} %select_n.84.table, bf16[10,2,128,128]{3,2,1,0:T(8,128)(2,1)S(1)} %get-tuple-element.37.qd_k, bf16[10,2,128,128]{3,2,1,0:T(8,128)(2,1)S(1)} %collective-permute-done.1.qd_o, ...), custom_call_target="tpu_custom_call" | custom-call | flops 12079595520 | bytes 6553600 | tf_op jit(solution)/shard_map/pallas_call | solution.py:219
  48.0 1.6 %collective-permute-start.6 = (bf16[10,128,128]{2,1,0:T(8,128)(2,1)S(1)}, bf16[10,128,128]{2,1,0:T(8,128)(2,1)S(1)}, u32[]{:S(2)}, u32[]{:S(2)}) collective-permute-start(bf16[10,128,128]{2,1,0:T(8,128)(2,1)S(1)} %get-tuple-element.20), channel_id=1, source_target_pairs={{0,4},{4,0},{8,12},{12,8},{16,20},{20,16},{24,28},{28,24},{1,5},{5... | collective-permute-start | bytes 983048 | tf_op jit(solution)/shard_map/ppermute | solution.py:24
  49.7 0.0 collective-permute-done.7.side_a
  49.7 3.1 %collective-permute-start.9 = (f32[10,2,256]{2,1,0:T(2,128)S(1)}, f32[10,2,256]{2,1,0:T(2,128)S(1)}, u32[]{:S(2)}, u32[]{:S(2)}) collective-permute-start(f32[10,2,256]{2,1,0:T(2,128)S(1)} %get-tuple-element.22.refs_0_), channel_id=1, source_target_pairs={{0,8},{1,9},{2,10},{3,11},{4,12},{5,13},{6,14},{7,15},{8,0},{9,1},... | collective-permute-start | bytes 61448 | tf_op jit(solution)/shard_map/ppermute | solution.py:46
  52.8 0.0 collective-permute-start.10
  52.8 1.1 %collective-permute-start.11 = (bf16[4,4,128,128]{3,2,1,0:T(8,128)(2,1)S(1)}, bf16[4,4,128,128]{3,2,1,0:T(8,128)(2,1)S(1)}, u32[]{:S(2)}, u32[]{:S(2)}) collective-permute-start(bf16[4,4,128,128]{3,2,1,0:T(8,128)(2,1)S(1)} %pad_maximum_fusion.2), channel_id=1, source_target_pairs={{0,8},{1,9},{2,10},{3,11},{4,12},{5,13},{6,14},{7,15},{8,0},{9,1},... | collective-permute-start | bytes 1572872 | tf_op jit(solution)/shard_map/ppermute | solution.py:46
  53.9 0.0 collective-permute-done.8.side_b
  53.9 0.0 collective-permute-start.12
  53.9 0.7 collective-permute-done.9.refs_1_
  54.5 0.0 collective-permute-done.10.refs_2_
  54.5 3.0 %shard_map.77 = (bf16[4,2,128,128]{3,2,1,0:T(8,128)(2,1)S(1)}, bf16[4,2,128,128]{3,2,1,0:T(8,128)(2,1)S(1)}) custom-call(f32[240]{0:T(256)S(1)} %select_n.84.table, bf16[10,2,128,128]{3,2,1,0:T(8,128)(2,1)S(1)} %constant_dynamic-slice_fusion.refs_0_.kv_k, bf16[10,2,128,128]{3,2,1,0:T(8,128)(2,1)S(1)} %collective-permute-done.refs_1_.kv_o, ...), custom_call_target="tpu_custom_call" | custom-call | flops 6442450944 | bytes 2621440 | tf_op jit(solution)/shard_map/pallas_call | solution.py:260
  57.6 0.7 collective-permute-start.13
  58.3 0.0 collective-permute-done.6
  58.4 0.9 %maximum_bitcast_fusion = bf16[128,20,128]{2,0,1:T(8,128)(2,1)} fusion(bf16[10,128,128]{2,1,0:T(8,128)(2,1)S(1)} %get-tuple-element.43, bf16[10,128,128]{2,1,0:T(8,128)(2,1)S(1)} %get-tuple-element.42), kind=kLoop, calls=%fused_computation.10 | loop fusion | flops 327680 | bytes 1310720 | tf_op jit(solution)/shard_map/transpose | solution.py:288
  59.3 6.4 %collective-permute-done.13 = bf16[4,2,128,128]{3,2,1,0:T(8,128)(2,1)S(1)} collective-permute-done((bf16[4,2,128,128]{3,2,1,0:T(8,128)(2,1)S(1)}, bf16[4,2,128,128]{3,2,1,0:T(8,128)(2,1)S(1)}, u32[]{:S(2)}, u32[]{:S(2)}) %collective-permute-start.13) | collective-permute-done | bytes 262176 | tf_op jit(solution)/shard_map/ppermute | solution.py:24
  65.7 0.8 collective-permute-start.14
  66.5 0.0 collective-permute-start.15
  66.5 0.7 collective-permute-done.11.side_a
  67.2 0.0 collective-permute-done.12.side_b
  67.2 3.0 %shard_map.78 = (bf16[4,2,128,128]{3,2,1,0:T(8,128)(2,1)S(1)}, bf16[4,2,128,128]{3,2,1,0:T(8,128)(2,1)S(1)}) custom-call(f32[240]{0:T(256)S(1)} %select_n.84.table, bf16[10,2,128,128]{3,2,1,0:T(8,128)(2,1)S(1)} %constant_dynamic-slice_fusion.refs_0_.kv_k, bf16[10,2,128,128]{3,2,1,0:T(8,128)(2,1)S(1)} %collective-permute-done.refs_1_.kv_o, ...), custom_call_target="tpu_custom_call" | custom-call | flops 6442450944 | bytes 2621440 | tf_op jit(solution)/shard_map/pallas_call | solution.py:260
  70.2 0.6 collective-permute-start.16
  70.9 2.0 %collective-permute-done.14.side_a = bf16[2,4,128,128]{3,2,1,0:T(8,128)(2,1)S(1)} collective-permute-done((bf16[2,4,128,128]{3,2,1,0:T(8,128)(2,1)S(1)}, bf16[2,4,128,128]{3,2,1,0:T(8,128)(2,1)S(1)}, u32[]{:S(2)}, u32[]{:S(2)}) %collective-permute-start.14) | collective-permute-done | bytes 262176 | tf_op jit(solution)/shard_map/ppermute | solution.py:46
  72.9 0.0 collective-permute-done.15.side_b
  72.9 1.9 %shard_map.79 = (bf16[2,2,128,128]{3,2,1,0:T(8,128)(2,1)S(1)}, bf16[2,2,128,128]{3,2,1,0:T(8,128)(2,1)S(1)}) custom-call(f32[240]{0:T(256)S(1)} %select_n.84.table, bf16[10,2,128,128]{3,2,1,0:T(8,128)(2,1)S(1)} %constant_dynamic-slice_fusion.refs_0_.kv_k, bf16[10,2,128,128]{3,2,1,0:T(8,128)(2,1)S(1)} %collective-permute-done.refs_1_.kv_o, ...), custom_call_target="tpu_custom_call" | custom-call | flops 3221225472 | bytes 1310720 | tf_op jit(solution)/shard_map/pallas_call | solution.py:260
  74.8 2.1 %collective-permute-start.17 = (bf16[2,2,128,128]{3,2,1,0:T(8,128)(2,1)S(1)}, bf16[2,2,128,128]{3,2,1,0:T(8,128)(2,1)S(1)}, u32[]{:S(2)}, u32[]{:S(2)}) collective-permute-start(bf16[2,2,128,128]{3,2,1,0:T(8,128)(2,1)S(1)} %get-tuple-element.30), channel_id=1, source_target_pairs={{0,4},{4,0},{8,12},{12,8},{16,20},{20,16},{24,28},{28,24},{1,5},{5... | collective-permute-start | bytes 393224 | tf_op jit(solution)/shard_map/ppermute | solution.py:24
  76.9 2.6 %collective-permute-done.16 = bf16[4,2,128,128]{3,2,1,0:T(8,128)(2,1)S(1)} collective-permute-done((bf16[4,2,128,128]{3,2,1,0:T(8,128)(2,1)S(1)}, bf16[4,2,128,128]{3,2,1,0:T(8,128)(2,1)S(1)}, u32[]{:S(2)}, u32[]{:S(2)}) %collective-permute-start.16) | collective-permute-done | bytes 262176 | tf_op jit(solution)/shard_map/ppermute | solution.py:24
  79.6 1.6 %collective-permute-done.17 = bf16[2,2,128,128]{3,2,1,0:T(8,128)(2,1)S(1)} collective-permute-done((bf16[2,2,128,128]{3,2,1,0:T(8,128)(2,1)S(1)}, bf16[2,2,128,128]{3,2,1,0:T(8,128)(2,1)S(1)}, u32[]{:S(2)}, u32[]{:S(2)}) %collective-permute-start.17) | collective-permute-done | bytes 131104 | tf_op jit(solution)/shard_map/ppermute | solution.py:24
  81.2 0.1 fusion.4
  81.3 1.2 %maximum_bitcast_fusion.1 = (bf16[128,20,128]{2,0,1:T(8,128)(2,1)}, bf16[128,20,128]{2,0,1:T(8,128)(2,1)}) fusion(bf16[10,128,128]{2,1,0:T(8,128)(2,1)S(1)} %get-tuple-element.34, bf16[10,128,128]{2,1,0:T(8,128)(2,1)S(1)} %get-tuple-element.35, bf16[10,128,128]{2,1,0:T(8,128)(2,1)S(1)} %fusion.3, bf16[10,128,128]{2,1,0:T(8,128)(2,1)S(1)} %get-tuple-element.33), kind=kLoop, calls=%fused_computation.11 | loop fusion | flops 655360 | bytes 2621440 | tf_op jit(solution)/shard_map/transpose | solution.py:288
  (27 shorter events, 0.6 us)
Async XLA Ops:
  0.6 7.6 %copy-start = (s32[20,8,5]{0,1,2:T(8,128)S(1)}, s32[20,8,5]{0,1,2:T(8,128)}, u32[]{:S(2)}) copy-start(s32[20,8,5]{0,1,2:T(8,128)} %param.9) | copy-start | bytes 9604
  0.6 5.1 %copy-start.2 = (bf16[128,20,128]{2,0,1:T(8,128)(2,1)S(1)}, bf16[128,20,128]{2,0,1:T(8,128)(2,1)}, u32[]{:S(2)}) copy-start(bf16[128,20,128]{2,0,1:T(8,128)(2,1)} %param.6) | copy-start | bytes 1966084
  0.7 5.1 %copy-start.1 = (bf16[128,20,128]{2,0,1:T(8,128)(2,1)S(1)}, bf16[128,20,128]{2,0,1:T(8,128)(2,1)}, u32[]{:S(2)}) copy-start(bf16[128,20,128]{2,0,1:T(8,128)(2,1)} %param.7) | copy-start | bytes 1966084
  2.8 17.9 %collective-permute-start = (bf16[10,2,128,128]{3,2,1,0:T(8,128)(2,1)}, bf16[10,2,128,128]{3,2,1,0:T(8,128)(2,1)S(1)}, u32[]{:S(2)}, u32[]{:S(2)}) collective-permute-start(bf16[10,2,128,128]{3,2,1,0:T(8,128)(2,1)} %fusion), channel_id=1, source_target_pairs={{0,4},{4,0},{8,12},{12,8},{16,20},{20,16},{24,28},{28,24},{1,5},{5... | collective-permute-start | bytes 1966088 | tf_op jit(solution)/shard_map/ppermute | solution.py:24
  5.9 2.7 %copy-start.3 = (bf16[128,20,128]{2,0,1:T(8,128)(2,1)S(1)}, bf16[128,20,128]{2,0,1:T(8,128)(2,1)}, u32[]{:S(2)}) copy-start(bf16[128,20,128]{2,0,1:T(8,128)(2,1)} %param.5) | copy-start | bytes 1966084
  5.9 32.6 %collective-permute-start.2 = (bf16[10,2,128,128]{3,2,1,0:T(8,128)(2,1)S(1)}, bf16[10,2,128,128]{3,2,1,0:T(8,128)(2,1)S(1)}, u32[]{:S(2)}, u32[]{:S(2)}) collective-permute-start(bf16[10,2,128,128]{3,2,1,0:T(8,128)(2,1)S(1)} %constant_dynamic-slice_fusion.refs_0_.kv_k), channel_id=1, source_target_pairs={{0,8},{1,9},{2,10},{3,11},{4,12},{5,13},{6,14},{7,15},{8,0},{9,1},... | collective-permute-start | bytes 1966088 | tf_op jit(solution)/shard_map/ppermute | solution.py:46
  7.6 31.0 %collective-permute-start.4 = (bf16[10,2,128,128]{3,2,1,0:T(8,128)(2,1)S(1)}, bf16[10,2,128,128]{3,2,1,0:T(8,128)(2,1)}, u32[]{:S(2)}, u32[]{:S(2)}) collective-permute-start(bf16[10,2,128,128]{3,2,1,0:T(8,128)(2,1)S(1)} %constant_dynamic-slice_fusion.refs_0_.kv_k), channel_id=1, source_target_pairs={{0,1},{1,0},{2,3},{3,2},{4,5},{5,4},{6,7},{7,6},{8,16},{9,17},{10,... | collective-permute-start | bytes 1966088 | tf_op jit(solution)/shard_map/ppermute | solution.py:46
  20.7 16.1 %collective-permute-start.1 = (bf16[10,2,128,128]{3,2,1,0:T(8,128)(2,1)}, bf16[10,2,128,128]{3,2,1,0:T(8,128)(2,1)S(1)}, u32[]{:S(2)}, u32[]{:S(2)}) collective-permute-start(bf16[10,2,128,128]{3,2,1,0:T(8,128)(2,1)} %get-tuple-element.17), channel_id=1, source_target_pairs={{0,4},{4,0},{8,12},{12,8},{16,20},{20,16},{24,28},{28,24},{1,5},{5... | collective-permute-start | bytes 1966088 | tf_op jit(solution)/shard_map/ppermute | solution.py:24
  22.4 16.1 %collective-permute-start.3 = (bf16[10,2,128,128]{3,2,1,0:T(8,128)(2,1)S(1)}, bf16[10,2,128,128]{3,2,1,0:T(8,128)(2,1)}, u32[]{:S(2)}, u32[]{:S(2)}) collective-permute-start(bf16[10,2,128,128]{3,2,1,0:T(8,128)(2,1)S(1)} %collective-permute-done.refs_1_.kv_o), channel_id=1, source_target_pairs={{0,8},{1,9},{2,10},{3,11},{4,12},{5,13},{6,14},{7,15},{8,0},{9,1},... | collective-permute-start | bytes 1966088 | tf_op jit(solution)/shard_map/ppermute | solution.py:46
  24.1 14.5 %collective-permute-start.5 = (bf16[10,2,128,128]{3,2,1,0:T(8,128)(2,1)S(1)}, bf16[10,2,128,128]{3,2,1,0:T(8,128)(2,1)}, u32[]{:S(2)}, u32[]{:S(2)}) collective-permute-start(bf16[10,2,128,128]{3,2,1,0:T(8,128)(2,1)S(1)} %collective-permute-done.refs_1_.kv_o), channel_id=1, source_target_pairs={{0,1},{1,0},{2,3},{3,2},{4,5},{5,4},{6,7},{7,6},{8,16},{9,17},{10,... | collective-permute-start | bytes 1966088 | tf_op jit(solution)/shard_map/ppermute | solution.py:46
  36.9 12.8 %collective-permute-start.7 = (bf16[4,4,128,128]{3,2,1,0:T(8,128)(2,1)S(1)}, bf16[4,4,128,128]{3,2,1,0:T(8,128)(2,1)S(1)}, u32[]{:S(2)}, u32[]{:S(2)}) collective-permute-start(bf16[4,4,128,128]{3,2,1,0:T(8,128)(2,1)S(1)} %pad_maximum_fusion.1), channel_id=1, source_target_pairs={{0,8},{1,9},{2,10},{3,11},{4,12},{5,13},{6,14},{7,15},{8,0},{9,1},... | collective-permute-start | bytes 1572872 | tf_op jit(solution)/shard_map/ppermute | solution.py:46
  38.6 15.3 %collective-permute-start.8 = (bf16[4,4,128,128]{3,2,1,0:T(8,128)(2,1)S(1)}, bf16[4,4,128,128]{3,2,1,0:T(8,128)(2,1)S(1)}, u32[]{:S(2)}, u32[]{:S(2)}) collective-permute-start(bf16[4,4,128,128]{3,2,1,0:T(8,128)(2,1)S(1)} %pad_maximum_fusion.1), channel_id=1, source_target_pairs={{0,1},{1,0},{2,3},{3,2},{4,5},{5,4},{6,7},{7,6},{8,16},{9,17},{10,... | collective-permute-start | bytes 1572872 | tf_op jit(solution)/shard_map/ppermute | solution.py:46
  48.0 10.3 %collective-permute-start.6 = (bf16[10,128,128]{2,1,0:T(8,128)(2,1)S(1)}, bf16[10,128,128]{2,1,0:T(8,128)(2,1)S(1)}, u32[]{:S(2)}, u32[]{:S(2)}) collective-permute-start(bf16[10,128,128]{2,1,0:T(8,128)(2,1)S(1)} %get-tuple-element.20), channel_id=1, source_target_pairs={{0,4},{4,0},{8,12},{12,8},{16,20},{20,16},{24,28},{28,24},{1,5},{5... | collective-permute-start | bytes 983048 | tf_op jit(solution)/shard_map/ppermute | solution.py:24
  49.7 4.8 %collective-permute-start.9 = (f32[10,2,256]{2,1,0:T(2,128)S(1)}, f32[10,2,256]{2,1,0:T(2,128)S(1)}, u32[]{:S(2)}, u32[]{:S(2)}) collective-permute-start(f32[10,2,256]{2,1,0:T(2,128)S(1)} %get-tuple-element.22.refs_0_), channel_id=1, source_target_pairs={{0,8},{1,9},{2,10},{3,11},{4,12},{5,13},{6,14},{7,15},{8,0},{9,1},... | collective-permute-start | bytes 61448 | tf_op jit(solution)/shard_map/ppermute | solution.py:46
  52.8 1.8 %collective-permute-start.10 = (f32[10,2,256]{2,1,0:T(2,128)S(1)}, f32[10,2,256]{2,1,0:T(2,128)S(1)}, u32[]{:S(2)}, u32[]{:S(2)}) collective-permute-start(f32[10,2,256]{2,1,0:T(2,128)S(1)} %get-tuple-element.22.refs_0_), channel_id=1, source_target_pairs={{0,1},{1,0},{2,3},{3,2},{4,5},{5,4},{6,7},{7,6},{8,16},{9,17},{10,... | collective-permute-start | bytes 61448 | tf_op jit(solution)/shard_map/ppermute | solution.py:46
  52.8 14.4 %collective-permute-start.11 = (bf16[4,4,128,128]{3,2,1,0:T(8,128)(2,1)S(1)}, bf16[4,4,128,128]{3,2,1,0:T(8,128)(2,1)S(1)}, u32[]{:S(2)}, u32[]{:S(2)}) collective-permute-start(bf16[4,4,128,128]{3,2,1,0:T(8,128)(2,1)S(1)} %pad_maximum_fusion.2), channel_id=1, source_target_pairs={{0,8},{1,9},{2,10},{3,11},{4,12},{5,13},{6,14},{7,15},{8,0},{9,1},... | collective-permute-start | bytes 1572872 | tf_op jit(solution)/shard_map/ppermute | solution.py:46
  53.9 13.3 %collective-permute-start.12 = (bf16[4,4,128,128]{3,2,1,0:T(8,128)(2,1)S(1)}, bf16[4,4,128,128]{3,2,1,0:T(8,128)(2,1)S(1)}, u32[]{:S(2)}, u32[]{:S(2)}) collective-permute-start(bf16[4,4,128,128]{3,2,1,0:T(8,128)(2,1)S(1)} %pad_maximum_fusion.2), channel_id=1, source_target_pairs={{0,1},{1,0},{2,3},{3,2},{4,5},{5,4},{6,7},{7,6},{8,16},{9,17},{10,... | collective-permute-start | bytes 1572872 | tf_op jit(solution)/shard_map/ppermute | solution.py:46
  57.6 8.1 %collective-permute-start.13 = (bf16[4,2,128,128]{3,2,1,0:T(8,128)(2,1)S(1)}, bf16[4,2,128,128]{3,2,1,0:T(8,128)(2,1)S(1)}, u32[]{:S(2)}, u32[]{:S(2)}) collective-permute-start(bf16[4,2,128,128]{3,2,1,0:T(8,128)(2,1)S(1)} %get-tuple-element.26), channel_id=1, source_target_pairs={{0,4},{4,0},{8,12},{12,8},{16,20},{20,16},{24,28},{28,24},{1,5},{5... | collective-permute-start | bytes 786440 | tf_op jit(solution)/shard_map/ppermute | solution.py:24
  65.7 7.2 %collective-permute-start.14 = (bf16[2,4,128,128]{3,2,1,0:T(8,128)(2,1)S(1)}, bf16[2,4,128,128]{3,2,1,0:T(8,128)(2,1)S(1)}, u32[]{:S(2)}, u32[]{:S(2)}) collective-permute-start(bf16[2,4,128,128]{3,2,1,0:T(8,128)(2,1)S(1)} %pad_maximum_fusion.3), channel_id=1, source_target_pairs={{0,8},{1,9},{2,10},{3,11},{4,12},{5,13},{6,14},{7,15},{8,0},{9,1},... | collective-permute-start | bytes 786440 | tf_op jit(solution)/shard_map/ppermute | solution.py:46
  66.5 6.4 %collective-permute-start.15 = (bf16[2,4,128,128]{3,2,1,0:T(8,128)(2,1)S(1)}, bf16[2,4,128,128]{3,2,1,0:T(8,128)(2,1)S(1)}, u32[]{:S(2)}, u32[]{:S(2)}) collective-permute-start(bf16[2,4,128,128]{3,2,1,0:T(8,128)(2,1)S(1)} %pad_maximum_fusion.3), channel_id=1, source_target_pairs={{0,1},{1,0},{2,3},{3,2},{4,5},{5,4},{6,7},{7,6},{8,16},{9,17},{10,... | collective-permute-start | bytes 786440 | tf_op jit(solution)/shard_map/ppermute | solution.py:46
  70.2 9.3 %collective-permute-start.16 = (bf16[4,2,128,128]{3,2,1,0:T(8,128)(2,1)S(1)}, bf16[4,2,128,128]{3,2,1,0:T(8,128)(2,1)S(1)}, u32[]{:S(2)}, u32[]{:S(2)}) collective-permute-start(bf16[4,2,128,128]{3,2,1,0:T(8,128)(2,1)S(1)} %get-tuple-element.29), channel_id=1, source_target_pairs={{0,4},{4,0},{8,12},{12,8},{16,20},{20,16},{24,28},{28,24},{1,5},{5... | collective-permute-start | bytes 786440 | tf_op jit(solution)/shard_map/ppermute | solution.py:24
  74.8 6.4 %collective-permute-start.17 = (bf16[2,2,128,128]{3,2,1,0:T(8,128)(2,1)S(1)}, bf16[2,2,128,128]{3,2,1,0:T(8,128)(2,1)S(1)}, u32[]{:S(2)}, u32[]{:S(2)}) collective-permute-start(bf16[2,2,128,128]{3,2,1,0:T(8,128)(2,1)S(1)} %get-tuple-element.30), channel_id=1, source_target_pairs={{0,4},{4,0},{8,12},{12,8},{16,20},{20,16},{24,28},{28,24},{1,5},{5... | collective-permute-start | bytes 393224 | tf_op jit(solution)/shard_map/ppermute | solution.py:24

commit v5 on v4

--- a/solution.py
+++ b/solution.py
@@ -135,7 +135,14 @@
             biases = [[table[at + 2 * a + b] for b in range(2)] for a in range(2)]
             level = stat_refs[side][head, 0:1, :]
             delta = stat_refs[side][head, 1:2, :]
-            weights = jnp.exp2(biased(nt(keys, queries) * factor, biases, block) - level)
+            raw = nt(keys, queries) * factor
+            halves = []
+            for a in range(2):
+                shift = jnp.concatenate(
+                    [biases[a][b] - level[:, b * block : (b + 1) * block] for b in range(2)], axis=1
+                )
+                halves.append(raw[a * block : (a + 1) * block] + shift)
+            weights = jnp.exp2(jnp.concatenate(halves, axis=0))
             weight_grad = nt(values, grads)
             score_grad = (weights * (weight_grad - delta)).astype(jnp.bfloat16)
             value_term = nn(weights.astype(jnp.bfloat16), grads)
@@ -207,7 +214,7 @@
     qd_sides = [[beside(qd_pieces[0], 0), beside(qd_pieces[0], 1)]]
     table = bias_table(block_mask, local, device // RANGE, position, range_total)
 
-    heads = 2 if local % 2 == 0 else 1
+    heads = local // 2 if local % 2 == 0 else local
     pair_spec = pl.BlockSpec((heads, 2, block, width), lambda i: (i, 0, 0, 0))
     quad_spec = pl.BlockSpec((heads, 4, block, width), lambda i: (i, 0, 0, 0))
     one_spec = pl.BlockSpec((heads, block, width), lambda i: (i, 0, 0))
@@ -228,7 +235,7 @@
         ],
         compiler_params=params,
         cost_estimate=pl.CostEstimate(
-            flops=WORK * 2 * 9 * local * tile, bytes_accessed=20 * local * block * width * 2, transcendentals=0
+            flops=2 * WORK * 2 * 9 * local * tile, bytes_accessed=20 * local * block * width * 2, transcendentals=0
         ),
     )(
         table,

time: 82.6 us -> 82 us (level)
  Pallas kernels: 17.4 us -> 16.5 us
    ppermute x12, waiting for transfers between devices: 3.41 us -> 4.46 us  [beside(): return lax.ppermute(value, ('seq', 'dp'), pairs)]
  transfers between devices with their start and end apart: 18 -> 18, of which waited for: 8 -> 8; matrix products, arithmetic and copies ran while one was open for 5% -> 5% of each run, Pallas kernels for 21% -> 20%
where the time goes in v5:
time: 82 us; the launch traced here: 81.8 us
  waiting for transfers between devices  37.1 us (45%)
  starting transfers between devices  19.4 us (24%)
  Pallas kernels  16.5 us (20%)
  other arithmetic  7 us (9%)
  between operations  0.96 us (1%)
  local copies, waits for them, and re-layouts  0.9 us (1%)
    ppermute x6, waiting for transfers between devices, across(): return lax.ppermute(value, axis, [(i, i ^ 1) for i in range(size)])  32.6 us
    ppermute x6, starting transfers between devices, across(): return lax.ppermute(value, axis, [(i, i ^ 1) for i in range(size)])  9.82 us
    ppermute x12, starting transfers between devices, beside(): return lax.ppermute(value, ('seq', 'dp'), pairs)  9.54 us
    pallas_call x1, Pallas kernels, per_device(): pl.pallas_call(partial(query_kernel, factor, scale, heads), grid=(local /...  8.65 us
    pallas_call x3, Pallas kernels, per_device(): pl.pallas_call(partial(key_kernel, factor, scale, heads, low), grid=(coun...  7.87 us
    ppermute x12, waiting for transfers between devices, beside(): return lax.ppermute(value, ('seq', 'dp'), pairs)  4.46 us
    another operation x3, other arithmetic, by_head(): jnp.stack([jnp.transpose(left, (1, 0, 2)), jnp.transpose(right, (1, 0, 2)...  4.24 us
    transpose x2, other arithmetic, home(): return jnp.transpose(jnp.concatenate([low, high], axis=0), (1, 0, 2))  2.07 us
  transfers between devices with their start and end apart: 18, of which 8 were waited for; matrix products, arithmetic and copies ran while one was open for 5% of the time, Pallas kernels for 20%

profile of v5, /device:TPU:0, one launch (start us, length us, event | category | flops | bytes accessed | tf_op | source)
XLA Modules:
  0.0 81.8 jit_solution(1426872990821834943)
XLA Ops:
  0.6 0.0 copy-start
  0.6 0.0 copy-start.2
  0.7 0.0 copy-start.1
  0.7 2.1 %fusion = bf16[10,2,128,128]{3,2,1,0:T(8,128)(2,1)} fusion(s32[]{:T(128)S(6)} %select_n.85, bf16[20,1,128,128]{3,2,1,0:T(8,128)(2,1)} %bitcast.57, bf16[20,1,128,128]{3,2,1,0:T(8,128)(2,1)} %bitcast.55), kind=kLoop, calls=%fused_computation.7 | loop fusion | flops 327680 | bytes 1966084 | tf_op jit(solution)/shard_map/stack | solution.py:197
  2.8 3.0 %collective-permute-start = (bf16[10,2,128,128]{3,2,1,0:T(8,128)(2,1)}, bf16[10,2,128,128]{3,2,1,0:T(8,128)(2,1)S(1)}, u32[]{:S(2)}, u32[]{:S(2)}) collective-permute-start(bf16[10,2,128,128]{3,2,1,0:T(8,128)(2,1)} %fusion), channel_id=1, source_target_pairs={{0,4},{4,0},{8,12},{12,8},{16,20},{20,16},{24,28},{28,24},{1,5},{5... | collective-permute-start | bytes 1966088 | tf_op jit(solution)/shard_map/ppermute | solution.py:24
  5.7 0.0 copy-done.2
  5.7 0.0 copy-done.1
  5.7 0.1 pad_maximum_fusion
  5.9 0.0 copy-start.3
  5.9 1.6 %collective-permute-start.2 = (bf16[10,2,128,128]{3,2,1,0:T(8,128)(2,1)S(1)}, bf16[10,2,128,128]{3,2,1,0:T(8,128)(2,1)S(1)}, u32[]{:S(2)}, u32[]{:S(2)}) collective-permute-start(bf16[10,2,128,128]{3,2,1,0:T(8,128)(2,1)S(1)} %constant_dynamic-slice_fusion.refs_0_.kv_k), channel_id=1, source_target_pairs={{0,8},{1,9},{2,10},{3,11},{4,12},{5,13},{6,14},{7,15},{8,0},{9,1},... | collective-permute-start | bytes 1966088 | tf_op jit(solution)/shard_map/ppermute | solution.py:46
  7.6 0.0 collective-permute-start.4
  7.6 0.1 broadcast_add_fusion.2
  7.7 0.1 add_multiply_fusion
  7.7 0.1 broadcast_add_fusion
  7.8 0.1 stack_broadcast_in_dim.11
  7.9 0.1 stack_broadcast_in_dim.10
  8.0 0.1 stack.56
  8.1 0.1 eq.66
  8.2 0.0 copy-done
  8.2 0.1 constant_dynamic-slice_fusion.1
  8.3 0.1 copy.24
  8.4 0.1 multiply_reduce_fusion
  8.6 2.0 %fusion.1 = (bf16[10,2,128,128]{3,2,1,0:T(8,128)(2,1)}, bf16[10,2,128,128]{3,2,1,0:T(8,128)(2,1)S(1)}) fusion(s32[]{:T(128)S(6)} %select_n.85, bf16[20,1,128,128]{3,2,1,0:T(8,128)(2,1)S(1)} %bitcast.59, bf16[20,1,128,128]{3,2,1,0:T(8,128)(2,1)} %bitcast.60, s32[]{:T(128)S(6)} %select_n.79), kind=kLoop, calls=%fused_computation.8 | loop fusion | flops 655360 | bytes 2621448 | tf_op jit(solution)/shard_map/stack | solution.py:197
  10.6 10.1 %collective-permute-done.refs_1_.kv_o = bf16[10,2,128,128]{3,2,1,0:T(8,128)(2,1)S(1)} collective-permute-done((bf16[10,2,128,128]{3,2,1,0:T(8,128)(2,1)}, bf16[10,2,128,128]{3,2,1,0:T(8,128)(2,1)S(1)}, u32[]{:S(2)}, u32[]{:S(2)}) %collective-permute-start) | collective-permute-done | bytes 655392 | tf_op jit(solution)/shard_map/ppermute | solution.py:24
  20.7 1.7 %collective-permute-start.1 = (bf16[10,2,128,128]{3,2,1,0:T(8,128)(2,1)}, bf16[10,2,128,128]{3,2,1,0:T(8,128)(2,1)S(1)}, u32[]{:S(2)}, u32[]{:S(2)}) collective-permute-start(bf16[10,2,128,128]{3,2,1,0:T(8,128)(2,1)} %get-tuple-element.17), channel_id=1, source_target_pairs={{0,4},{4,0},{8,12},{12,8},{16,20},{20,16},{24,28},{28,24},{1,5},{5... | collective-permute-start | bytes 1966088 | tf_op jit(solution)/shard_map/ppermute | solution.py:24
  22.4 1.6 %collective-permute-start.3 = (bf16[10,2,128,128]{3,2,1,0:T(8,128)(2,1)S(1)}, bf16[10,2,128,128]{3,2,1,0:T(8,128)(2,1)}, u32[]{:S(2)}, u32[]{:S(2)}) collective-permute-start(bf16[10,2,128,128]{3,2,1,0:T(8,128)(2,1)S(1)} %collective-permute-done.refs_1_.kv_o), channel_id=1, source_target_pairs={{0,8},{1,9},{2,10},{3,11},{4,12},{5,13},{6,14},{7,15},{8,0},{9,1},... | collective-permute-start | bytes 1966088 | tf_op jit(solution)/shard_map/ppermute | solution.py:46
  24.1 0.0 collective-permute-start.5
  24.1 0.1 select_n.84.table
  24.2 12.6 %collective-permute-done.1.qd_o = bf16[10,2,128,128]{3,2,1,0:T(8,128)(2,1)S(1)} collective-permute-done((bf16[10,2,128,128]{3,2,1,0:T(8,128)(2,1)}, bf16[10,2,128,128]{3,2,1,0:T(8,128)(2,1)S(1)}, u32[]{:S(2)}, u32[]{:S(2)}) %collective-permute-start.1) | collective-permute-done | bytes 655392 | tf_op jit(solution)/shard_map/ppermute | solution.py:24
  36.9 1.7 %collective-permute-start.7 = (bf16[4,4,128,128]{3,2,1,0:T(8,128)(2,1)S(1)}, bf16[4,4,128,128]{3,2,1,0:T(8,128)(2,1)S(1)}, u32[]{:S(2)}, u32[]{:S(2)}) collective-permute-start(bf16[4,4,128,128]{3,2,1,0:T(8,128)(2,1)S(1)} %pad_maximum_fusion.1), channel_id=1, source_target_pairs={{0,8},{1,9},{2,10},{3,11},{4,12},{5,13},{6,14},{7,15},{8,0},{9,1},... | collective-permute-start | bytes 1572872 | tf_op jit(solution)/shard_map/ppermute | solution.py:46
  38.5 0.0 collective-permute-done.2.refs_2_
  38.6 0.0 collective-permute-start.8
  38.6 0.0 collective-permute-done.4.refs_4_
  38.6 0.0 collective-permute-done.3.refs_3_
  38.6 0.0 collective-permute-done.5.refs_5_
  38.6 8.7 %shard_map.76 = (bf16[10,128,128]{2,1,0:T(8,128)(2,1)S(1)}, bf16[10,128,128]{2,1,0:T(8,128)(2,1)S(1)}, f32[10,2,256]{2,1,0:T(2,128)S(1)}) custom-call(f32[240]{0:T(256)S(1)} %select_n.84.table, bf16[10,2,128,128]{3,2,1,0:T(8,128)(2,1)S(1)} %get-tuple-element.37.qd_k, bf16[10,2,128,128]{3,2,1,0:T(8,128)(2,1)S(1)} %collective-permute-done.1.qd_o, ...), custom_call_target="tpu_custom_call" | custom-call | flops 24159191040 | bytes 6553600 | tf_op jit(solution)/shard_map/pallas_call | solution.py:226
  47.2 1.6 %collective-permute-start.6 = (bf16[10,128,128]{2,1,0:T(8,128)(2,1)S(1)}, bf16[10,128,128]{2,1,0:T(8,128)(2,1)S(1)}, u32[]{:S(2)}, u32[]{:S(2)}) collective-permute-start(bf16[10,128,128]{2,1,0:T(8,128)(2,1)S(1)} %get-tuple-element.20), channel_id=1, source_target_pairs={{0,4},{4,0},{8,12},{12,8},{16,20},{20,16},{24,28},{28,24},{1,5},{5... | collective-permute-start | bytes 983048 | tf_op jit(solution)/shard_map/ppermute | solution.py:24
  48.9 0.4 collective-permute-done.7.side_a
  49.3 2.8 %collective-permute-start.9 = (f32[10,2,256]{2,1,0:T(2,128)S(1)}, f32[10,2,256]{2,1,0:T(2,128)S(1)}, u32[]{:S(2)}, u32[]{:S(2)}) collective-permute-start(f32[10,2,256]{2,1,0:T(2,128)S(1)} %get-tuple-element.22.refs_0_), channel_id=1, source_target_pairs={{0,8},{1,9},{2,10},{3,11},{4,12},{5,13},{6,14},{7,15},{8,0},{9,1},... | collective-permute-start | bytes 61448 | tf_op jit(solution)/shard_map/ppermute | solution.py:46
  52.0 0.0 collective-permute-start.10
  52.0 1.8 %collective-permute-start.11 = (bf16[4,4,128,128]{3,2,1,0:T(8,128)(2,1)S(1)}, bf16[4,4,128,128]{3,2,1,0:T(8,128)(2,1)S(1)}, u32[]{:S(2)}, u32[]{:S(2)}) collective-permute-start(bf16[4,4,128,128]{3,2,1,0:T(8,128)(2,1)S(1)} %pad_maximum_fusion.2), channel_id=1, source_target_pairs={{0,8},{1,9},{2,10},{3,11},{4,12},{5,13},{6,14},{7,15},{8,0},{9,1},... | collective-permute-start | bytes 1572872 | tf_op jit(solution)/shard_map/ppermute | solution.py:46
  53.9 0.0 collective-permute-done.8.side_b
  53.9 0.0 collective-permute-start.12
  53.9 0.0 collective-permute-done.9.refs_1_
  53.9 0.0 collective-permute-done.10.refs_2_
  53.9 3.0 %shard_map.77 = (bf16[4,2,128,128]{3,2,1,0:T(8,128)(2,1)S(1)}, bf16[4,2,128,128]{3,2,1,0:T(8,128)(2,1)S(1)}) custom-call(f32[240]{0:T(256)S(1)} %select_n.84.table, bf16[10,2,128,128]{3,2,1,0:T(8,128)(2,1)S(1)} %constant_dynamic-slice_fusion.refs_0_.kv_k, bf16[10,2,128,128]{3,2,1,0:T(8,128)(2,1)S(1)} %collective-permute-done.refs_1_.kv_o, ...), custom_call_target="tpu_custom_call" | custom-call | flops 6442450944 | bytes 2621440 | tf_op jit(solution)/shard_map/pallas_call | solution.py:267
  56.9 1.4 %collective-permute-start.13 = (bf16[4,2,128,128]{3,2,1,0:T(8,128)(2,1)S(1)}, bf16[4,2,128,128]{3,2,1,0:T(8,128)(2,1)S(1)}, u32[]{:S(2)}, u32[]{:S(2)}) collective-permute-start(bf16[4,2,128,128]{3,2,1,0:T(8,128)(2,1)S(1)} %get-tuple-element.26), channel_id=1, source_target_pairs={{0,4},{4,0},{8,12},{12,8},{16,20},{20,16},{24,28},{28,24},{1,5},{5... | collective-permute-start | bytes 786440 | tf_op jit(solution)/shard_map/ppermute | solution.py:24
  58.3 0.0 collective-permute-done.6
  58.3 0.9 %maximum_bitcast_fusion = bf16[128,20,128]{2,0,1:T(8,128)(2,1)} fusion(bf16[10,128,128]{2,1,0:T(8,128)(2,1)S(1)} %get-tuple-element.43, bf16[10,128,128]{2,1,0:T(8,128)(2,1)S(1)} %get-tuple-element.42), kind=kLoop, calls=%fused_computation.10 | loop fusion | flops 327680 | bytes 1310720 | tf_op jit(solution)/shard_map/transpose | solution.py:295
  59.3 6.4 %collective-permute-done.13 = bf16[4,2,128,128]{3,2,1,0:T(8,128)(2,1)S(1)} collective-permute-done((bf16[4,2,128,128]{3,2,1,0:T(8,128)(2,1)S(1)}, bf16[4,2,128,128]{3,2,1,0:T(8,128)(2,1)S(1)}, u32[]{:S(2)}, u32[]{:S(2)}) %collective-permute-start.13) | collective-permute-done | bytes 262176 | tf_op jit(solution)/shard_map/ppermute | solution.py:24
  65.7 0.0 collective-permute-start.14
  65.7 0.0 collective-permute-start.15
  65.7 0.7 collective-permute-done.11.side_a
  66.4 0.0 collective-permute-done.12.side_b
  66.4 3.0 %shard_map.78 = (bf16[4,2,128,128]{3,2,1,0:T(8,128)(2,1)S(1)}, bf16[4,2,128,128]{3,2,1,0:T(8,128)(2,1)S(1)}) custom-call(f32[240]{0:T(256)S(1)} %select_n.84.table, bf16[10,2,128,128]{3,2,1,0:T(8,128)(2,1)S(1)} %constant_dynamic-slice_fusion.refs_0_.kv_k, bf16[10,2,128,128]{3,2,1,0:T(8,128)(2,1)S(1)} %collective-permute-done.refs_1_.kv_o, ...), custom_call_target="tpu_custom_call" | custom-call | flops 6442450944 | bytes 2621440 | tf_op jit(solution)/shard_map/pallas_call | solution.py:267
  69.5 0.8 collective-permute-start.16
  70.3 3.3 %collective-permute-done.14.side_a = bf16[2,4,128,128]{3,2,1,0:T(8,128)(2,1)S(1)} collective-permute-done((bf16[2,4,128,128]{3,2,1,0:T(8,128)(2,1)S(1)}, bf16[2,4,128,128]{3,2,1,0:T(8,128)(2,1)S(1)}, u32[]{:S(2)}, u32[]{:S(2)}) %collective-permute-start.14) | collective-permute-done | bytes 262176 | tf_op jit(solution)/shard_map/ppermute | solution.py:46
  73.6 0.0 collective-permute-done.15.side_b
  73.6 1.9 %shard_map.79 = (bf16[2,2,128,128]{3,2,1,0:T(8,128)(2,1)S(1)}, bf16[2,2,128,128]{3,2,1,0:T(8,128)(2,1)S(1)}) custom-call(f32[240]{0:T(256)S(1)} %select_n.84.table, bf16[10,2,128,128]{3,2,1,0:T(8,128)(2,1)S(1)} %constant_dynamic-slice_fusion.refs_0_.kv_k, bf16[10,2,128,128]{3,2,1,0:T(8,128)(2,1)S(1)} %collective-permute-done.refs_1_.kv_o, ...), custom_call_target="tpu_custom_call" | custom-call | flops 3221225472 | bytes 1310720 | tf_op jit(solution)/shard_map/pallas_call | solution.py:267
  75.5 1.4 %collective-permute-start.17 = (bf16[2,2,128,128]{3,2,1,0:T(8,128)(2,1)S(1)}, bf16[2,2,128,128]{3,2,1,0:T(8,128)(2,1)S(1)}, u32[]{:S(2)}, u32[]{:S(2)}) collective-permute-start(bf16[2,2,128,128]{3,2,1,0:T(8,128)(2,1)S(1)} %get-tuple-element.30), channel_id=1, source_target_pairs={{0,4},{4,0},{8,12},{12,8},{16,20},{20,16},{24,28},{28,24},{1,5},{5... | collective-permute-start | bytes 393224 | tf_op jit(solution)/shard_map/ppermute | solution.py:24
  76.9 1.1 %collective-permute-done.16 = bf16[4,2,128,128]{3,2,1,0:T(8,128)(2,1)S(1)} collective-permute-done((bf16[4,2,128,128]{3,2,1,0:T(8,128)(2,1)S(1)}, bf16[4,2,128,128]{3,2,1,0:T(8,128)(2,1)S(1)}, u32[]{:S(2)}, u32[]{:S(2)}) %collective-permute-start.16) | collective-permute-done | bytes 262176 | tf_op jit(solution)/shard_map/ppermute | solution.py:24
  78.1 2.4 %collective-permute-done.17 = bf16[2,2,128,128]{3,2,1,0:T(8,128)(2,1)S(1)} collective-permute-done((bf16[2,2,128,128]{3,2,1,0:T(8,128)(2,1)S(1)}, bf16[2,2,128,128]{3,2,1,0:T(8,128)(2,1)S(1)}, u32[]{:S(2)}, u32[]{:S(2)}) %collective-permute-start.17) | collective-permute-done | bytes 131104 | tf_op jit(solution)/shard_map/ppermute | solution.py:24
  80.5 0.1 fusion.4
  80.7 1.2 %maximum_bitcast_fusion.1 = (bf16[128,20,128]{2,0,1:T(8,128)(2,1)}, bf16[128,20,128]{2,0,1:T(8,128)(2,1)}) fusion(bf16[10,128,128]{2,1,0:T(8,128)(2,1)S(1)} %get-tuple-element.34, bf16[10,128,128]{2,1,0:T(8,128)(2,1)S(1)} %get-tuple-element.35, bf16[10,128,128]{2,1,0:T(8,128)(2,1)S(1)} %fusion.3, bf16[10,128,128]{2,1,0:T(8,128)(2,1)S(1)} %get-tuple-element.33), kind=kLoop, calls=%fused_computation.11 | loop fusion | flops 655360 | bytes 2621440 | tf_op jit(solution)/shard_map/transpose | solution.py:295
  (27 shorter events, 0.6 us)
Async XLA Ops:
  0.6 7.6 %copy-start = (s32[20,8,5]{0,1,2:T(8,128)S(1)}, s32[20,8,5]{0,1,2:T(8,128)}, u32[]{:S(2)}) copy-start(s32[20,8,5]{0,1,2:T(8,128)} %param.9) | copy-start | bytes 9604
  0.6 5.1 %copy-start.2 = (bf16[128,20,128]{2,0,1:T(8,128)(2,1)S(1)}, bf16[128,20,128]{2,0,1:T(8,128)(2,1)}, u32[]{:S(2)}) copy-start(bf16[128,20,128]{2,0,1:T(8,128)(2,1)} %param.6) | copy-start | bytes 1966084
  0.7 5.1 %copy-start.1 = (bf16[128,20,128]{2,0,1:T(8,128)(2,1)S(1)}, bf16[128,20,128]{2,0,1:T(8,128)(2,1)}, u32[]{:S(2)}) copy-start(bf16[128,20,128]{2,0,1:T(8,128)(2,1)} %param.7) | copy-start | bytes 1966084
  2.8 17.9 %collective-permute-start = (bf16[10,2,128,128]{3,2,1,0:T(8,128)(2,1)}, bf16[10,2,128,128]{3,2,1,0:T(8,128)(2,1)S(1)}, u32[]{:S(2)}, u32[]{:S(2)}) collective-permute-start(bf16[10,2,128,128]{3,2,1,0:T(8,128)(2,1)} %fusion), channel_id=1, source_target_pairs={{0,4},{4,0},{8,12},{12,8},{16,20},{20,16},{24,28},{28,24},{1,5},{5... | collective-permute-start | bytes 1966088 | tf_op jit(solution)/shard_map/ppermute | solution.py:24
  5.9 2.7 %copy-start.3 = (bf16[128,20,128]{2,0,1:T(8,128)(2,1)S(1)}, bf16[128,20,128]{2,0,1:T(8,128)(2,1)}, u32[]{:S(2)}) copy-start(bf16[128,20,128]{2,0,1:T(8,128)(2,1)} %param.5) | copy-start | bytes 1966084
  5.9 32.6 %collective-permute-start.2 = (bf16[10,2,128,128]{3,2,1,0:T(8,128)(2,1)S(1)}, bf16[10,2,128,128]{3,2,1,0:T(8,128)(2,1)S(1)}, u32[]{:S(2)}, u32[]{:S(2)}) collective-permute-start(bf16[10,2,128,128]{3,2,1,0:T(8,128)(2,1)S(1)} %constant_dynamic-slice_fusion.refs_0_.kv_k), channel_id=1, source_target_pairs={{0,8},{1,9},{2,10},{3,11},{4,12},{5,13},{6,14},{7,15},{8,0},{9,1},... | collective-permute-start | bytes 1966088 | tf_op jit(solution)/shard_map/ppermute | solution.py:46
  7.6 31.0 %collective-permute-start.4 = (bf16[10,2,128,128]{3,2,1,0:T(8,128)(2,1)S(1)}, bf16[10,2,128,128]{3,2,1,0:T(8,128)(2,1)}, u32[]{:S(2)}, u32[]{:S(2)}) collective-permute-start(bf16[10,2,128,128]{3,2,1,0:T(8,128)(2,1)S(1)} %constant_dynamic-slice_fusion.refs_0_.kv_k), channel_id=1, source_target_pairs={{0,1},{1,0},{2,3},{3,2},{4,5},{5,4},{6,7},{7,6},{8,16},{9,17},{10,... | collective-permute-start | bytes 1966088 | tf_op jit(solution)/shard_map/ppermute | solution.py:46
  20.7 16.1 %collective-permute-start.1 = (bf16[10,2,128,128]{3,2,1,0:T(8,128)(2,1)}, bf16[10,2,128,128]{3,2,1,0:T(8,128)(2,1)S(1)}, u32[]{:S(2)}, u32[]{:S(2)}) collective-permute-start(bf16[10,2,128,128]{3,2,1,0:T(8,128)(2,1)} %get-tuple-element.17), channel_id=1, source_target_pairs={{0,4},{4,0},{8,12},{12,8},{16,20},{20,16},{24,28},{28,24},{1,5},{5... | collective-permute-start | bytes 1966088 | tf_op jit(solution)/shard_map/ppermute | solution.py:24
  22.4 16.1 %collective-permute-start.3 = (bf16[10,2,128,128]{3,2,1,0:T(8,128)(2,1)S(1)}, bf16[10,2,128,128]{3,2,1,0:T(8,128)(2,1)}, u32[]{:S(2)}, u32[]{:S(2)}) collective-permute-start(bf16[10,2,128,128]{3,2,1,0:T(8,128)(2,1)S(1)} %collective-permute-done.refs_1_.kv_o), channel_id=1, source_target_pairs={{0,8},{1,9},{2,10},{3,11},{4,12},{5,13},{6,14},{7,15},{8,0},{9,1},... | collective-permute-start | bytes 1966088 | tf_op jit(solution)/shard_map/ppermute | solution.py:46
  24.1 14.5 %collective-permute-start.5 = (bf16[10,2,128,128]{3,2,1,0:T(8,128)(2,1)S(1)}, bf16[10,2,128,128]{3,2,1,0:T(8,128)(2,1)}, u32[]{:S(2)}, u32[]{:S(2)}) collective-permute-start(bf16[10,2,128,128]{3,2,1,0:T(8,128)(2,1)S(1)} %collective-permute-done.refs_1_.kv_o), channel_id=1, source_target_pairs={{0,1},{1,0},{2,3},{3,2},{4,5},{5,4},{6,7},{7,6},{8,16},{9,17},{10,... | collective-permute-start | bytes 1966088 | tf_op jit(solution)/shard_map/ppermute | solution.py:46
  36.9 12.4 %collective-permute-start.7 = (bf16[4,4,128,128]{3,2,1,0:T(8,128)(2,1)S(1)}, bf16[4,4,128,128]{3,2,1,0:T(8,128)(2,1)S(1)}, u32[]{:S(2)}, u32[]{:S(2)}) collective-permute-start(bf16[4,4,128,128]{3,2,1,0:T(8,128)(2,1)S(1)} %pad_maximum_fusion.1), channel_id=1, source_target_pairs={{0,8},{1,9},{2,10},{3,11},{4,12},{5,13},{6,14},{7,15},{8,0},{9,1},... | collective-permute-start | bytes 1572872 | tf_op jit(solution)/shard_map/ppermute | solution.py:46
  38.6 15.3 %collective-permute-start.8 = (bf16[4,4,128,128]{3,2,1,0:T(8,128)(2,1)S(1)}, bf16[4,4,128,128]{3,2,1,0:T(8,128)(2,1)S(1)}, u32[]{:S(2)}, u32[]{:S(2)}) collective-permute-start(bf16[4,4,128,128]{3,2,1,0:T(8,128)(2,1)S(1)} %pad_maximum_fusion.1), channel_id=1, source_target_pairs={{0,1},{1,0},{2,3},{3,2},{4,5},{5,4},{6,7},{7,6},{8,16},{9,17},{10,... | collective-permute-start | bytes 1572872 | tf_op jit(solution)/shard_map/ppermute | solution.py:46
  47.2 11.0 %collective-permute-start.6 = (bf16[10,128,128]{2,1,0:T(8,128)(2,1)S(1)}, bf16[10,128,128]{2,1,0:T(8,128)(2,1)S(1)}, u32[]{:S(2)}, u32[]{:S(2)}) collective-permute-start(bf16[10,128,128]{2,1,0:T(8,128)(2,1)S(1)} %get-tuple-element.20), channel_id=1, source_target_pairs={{0,4},{4,0},{8,12},{12,8},{16,20},{20,16},{24,28},{28,24},{1,5},{5... | collective-permute-start | bytes 983048 | tf_op jit(solution)/shard_map/ppermute | solution.py:24
  49.3 4.6 %collective-permute-start.9 = (f32[10,2,256]{2,1,0:T(2,128)S(1)}, f32[10,2,256]{2,1,0:T(2,128)S(1)}, u32[]{:S(2)}, u32[]{:S(2)}) collective-permute-start(f32[10,2,256]{2,1,0:T(2,128)S(1)} %get-tuple-element.22.refs_0_), channel_id=1, source_target_pairs={{0,8},{1,9},{2,10},{3,11},{4,12},{5,13},{6,14},{7,15},{8,0},{9,1},... | collective-permute-start | bytes 61448 | tf_op jit(solution)/shard_map/ppermute | solution.py:46
  52.0 1.9 %collective-permute-start.10 = (f32[10,2,256]{2,1,0:T(2,128)S(1)}, f32[10,2,256]{2,1,0:T(2,128)S(1)}, u32[]{:S(2)}, u32[]{:S(2)}) collective-permute-start(f32[10,2,256]{2,1,0:T(2,128)S(1)} %get-tuple-element.22.refs_0_), channel_id=1, source_target_pairs={{0,1},{1,0},{2,3},{3,2},{4,5},{5,4},{6,7},{7,6},{8,16},{9,17},{10,... | collective-permute-start | bytes 61448 | tf_op jit(solution)/shard_map/ppermute | solution.py:46
  52.0 14.4 %collective-permute-start.11 = (bf16[4,4,128,128]{3,2,1,0:T(8,128)(2,1)S(1)}, bf16[4,4,128,128]{3,2,1,0:T(8,128)(2,1)S(1)}, u32[]{:S(2)}, u32[]{:S(2)}) collective-permute-start(bf16[4,4,128,128]{3,2,1,0:T(8,128)(2,1)S(1)} %pad_maximum_fusion.2), channel_id=1, source_target_pairs={{0,8},{1,9},{2,10},{3,11},{4,12},{5,13},{6,14},{7,15},{8,0},{9,1},... | collective-permute-start | bytes 1572872 | tf_op jit(solution)/shard_map/ppermute | solution.py:46
  53.9 12.6 %collective-permute-start.12 = (bf16[4,4,128,128]{3,2,1,0:T(8,128)(2,1)S(1)}, bf16[4,4,128,128]{3,2,1,0:T(8,128)(2,1)S(1)}, u32[]{:S(2)}, u32[]{:S(2)}) collective-permute-start(bf16[4,4,128,128]{3,2,1,0:T(8,128)(2,1)S(1)} %pad_maximum_fusion.2), channel_id=1, source_target_pairs={{0,1},{1,0},{2,3},{3,2},{4,5},{5,4},{6,7},{7,6},{8,16},{9,17},{10,... | collective-permute-start | bytes 1572872 | tf_op jit(solution)/shard_map/ppermute | solution.py:46
  56.9 8.8 %collective-permute-start.13 = (bf16[4,2,128,128]{3,2,1,0:T(8,128)(2,1)S(1)}, bf16[4,2,128,128]{3,2,1,0:T(8,128)(2,1)S(1)}, u32[]{:S(2)}, u32[]{:S(2)}) collective-permute-start(bf16[4,2,128,128]{3,2,1,0:T(8,128)(2,1)S(1)} %get-tuple-element.26), channel_id=1, source_target_pairs={{0,4},{4,0},{8,12},{12,8},{16,20},{20,16},{24,28},{28,24},{1,5},{5... | collective-permute-start | bytes 786440 | tf_op jit(solution)/shard_map/ppermute | solution.py:24
  65.7 7.9 %collective-permute-start.14 = (bf16[2,4,128,128]{3,2,1,0:T(8,128)(2,1)S(1)}, bf16[2,4,128,128]{3,2,1,0:T(8,128)(2,1)S(1)}, u32[]{:S(2)}, u32[]{:S(2)}) collective-permute-start(bf16[2,4,128,128]{3,2,1,0:T(8,128)(2,1)S(1)} %pad_maximum_fusion.3), channel_id=1, source_target_pairs={{0,8},{1,9},{2,10},{3,11},{4,12},{5,13},{6,14},{7,15},{8,0},{9,1},... | collective-permute-start | bytes 786440 | tf_op jit(solution)/shard_map/ppermute | solution.py:46
  65.7 7.9 %collective-permute-start.15 = (bf16[2,4,128,128]{3,2,1,0:T(8,128)(2,1)S(1)}, bf16[2,4,128,128]{3,2,1,0:T(8,128)(2,1)S(1)}, u32[]{:S(2)}, u32[]{:S(2)}) collective-permute-start(bf16[2,4,128,128]{3,2,1,0:T(8,128)(2,1)S(1)} %pad_maximum_fusion.3), channel_id=1, source_target_pairs={{0,1},{1,0},{2,3},{3,2},{4,5},{5,4},{6,7},{7,6},{8,16},{9,17},{10,... | collective-permute-start | bytes 786440 | tf_op jit(solution)/shard_map/ppermute | solution.py:46
  69.5 8.6 %collective-permute-start.16 = (bf16[4,2,128,128]{3,2,1,0:T(8,128)(2,1)S(1)}, bf16[4,2,128,128]{3,2,1,0:T(8,128)(2,1)S(1)}, u32[]{:S(2)}, u32[]{:S(2)}) collective-permute-start(bf16[4,2,128,128]{3,2,1,0:T(8,128)(2,1)S(1)} %get-tuple-element.29), channel_id=1, source_target_pairs={{0,4},{4,0},{8,12},{12,8},{16,20},{20,16},{24,28},{28,24},{1,5},{5... | collective-permute-start | bytes 786440 | tf_op jit(solution)/shard_map/ppermute | solution.py:24
  75.5 5.0 %collective-permute-start.17 = (bf16[2,2,128,128]{3,2,1,0:T(8,128)(2,1)S(1)}, bf16[2,2,128,128]{3,2,1,0:T(8,128)(2,1)S(1)}, u32[]{:S(2)}, u32[]{:S(2)}) collective-permute-start(bf16[2,2,128,128]{3,2,1,0:T(8,128)(2,1)S(1)} %get-tuple-element.30), channel_id=1, source_target_pairs={{0,4},{4,0},{8,12},{12,8},{16,20},{20,16},{24,28},{28,24},{1,5},{5... | collective-permute-start | bytes 393224 | tf_op jit(solution)/shard_map/ppermute | solution.py:24

commit v6 on v5

--- a/solution.py
+++ b/solution.py
@@ -200,8 +200,12 @@
         return lax.dynamic_slice_in_dim(pair, place * local, local)
 
     kv, qd = by_head(keys, values), by_head(queries, out_grad)
-    kv_send = half(kv, 1 - position)
-    kv_keep = half(after(kv, kv_send), position)
+    def cut(array, place):
+        return half(jnp.transpose(array, (1, 0, 2)), place)
+
+    kv_send = jnp.stack([cut(keys, 1 - position), cut(values, 1 - position)], axis=1)
+    later = after(position, kv_send)
+    kv_keep = jnp.stack([cut(keys, later), cut(values, later)], axis=1)
     qd_send, qd_keep = half(qd, 1 - position), half(qd, position)
     kv_other = across(kv_send, "seq")
     kv_sides = [beside(kv_keep, 0), beside(kv_keep, 1)]

time: 82 us -> 81.6 us (level)
  other arithmetic: 7 us -> 5.75 us
  local copies, waits for them, and re-layouts: 0.9 us -> 2.04 us
    another operation x3 -> x1, other arithmetic: 4.24 us -> 2.23 us  [by_head(): jnp.stack([jnp.transpose(left, (1, 0, 2)), jnp.transpose(right, (1, 0, 2)...]
    another operation x0 -> x3, local copies, waits for them, and re-layouts: none -> 1.18 us  [the longest x1 1.13 us: per_device(): jnp.stack([cut(keys, 1 - position), cut(values, 1 - position)], axis=1)]
    transpose x2 -> x3, other arithmetic: 2.07 us -> 2.68 us  [home(): return jnp.transpose(jnp.concatenate([low, high], axis=0), (1, 0, 2))]
  transfers between devices with their start and end apart: 18 -> 18, of which waited for: 8 -> 8; matrix products, arithmetic and copies ran while one was open for 5% -> 6% of each run, Pallas kernels for 20% -> 20%
where the time goes in v6:
time: 81.6 us; the launch traced here: 81.5 us
  waiting for transfers between devices  36.7 us (45%)
  starting transfers between devices  19.5 us (24%)
  Pallas kernels  16.5 us (20%)
  other arithmetic  5.75 us (7%)
  local copies, waits for them, and re-layouts  2.04 us (2%)
  between operations  0.97 us (1%)
    ppermute x6, waiting for transfers between devices, across(): return lax.ppermute(value, axis, [(i, i ^ 1) for i in range(size)])  32.3 us
    ppermute x6, starting transfers between devices, across(): return lax.ppermute(value, axis, [(i, i ^ 1) for i in range(size)])  9.93 us
    ppermute x12, starting transfers between devices, beside(): return lax.ppermute(value, ('seq', 'dp'), pairs)  9.52 us
    pallas_call x1, Pallas kernels, per_device(): pl.pallas_call(partial(query_kernel, factor, scale, heads), grid=(local /...  8.65 us
    pallas_call x3, Pallas kernels, per_device(): pl.pallas_call(partial(key_kernel, factor, scale, heads, low), grid=(coun...  7.87 us
    ppermute x12, waiting for transfers between devices, beside(): return lax.ppermute(value, ('seq', 'dp'), pairs)  4.46 us
    transpose x3, other arithmetic, home(): return jnp.transpose(jnp.concatenate([low, high], axis=0), (1, 0, 2))  2.68 us
    another operation x1, other arithmetic, by_head(): jnp.stack([jnp.transpose(left, (1, 0, 2)), jnp.transpose(right, (1, 0, 2)...  2.23 us
  transfers between devices with their start and end apart: 18, of which 8 were waited for; matrix products, arithmetic and copies ran while one was open for 6% of the time, Pallas kernels for 20%

profile of v6, /device:TPU:0, one launch (start us, length us, event | category | flops | bytes accessed | tf_op | source)
XLA Modules:
  0.0 81.5 jit_solution(15377399233730347831)
XLA Ops:
  0.6 0.0 copy-start
  0.7 1.1 %dynamic-slice_bitcast_fusion.2 = (bf16[10,1,128,128]{3,2,1,0:T(8,128)(2,1)S(1)}, bf16[10,1,128,128]{3,2,1,0:T(8,128)(2,1)S(1)}) fusion(bf16[128,20,128]{2,0,1:T(8,128)(2,1)} %param.7, s32[]{:T(128)S(6)} %select_n.89, bf16[128,20,128]{2,0,1:T(8,128)(2,1)} %param.6), kind=kLoop, calls=%fused_computation.23 | loop fusion | bytes 1310724 | tf_op jit(solution)/shard_map/stack | solution.py:206
  1.8 0.0 copy-start.3
  1.8 0.1 pad_maximum_fusion
  1.9 0.0 copy-start.4
  1.9 3.0 %collective-permute-start = (bf16[10,2,128,128]{3,2,1,0:T(8,128)(2,1)S(1)}, bf16[10,2,128,128]{3,2,1,0:T(8,128)(2,1)S(1)}, u32[]{:S(2)}, u32[]{:S(2)}) collective-permute-start(bf16[10,2,128,128]{3,2,1,0:T(8,128)(2,1)S(1)} %pad_maximum_fusion), channel_id=1, source_target_pairs={{0,4},{4,0},{8,12},{12,8},{16,20},{20,16},{24,28},{28,24},{1,5},{5... | collective-permute-start | bytes 1966088 | tf_op jit(solution)/shard_map/ppermute | solution.py:24
  4.9 0.0 copy-done.3
  5.0 0.1 pad_maximum_fusion.1.refs_0_.kv_k
  5.1 1.6 %collective-permute-start.2 = (bf16[10,2,128,128]{3,2,1,0:T(8,128)(2,1)S(1)}, bf16[10,2,128,128]{3,2,1,0:T(8,128)(2,1)S(1)}, u32[]{:S(2)}, u32[]{:S(2)}) collective-permute-start(bf16[10,2,128,128]{3,2,1,0:T(8,128)(2,1)S(1)} %pad_maximum_fusion.1.refs_0_.kv_k), channel_id=1, source_target_pairs={{0,8},{1,9},{2,10},{3,11},{4,12},{5,13},{6,14},{7,15},{8,0},{9,1},... | collective-permute-start | bytes 1966088 | tf_op jit(solution)/shard_map/ppermute | solution.py:46
  6.7 0.0 collective-permute-start.4
  6.7 0.1 broadcast_add_fusion.2
  6.8 0.1 add_multiply_fusion
  6.9 0.1 broadcast_add_fusion
  7.0 0.1 stack_broadcast_in_dim.11
  7.0 0.1 stack_broadcast_in_dim.10
  7.1 0.1 stack.65
  7.2 0.1 eq.66
  7.4 0.1 constant_dynamic-slice_fusion
  7.4 0.1 copy.24
  7.6 0.1 multiply_reduce_fusion
  7.7 2.2 %fusion = (bf16[10,2,128,128]{3,2,1,0:T(8,128)(2,1)}, bf16[10,2,128,128]{3,2,1,0:T(8,128)(2,1)S(1)}) fusion(s32[]{:T(128)S(6)} %select_n.89, bf16[20,1,128,128]{3,2,1,0:T(8,128)(2,1)} %bitcast.65, bf16[20,1,128,128]{3,2,1,0:T(8,128)(2,1)} %bitcast.66, s32[]{:T(128)S(6)} %select_n.83), kind=kLoop, calls=%fused_computation.4 | loop fusion | flops 655360 | bytes 2621448 | tf_op jit(solution)/shard_map/stack | solution.py:197
  10.0 9.7 %collective-permute-done.refs_1_.kv_o = bf16[10,2,128,128]{3,2,1,0:T(8,128)(2,1)S(1)} collective-permute-done((bf16[10,2,128,128]{3,2,1,0:T(8,128)(2,1)S(1)}, bf16[10,2,128,128]{3,2,1,0:T(8,128)(2,1)S(1)}, u32[]{:S(2)}, u32[]{:S(2)}) %collective-permute-start) | collective-permute-done | bytes 655392 | tf_op jit(solution)/shard_map/ppermute | solution.py:24
  19.7 1.7 %collective-permute-start.1 = (bf16[10,2,128,128]{3,2,1,0:T(8,128)(2,1)}, bf16[10,2,128,128]{3,2,1,0:T(8,128)(2,1)S(1)}, u32[]{:S(2)}, u32[]{:S(2)}) collective-permute-start(bf16[10,2,128,128]{3,2,1,0:T(8,128)(2,1)} %get-tuple-element.17), channel_id=1, source_target_pairs={{0,4},{4,0},{8,12},{12,8},{16,20},{20,16},{24,28},{28,24},{1,5},{5... | collective-permute-start | bytes 1966088 | tf_op jit(solution)/shard_map/ppermute | solution.py:24
  21.4 1.6 %collective-permute-start.3 = (bf16[10,2,128,128]{3,2,1,0:T(8,128)(2,1)S(1)}, bf16[10,2,128,128]{3,2,1,0:T(8,128)(2,1)}, u32[]{:S(2)}, u32[]{:S(2)}) collective-permute-start(bf16[10,2,128,128]{3,2,1,0:T(8,128)(2,1)S(1)} %collective-permute-done.refs_1_.kv_o), channel_id=1, source_target_pairs={{0,8},{1,9},{2,10},{3,11},{4,12},{5,13},{6,14},{7,15},{8,0},{9,1},... | collective-permute-start | bytes 1966088 | tf_op jit(solution)/shard_map/ppermute | solution.py:46
  23.1 0.0 collective-permute-start.5
  23.1 0.1 select_n.88.table
  23.2 12.6 %collective-permute-done.1.qd_o = bf16[10,2,128,128]{3,2,1,0:T(8,128)(2,1)S(1)} collective-permute-done((bf16[10,2,128,128]{3,2,1,0:T(8,128)(2,1)}, bf16[10,2,128,128]{3,2,1,0:T(8,128)(2,1)S(1)}, u32[]{:S(2)}, u32[]{:S(2)}) %collective-permute-start.1) | collective-permute-done | bytes 655392 | tf_op jit(solution)/shard_map/ppermute | solution.py:24
  35.9 1.6 %collective-permute-start.7 = (bf16[4,4,128,128]{3,2,1,0:T(8,128)(2,1)S(1)}, bf16[4,4,128,128]{3,2,1,0:T(8,128)(2,1)S(1)}, u32[]{:S(2)}, u32[]{:S(2)}) collective-permute-start(bf16[4,4,128,128]{3,2,1,0:T(8,128)(2,1)S(1)} %pad_maximum_fusion.2), channel_id=1, source_target_pairs={{0,8},{1,9},{2,10},{3,11},{4,12},{5,13},{6,14},{7,15},{8,0},{9,1},... | collective-permute-start | bytes 1572872 | tf_op jit(solution)/shard_map/ppermute | solution.py:46
  37.6 0.0 collective-permute-done.2.refs_2_
  37.6 0.0 collective-permute-start.8
  37.6 0.0 collective-permute-done.4.refs_4_
  37.6 0.0 collective-permute-done.3.refs_3_
  37.6 0.0 collective-permute-done.5.refs_5_
  37.6 8.6 %shard_map.76 = (bf16[10,128,128]{2,1,0:T(8,128)(2,1)S(1)}, bf16[10,128,128]{2,1,0:T(8,128)(2,1)S(1)}, f32[10,2,256]{2,1,0:T(2,128)S(1)}) custom-call(f32[240]{0:T(256)S(1)} %select_n.88.table, bf16[10,2,128,128]{3,2,1,0:T(8,128)(2,1)S(1)} %get-tuple-element.37.qd_k, bf16[10,2,128,128]{3,2,1,0:T(8,128)(2,1)S(1)} %collective-permute-done.1.qd_o, ...), custom_call_target="tpu_custom_call" | custom-call | flops 24159191040 | bytes 6553600 | tf_op jit(solution)/shard_map/pallas_call | solution.py:230
  46.2 1.6 %collective-permute-start.6 = (bf16[10,128,128]{2,1,0:T(8,128)(2,1)S(1)}, bf16[10,128,128]{2,1,0:T(8,128)(2,1)S(1)}, u32[]{:S(2)}, u32[]{:S(2)}) collective-permute-start(bf16[10,128,128]{2,1,0:T(8,128)(2,1)S(1)} %get-tuple-element.20), channel_id=1, source_target_pairs={{0,4},{4,0},{8,12},{12,8},{16,20},{20,16},{24,28},{28,24},{1,5},{5... | collective-permute-start | bytes 983048 | tf_op jit(solution)/shard_map/ppermute | solution.py:24
  47.9 0.4 collective-permute-done.7.side_a
  48.3 2.7 %collective-permute-start.9 = (f32[10,2,256]{2,1,0:T(2,128)S(1)}, f32[10,2,256]{2,1,0:T(2,128)S(1)}, u32[]{:S(2)}, u32[]{:S(2)}) collective-permute-start(f32[10,2,256]{2,1,0:T(2,128)S(1)} %get-tuple-element.22.refs_0_), channel_id=1, source_target_pairs={{0,8},{1,9},{2,10},{3,11},{4,12},{5,13},{6,14},{7,15},{8,0},{9,1},... | collective-permute-start | bytes 61448 | tf_op jit(solution)/shard_map/ppermute | solution.py:46
  51.0 0.0 collective-permute-start.10
  51.0 1.8 %collective-permute-start.11 = (bf16[4,4,128,128]{3,2,1,0:T(8,128)(2,1)S(1)}, bf16[4,4,128,128]{3,2,1,0:T(8,128)(2,1)S(1)}, u32[]{:S(2)}, u32[]{:S(2)}) collective-permute-start(bf16[4,4,128,128]{3,2,1,0:T(8,128)(2,1)S(1)} %pad_maximum_fusion.3), channel_id=1, source_target_pairs={{0,8},{1,9},{2,10},{3,11},{4,12},{5,13},{6,14},{7,15},{8,0},{9,1},... | collective-permute-start | bytes 1572872 | tf_op jit(solution)/shard_map/ppermute | solution.py:46
  52.9 0.0 collective-permute-done.8.side_b
  52.9 0.0 collective-permute-start.12
  52.9 0.0 collective-permute-done.9.refs_1_
  52.9 0.0 collective-permute-done.10.refs_2_
  52.9 0.0 copy-done.2
  52.9 3.0 %shard_map.77 = (bf16[4,2,128,128]{3,2,1,0:T(8,128)(2,1)S(1)}, bf16[4,2,128,128]{3,2,1,0:T(8,128)(2,1)S(1)}) custom-call(f32[240]{0:T(256)S(1)} %select_n.88.table, bf16[10,2,128,128]{3,2,1,0:T(8,128)(2,1)S(1)} %pad_maximum_fusion.1.refs_0_.kv_k, bf16[10,2,128,128]{3,2,1,0:T(8,128)(2,1)S(1)} %collective-permute-done.refs_1_.kv_o, ...), custom_call_target="tpu_custom_call" | custom-call | flops 6442450944 | bytes 2621440 | tf_op jit(solution)/shard_map/pallas_call | solution.py:271
  55.9 1.4 %collective-permute-start.13 = (bf16[4,2,128,128]{3,2,1,0:T(8,128)(2,1)S(1)}, bf16[4,2,128,128]{3,2,1,0:T(8,128)(2,1)S(1)}, u32[]{:S(2)}, u32[]{:S(2)}) collective-permute-start(bf16[4,2,128,128]{3,2,1,0:T(8,128)(2,1)S(1)} %get-tuple-element.26), channel_id=1, source_target_pairs={{0,4},{4,0},{8,12},{12,8},{16,20},{20,16},{24,28},{28,24},{1,5},{5... | collective-permute-start | bytes 786440 | tf_op jit(solution)/shard_map/ppermute | solution.py:24
  57.3 0.0 collective-permute-done.6
  57.4 0.9 %maximum_bitcast_fusion = bf16[128,20,128]{2,0,1:T(8,128)(2,1)} fusion(bf16[10,128,128]{2,1,0:T(8,128)(2,1)S(1)} %get-tuple-element.43, bf16[10,128,128]{2,1,0:T(8,128)(2,1)S(1)} %get-tuple-element.42), kind=kLoop, calls=%fused_computation.8 | loop fusion | flops 327680 | bytes 1310720 | tf_op jit(solution)/shard_map/transpose | solution.py:299
  58.3 6.4 %collective-permute-done.13 = bf16[4,2,128,128]{3,2,1,0:T(8,128)(2,1)S(1)} collective-permute-done((bf16[4,2,128,128]{3,2,1,0:T(8,128)(2,1)S(1)}, bf16[4,2,128,128]{3,2,1,0:T(8,128)(2,1)S(1)}, u32[]{:S(2)}, u32[]{:S(2)}) %collective-permute-start.13) | collective-permute-done | bytes 262176 | tf_op jit(solution)/shard_map/ppermute | solution.py:24
  64.7 0.0 collective-permute-start.14
  64.7 0.0 collective-permute-start.15
  64.7 0.7 collective-permute-done.11.side_a
  65.4 0.0 collective-permute-done.12.side_b
  65.4 3.0 %shard_map.78 = (bf16[4,2,128,128]{3,2,1,0:T(8,128)(2,1)S(1)}, bf16[4,2,128,128]{3,2,1,0:T(8,128)(2,1)S(1)}) custom-call(f32[240]{0:T(256)S(1)} %select_n.88.table, bf16[10,2,128,128]{3,2,1,0:T(8,128)(2,1)S(1)} %pad_maximum_fusion.1.refs_0_.kv_k, bf16[10,2,128,128]{3,2,1,0:T(8,128)(2,1)S(1)} %collective-permute-done.refs_1_.kv_o, ...), custom_call_target="tpu_custom_call" | custom-call | flops 6442450944 | bytes 2621440 | tf_op jit(solution)/shard_map/pallas_call | solution.py:271
  68.4 0.8 collective-permute-start.16
  69.3 3.3 %collective-permute-done.14.side_a = bf16[2,4,128,128]{3,2,1,0:T(8,128)(2,1)S(1)} collective-permute-done((bf16[2,4,128,128]{3,2,1,0:T(8,128)(2,1)S(1)}, bf16[2,4,128,128]{3,2,1,0:T(8,128)(2,1)S(1)}, u32[]{:S(2)}, u32[]{:S(2)}) %collective-permute-start.14) | collective-permute-done | bytes 262176 | tf_op jit(solution)/shard_map/ppermute | solution.py:46
  72.6 0.0 collective-permute-done.15.side_b
  72.6 1.9 %shard_map.79 = (bf16[2,2,128,128]{3,2,1,0:T(8,128)(2,1)S(1)}, bf16[2,2,128,128]{3,2,1,0:T(8,128)(2,1)S(1)}) custom-call(f32[240]{0:T(256)S(1)} %select_n.88.table, bf16[10,2,128,128]{3,2,1,0:T(8,128)(2,1)S(1)} %pad_maximum_fusion.1.refs_0_.kv_k, bf16[10,2,128,128]{3,2,1,0:T(8,128)(2,1)S(1)} %collective-permute-done.refs_1_.kv_o, ...), custom_call_target="tpu_custom_call" | custom-call | flops 3221225472 | bytes 1310720 | tf_op jit(solution)/shard_map/pallas_call | solution.py:271
  74.5 1.4 %collective-permute-start.17 = (bf16[2,2,128,128]{3,2,1,0:T(8,128)(2,1)S(1)}, bf16[2,2,128,128]{3,2,1,0:T(8,128)(2,1)S(1)}, u32[]{:S(2)}, u32[]{:S(2)}) collective-permute-start(bf16[2,2,128,128]{3,2,1,0:T(8,128)(2,1)S(1)} %get-tuple-element.30), channel_id=1, source_target_pairs={{0,4},{4,0},{8,12},{12,8},{16,20},{20,16},{24,28},{28,24},{1,5},{5... | collective-permute-start | bytes 393224 | tf_op jit(solution)/shard_map/ppermute | solution.py:24
  75.9 1.1 %collective-permute-done.16 = bf16[4,2,128,128]{3,2,1,0:T(8,128)(2,1)S(1)} collective-permute-done((bf16[4,2,128,128]{3,2,1,0:T(8,128)(2,1)S(1)}, bf16[4,2,128,128]{3,2,1,0:T(8,128)(2,1)S(1)}, u32[]{:S(2)}, u32[]{:S(2)}) %collective-permute-start.16) | collective-permute-done | bytes 262176 | tf_op jit(solution)/shard_map/ppermute | solution.py:24
  77.1 2.5 %collective-permute-done.17 = bf16[2,2,128,128]{3,2,1,0:T(8,128)(2,1)S(1)} collective-permute-done((bf16[2,2,128,128]{3,2,1,0:T(8,128)(2,1)S(1)}, bf16[2,2,128,128]{3,2,1,0:T(8,128)(2,1)S(1)}, u32[]{:S(2)}, u32[]{:S(2)}) %collective-permute-start.17) | collective-permute-done | bytes 131104 | tf_op jit(solution)/shard_map/ppermute | solution.py:24
  79.5 0.1 fusion.3
  79.7 0.9 %maximum_bitcast_fusion.1 = bf16[128,20,128]{2,0,1:T(8,128)(2,1)} fusion(bf16[10,128,128]{2,1,0:T(8,128)(2,1)S(1)} %get-tuple-element.34, bf16[10,128,128]{2,1,0:T(8,128)(2,1)S(1)} %get-tuple-element.35), kind=kLoop, calls=%fused_computation.9 | loop fusion | flops 327680 | bytes 1310720 | tf_op jit(solution)/shard_map/transpose | solution.py:299
  80.6 0.9 %maximum_bitcast_fusion.2 = bf16[128,20,128]{2,0,1:T(8,128)(2,1)} fusion(bf16[10,128,128]{2,1,0:T(8,128)(2,1)S(1)} %fusion.2, bf16[10,128,128]{2,1,0:T(8,128)(2,1)S(1)} %get-tuple-element.33), kind=kLoop, calls=%fused_computation.10 | loop fusion | flops 327680 | bytes 1310720 | tf_op jit(solution)/shard_map/transpose | solution.py:299
  (33 shorter events, 0.6 us)
Async XLA Ops:
  0.6 6.7 %copy-start = (s32[20,8,5]{0,1,2:T(8,128)S(1)}, s32[20,8,5]{0,1,2:T(8,128)}, u32[]{:S(2)}) copy-start(s32[20,8,5]{0,1,2:T(8,128)} %param.9) | copy-start | bytes 9604
  1.8 3.1 %copy-start.3 = (bf16[128,20,128]{2,0,1:T(8,128)(2,1)S(1)}, bf16[128,20,128]{2,0,1:T(8,128)(2,1)}, u32[]{:S(2)}) copy-start(bf16[128,20,128]{2,0,1:T(8,128)(2,1)} %param.7) | copy-start | bytes 1966084
  1.9 3.1 %copy-start.4 = (bf16[128,20,128]{2,0,1:T(8,128)(2,1)S(1)}, bf16[128,20,128]{2,0,1:T(8,128)(2,1)}, u32[]{:S(2)}) copy-start(bf16[128,20,128]{2,0,1:T(8,128)(2,1)} %param.6) | copy-start | bytes 1966084
  1.9 17.8 %collective-permute-start = (bf16[10,2,128,128]{3,2,1,0:T(8,128)(2,1)S(1)}, bf16[10,2,128,128]{3,2,1,0:T(8,128)(2,1)S(1)}, u32[]{:S(2)}, u32[]{:S(2)}) collective-permute-start(bf16[10,2,128,128]{3,2,1,0:T(8,128)(2,1)S(1)} %pad_maximum_fusion), channel_id=1, source_target_pairs={{0,4},{4,0},{8,12},{12,8},{16,20},{20,16},{24,28},{28,24},{1,5},{5... | collective-permute-start | bytes 1966088 | tf_op jit(solution)/shard_map/ppermute | solution.py:24
  5.1 32.5 %collective-permute-start.2 = (bf16[10,2,128,128]{3,2,1,0:T(8,128)(2,1)S(1)}, bf16[10,2,128,128]{3,2,1,0:T(8,128)(2,1)S(1)}, u32[]{:S(2)}, u32[]{:S(2)}) collective-permute-start(bf16[10,2,128,128]{3,2,1,0:T(8,128)(2,1)S(1)} %pad_maximum_fusion.1.refs_0_.kv_k), channel_id=1, source_target_pairs={{0,8},{1,9},{2,10},{3,11},{4,12},{5,13},{6,14},{7,15},{8,0},{9,1},... | collective-permute-start | bytes 1966088 | tf_op jit(solution)/shard_map/ppermute | solution.py:46
  6.7 30.8 %collective-permute-start.4 = (bf16[10,2,128,128]{3,2,1,0:T(8,128)(2,1)S(1)}, bf16[10,2,128,128]{3,2,1,0:T(8,128)(2,1)}, u32[]{:S(2)}, u32[]{:S(2)}) collective-permute-start(bf16[10,2,128,128]{3,2,1,0:T(8,128)(2,1)S(1)} %pad_maximum_fusion.1.refs_0_.kv_k), channel_id=1, source_target_pairs={{0,1},{1,0},{2,3},{3,2},{4,5},{5,4},{6,7},{7,6},{8,16},{9,17},{10,... | collective-permute-start | bytes 1966088 | tf_op jit(solution)/shard_map/ppermute | solution.py:46
  19.7 16.1 %collective-permute-start.1 = (bf16[10,2,128,128]{3,2,1,0:T(8,128)(2,1)}, bf16[10,2,128,128]{3,2,1,0:T(8,128)(2,1)S(1)}, u32[]{:S(2)}, u32[]{:S(2)}) collective-permute-start(bf16[10,2,128,128]{3,2,1,0:T(8,128)(2,1)} %get-tuple-element.17), channel_id=1, source_target_pairs={{0,4},{4,0},{8,12},{12,8},{16,20},{20,16},{24,28},{28,24},{1,5},{5... | collective-permute-start | bytes 1966088 | tf_op jit(solution)/shard_map/ppermute | solution.py:24
  21.4 16.1 %collective-permute-start.3 = (bf16[10,2,128,128]{3,2,1,0:T(8,128)(2,1)S(1)}, bf16[10,2,128,128]{3,2,1,0:T(8,128)(2,1)}, u32[]{:S(2)}, u32[]{:S(2)}) collective-permute-start(bf16[10,2,128,128]{3,2,1,0:T(8,128)(2,1)S(1)} %collective-permute-done.refs_1_.kv_o), channel_id=1, source_target_pairs={{0,8},{1,9},{2,10},{3,11},{4,12},{5,13},{6,14},{7,15},{8,0},{9,1},... | collective-permute-start | bytes 1966088 | tf_op jit(solution)/shard_map/ppermute | solution.py:46
  23.1 14.5 %collective-permute-start.5 = (bf16[10,2,128,128]{3,2,1,0:T(8,128)(2,1)S(1)}, bf16[10,2,128,128]{3,2,1,0:T(8,128)(2,1)}, u32[]{:S(2)}, u32[]{:S(2)}) collective-permute-start(bf16[10,2,128,128]{3,2,1,0:T(8,128)(2,1)S(1)} %collective-permute-done.refs_1_.kv_o), channel_id=1, source_target_pairs={{0,1},{1,0},{2,3},{3,2},{4,5},{5,4},{6,7},{7,6},{8,16},{9,17},{10,... | collective-permute-start | bytes 1966088 | tf_op jit(solution)/shard_map/ppermute | solution.py:46
  35.8 12.0 %copy-start.1 = (bf16[10,2,128,128]{3,2,1,0:T(8,128)(2,1)}, bf16[10,2,128,128]{3,2,1,0:T(8,128)(2,1)S(1)}, u32[]{:S(2)}) copy-start(bf16[10,2,128,128]{3,2,1,0:T(8,128)(2,1)S(1)} %collective-permute-done.1.qd_o) | copy-start | bytes 1966084
  35.9 12.4 %collective-permute-start.7 = (bf16[4,4,128,128]{3,2,1,0:T(8,128)(2,1)S(1)}, bf16[4,4,128,128]{3,2,1,0:T(8,128)(2,1)S(1)}, u32[]{:S(2)}, u32[]{:S(2)}) collective-permute-start(bf16[4,4,128,128]{3,2,1,0:T(8,128)(2,1)S(1)} %pad_maximum_fusion.2), channel_id=1, source_target_pairs={{0,8},{1,9},{2,10},{3,11},{4,12},{5,13},{6,14},{7,15},{8,0},{9,1},... | collective-permute-start | bytes 1572872 | tf_op jit(solution)/shard_map/ppermute | solution.py:46
  37.6 15.3 %collective-permute-start.8 = (bf16[4,4,128,128]{3,2,1,0:T(8,128)(2,1)S(1)}, bf16[4,4,128,128]{3,2,1,0:T(8,128)(2,1)S(1)}, u32[]{:S(2)}, u32[]{:S(2)}) collective-permute-start(bf16[4,4,128,128]{3,2,1,0:T(8,128)(2,1)S(1)} %pad_maximum_fusion.2), channel_id=1, source_target_pairs={{0,1},{1,0},{2,3},{3,2},{4,5},{5,4},{6,7},{7,6},{8,16},{9,17},{10,... | collective-permute-start | bytes 1572872 | tf_op jit(solution)/shard_map/ppermute | solution.py:46
  46.2 11.1 %collective-permute-start.6 = (bf16[10,128,128]{2,1,0:T(8,128)(2,1)S(1)}, bf16[10,128,128]{2,1,0:T(8,128)(2,1)S(1)}, u32[]{:S(2)}, u32[]{:S(2)}) collective-permute-start(bf16[10,128,128]{2,1,0:T(8,128)(2,1)S(1)} %get-tuple-element.20), channel_id=1, source_target_pairs={{0,4},{4,0},{8,12},{12,8},{16,20},{20,16},{24,28},{28,24},{1,5},{5... | collective-permute-start | bytes 983048 | tf_op jit(solution)/shard_map/ppermute | solution.py:24
  47.8 3.2 %slice-start = ((bf16[10,2,128,128]{3,2,1,0:T(8,128)(2,1)}), bf16[2,2,128,128]{3,2,1,0:T(8,128)(2,1)S(1)}, s32[]{:S(2)}) async-start(bf16[10,2,128,128]{3,2,1,0:T(8,128)(2,1)} %copy-done.1), calls=%async_computation | async-start | bytes 262144 | tf_op jit(solution)/shard_map/slice | solution.py:216
  47.8 5.1 %copy-start.2 = (bf16[10,2,128,128]{3,2,1,0:T(8,128)(2,1)S(1)}, bf16[10,2,128,128]{3,2,1,0:T(8,128)(2,1)}, u32[]{:S(2)}) copy-start(bf16[10,2,128,128]{3,2,1,0:T(8,128)(2,1)} %copy-done.1) | copy-start | bytes 1966084
  48.3 4.6 %collective-permute-start.9 = (f32[10,2,256]{2,1,0:T(2,128)S(1)}, f32[10,2,256]{2,1,0:T(2,128)S(1)}, u32[]{:S(2)}, u32[]{:S(2)}) collective-permute-start(f32[10,2,256]{2,1,0:T(2,128)S(1)} %get-tuple-element.22.refs_0_), channel_id=1, source_target_pairs={{0,8},{1,9},{2,10},{3,11},{4,12},{5,13},{6,14},{7,15},{8,0},{9,1},... | collective-permute-start | bytes 61448 | tf_op jit(solution)/shard_map/ppermute | solution.py:46
  51.0 1.9 %collective-permute-start.10 = (f32[10,2,256]{2,1,0:T(2,128)S(1)}, f32[10,2,256]{2,1,0:T(2,128)S(1)}, u32[]{:S(2)}, u32[]{:S(2)}) collective-permute-start(f32[10,2,256]{2,1,0:T(2,128)S(1)} %get-tuple-element.22.refs_0_), channel_id=1, source_target_pairs={{0,1},{1,0},{2,3},{3,2},{4,5},{5,4},{6,7},{7,6},{8,16},{9,17},{10,... | collective-permute-start | bytes 61448 | tf_op jit(solution)/shard_map/ppermute | solution.py:46
  51.0 14.4 %collective-permute-start.11 = (bf16[4,4,128,128]{3,2,1,0:T(8,128)(2,1)S(1)}, bf16[4,4,128,128]{3,2,1,0:T(8,128)(2,1)S(1)}, u32[]{:S(2)}, u32[]{:S(2)}) collective-permute-start(bf16[4,4,128,128]{3,2,1,0:T(8,128)(2,1)S(1)} %pad_maximum_fusion.3), channel_id=1, source_target_pairs={{0,8},{1,9},{2,10},{3,11},{4,12},{5,13},{6,14},{7,15},{8,0},{9,1},... | collective-permute-start | bytes 1572872 | tf_op jit(solution)/shard_map/ppermute | solution.py:46
  52.9 12.6 %collective-permute-start.12 = (bf16[4,4,128,128]{3,2,1,0:T(8,128)(2,1)S(1)}, bf16[4,4,128,128]{3,2,1,0:T(8,128)(2,1)S(1)}, u32[]{:S(2)}, u32[]{:S(2)}) collective-permute-start(bf16[4,4,128,128]{3,2,1,0:T(8,128)(2,1)S(1)} %pad_maximum_fusion.3), channel_id=1, source_target_pairs={{0,1},{1,0},{2,3},{3,2},{4,5},{5,4},{6,7},{7,6},{8,16},{9,17},{10,... | collective-permute-start | bytes 1572872 | tf_op jit(solution)/shard_map/ppermute | solution.py:46
  55.9 8.8 %collective-permute-start.13 = (bf16[4,2,128,128]{3,2,1,0:T(8,128)(2,1)S(1)}, bf16[4,2,128,128]{3,2,1,0:T(8,128)(2,1)S(1)}, u32[]{:S(2)}, u32[]{:S(2)}) collective-permute-start(bf16[4,2,128,128]{3,2,1,0:T(8,128)(2,1)S(1)} %get-tuple-element.26), channel_id=1, source_target_pairs={{0,4},{4,0},{8,12},{12,8},{16,20},{20,16},{24,28},{28,24},{1,5},{5... | collective-permute-start | bytes 786440 | tf_op jit(solution)/shard_map/ppermute | solution.py:24
  64.7 7.9 %collective-permute-start.14 = (bf16[2,4,128,128]{3,2,1,0:T(8,128)(2,1)S(1)}, bf16[2,4,128,128]{3,2,1,0:T(8,128)(2,1)S(1)}, u32[]{:S(2)}, u32[]{:S(2)}) collective-permute-start(bf16[2,4,128,128]{3,2,1,0:T(8,128)(2,1)S(1)} %pad_maximum_fusion.4), channel_id=1, source_target_pairs={{0,8},{1,9},{2,10},{3,11},{4,12},{5,13},{6,14},{7,15},{8,0},{9,1},... | collective-permute-start | bytes 786440 | tf_op jit(solution)/shard_map/ppermute | solution.py:46
  64.7 7.9 %collective-permute-start.15 = (bf16[2,4,128,128]{3,2,1,0:T(8,128)(2,1)S(1)}, bf16[2,4,128,128]{3,2,1,0:T(8,128)(2,1)S(1)}, u32[]{:S(2)}, u32[]{:S(2)}) collective-permute-start(bf16[2,4,128,128]{3,2,1,0:T(8,128)(2,1)S(1)} %pad_maximum_fusion.4), channel_id=1, source_target_pairs={{0,1},{1,0},{2,3},{3,2},{4,5},{5,4},{6,7},{7,6},{8,16},{9,17},{10,... | collective-permute-start | bytes 786440 | tf_op jit(solution)/shard_map/ppermute | solution.py:46
  68.4 8.6 %collective-permute-start.16 = (bf16[4,2,128,128]{3,2,1,0:T(8,128)(2,1)S(1)}, bf16[4,2,128,128]{3,2,1,0:T(8,128)(2,1)S(1)}, u32[]{:S(2)}, u32[]{:S(2)}) collective-permute-start(bf16[4,2,128,128]{3,2,1,0:T(8,128)(2,1)S(1)} %get-tuple-element.29), channel_id=1, source_target_pairs={{0,4},{4,0},{8,12},{12,8},{16,20},{20,16},{24,28},{28,24},{1,5},{5... | collective-permute-start | bytes 786440 | tf_op jit(solution)/shard_map/ppermute | solution.py:24
  74.5 5.0 %collective-permute-start.17 = (bf16[2,2,128,128]{3,2,1,0:T(8,128)(2,1)S(1)}, bf16[2,2,128,128]{3,2,1,0:T(8,128)(2,1)S(1)}, u32[]{:S(2)}, u32[]{:S(2)}) collective-permute-start(bf16[2,2,128,128]{3,2,1,0:T(8,128)(2,1)S(1)} %get-tuple-element.30), channel_id=1, source_target_pairs={{0,4},{4,0},{8,12},{12,8},{16,20},{20,16},{24,28},{28,24},{1,5},{5... | collective-permute-start | bytes 393224 | tf_op jit(solution)/shard_map/ppermute | solution.py:24
